TPU v7x, 32 devices: a whole 2x2x4 slice. The times are simulated.
32 devices in a mesh: section: 2 (over core), dp: 4 (over z), tensor: 4 (over y, x).
Axes of the slice: x: 2, y: 2, z: 4, core: 2. Of those that a mesh axis runs over, the one named last changes fastest.
Arguments:
- inputs: float32 [2, 4096, 1024], P(None, ('dp', 'tensor')), may hold values from -6 to 6
- cotangent: float32 [2, 4096, 1024], P(None, ('dp', 'tensor')), may hold values from -6 to 6
- split: int32 [2, 4], P(None, 'dp'), may hold values from 0 to 1, as said below
- query_key_value_weight: bfloat16 [2, 1024, 3, 1024], P('section', 'dp', None, 'tensor'), may hold values from -0.1875 to 0.1875
- output_weight: bfloat16 [2, 1024, 1024], P('section', 'tensor', 'dp'), may hold values from -0.75 to 0.75
- up_weight: bfloat16 [2, 1024, 4096], P('section', 'dp', 'tensor'), may hold values from -0.1875 to 0.1875
- down_weight: bfloat16 [2, 4096, 1024], P('section', 'tensor', 'dp'), may hold values from -0.1875 to 0.1875
- qkv_adapter_input: float32 [2, 1024, 128], P('section'), may hold values from -0.1875 to 0.1875
- qkv_adapter_output: float32 [2, 128, 3, 1024], P('section', None, None, 'tensor'), may hold values from -0.5 to 0.5
- out_adapter_input: float32 [2, 1024, 128], P('section', 'tensor'), may hold values from -0.75 to 0.75
- out_adapter_output: float32 [2, 128, 1024], P('section'), may hold values from -0.5 to 0.5
- up_adapter_input: float32 [2, 1024, 128], P('section'), may hold values from -0.1875 to 0.1875
- up_adapter_output: float32 [2, 128, 4096], P('section', None, 'tensor'), may hold values from -0.5 to 0.5
- down_adapter_input: float32 [2, 4096, 128], P('section', 'tensor'), may hold values from -0.1875 to 0.1875
- down_adapter_output: float32 [2, 128, 1024], P('section'), may hold values from -0.5 to 0.5
- ln_gain: float32 [2, 2, 1024], P('section'), may hold values from 0.5 to 1.5
- ln_bias: float32 [2, 2, 1024], P('section'), may hold values from -2 to 2
Outputs:
- activations: float32 [2, 2, 4096, 1024], P('section', None, ('dp', 'tensor'))
- input_grads: float32 [2, 2, 4096, 1024], P('section', None, ('dp', 'tensor'))
- grad_a_qkv: float32 [2, 1024, 128], P('section')
- qkv_adapter_gradient: float32 [2, 128, 3, 1024], P('section', None, None, 'tensor')
- grad_a_out: float32 [2, 1024, 128], P('section', 'tensor')
- out_adapter_gradient: float32 [2, 128, 1024], P('section')
- grad_a_up: float32 [2, 1024, 128], P('section')
- up_adapter_gradient: float32 [2, 128, 4096], P('section', None, 'tensor')
- grad_a_down: float32 [2, 4096, 128], P('section', 'tensor')
- down_adapter_gradient: float32 [2, 128, 1024], P('section')
- grad_gain: float32 [2, 2, 1024], P('section')
- grad_bias: float32 [2, 2, 1024], P('section')
- combined_qkv_weight: float32 [2, 1024, 3, 1024], P('section', 'dp', None, 'tensor')
- combined_out_weight: float32 [2, 1024, 1024], P('section', 'tensor', 'dp')
- combined_up_weight: float32 [2, 1024, 4096], P('section', 'dp', 'tensor')
- combined_down_weight: float32 [2, 4096, 1024], P('section', 'tensor', 'dp')
Inputs may be any that keep to these rules, and one draw needn't show every extreme that they name: `split`: in each micro-batch exactly 2 of the blocks hold two sequences (value 1), the others one (value 0).
All inputs are finite; a program needn't handle non-finite values.
Results may differ from a plain program's by a relative error of at most 0.023.
Values may be sent and summed in bfloat16 or wider, within the bound.
A program may use at most 256 MiB of HBM per device.

v0:
```python
import jax
import jax.numpy as jnp
from jax import lax
from jax.sharding import PartitionSpec as P

HEAD = 64
ROT = 16


ADAPTER_SCALE = 0.25
EPSILON = 1e-05
MASKED = -1e30
FULL_PRECISION = lax.Precision.HIGHEST


def from_behind(x, axis, by):
    size = lax.axis_size(axis)
    pairs = [(i, i + by) for i in range(size) if 0 <= i + by < size]
    return lax.ppermute(x, axis, pairs)


def matrix_product(left_side, right_side):
    return jnp.dot(left_side, right_side, preferred_element_type=jnp.float32)


def inner_feature_rows(left_side, right_side):
    return lax.dot_general(
        left_side, right_side, (((0,), (0,)), ((), ())), preferred_element_type=jnp.float32
    )


def contracted_with(left_side, right_side):
    return lax.dot_general(
        left_side, right_side, (((1,), (1,)), ((), ())), preferred_element_type=jnp.float32
    )


def layer_norms(source, gain_rows, bias_rows):
    row_mean = jnp.mean(source, axis=-1, keepdims=True)
    centred = source - row_mean
    spread = jnp.mean(centred * centred, axis=-1, keepdims=True)
    normed = centred * lax.rsqrt(spread + EPSILON)
    return (normed * gain_rows[0] + bias_rows[0], normed * gain_rows[1] + bias_rows[1])


def geometry(split_flag, length):
    token_index = jnp.arange(length, dtype=jnp.int32)
    second_doc = (token_index >= length // 2).astype(jnp.int32) * split_flag
    places = (token_index - length // 2 * second_doc).astype(jnp.float32)
    half_rot = ROT // 2
    inverse = 10000.0 ** (-jnp.arange(half_rot, dtype=jnp.float32) * 2.0 / ROT)
    angles = places[:, None] * inverse[None, :]
    angles = jnp.concatenate([angles, angles], axis=-1)[:, None, :]
    allowed = (token_index[:, None] >= token_index[None, :]) & (
        second_doc[:, None] == second_doc[None, :]
    )
    return (jnp.cos(angles), jnp.sin(angles), allowed)


def rotate(heads_view, cosine_table, sine_table):
    half_rot = ROT // 2
    leading_part = heads_view[..., :ROT]
    turned = jnp.concatenate([-leading_part[..., half_rot:], leading_part[..., :half_rot]], axis=-1)
    return jnp.concatenate(
        [leading_part * cosine_table + turned * sine_table, heads_view[..., ROT:]], axis=-1
    )


def weights_of(scores, allowed):
    masked_scores = jnp.where(allowed[None], scores, MASKED)
    row_max = jnp.max(masked_scores, axis=-1, keepdims=True)
    exponent = jnp.exp(masked_scores - row_max)
    return exponent / jnp.sum(exponent, axis=-1, keepdims=True)


def collect(query_key_value_weight, output_weight, up_weight, down_weight):
    rows_qkv, rows_up = (
        lax.all_gather(query_key_value_weight[0], "dp", axis=0, tiled=True),
        lax.all_gather(up_weight[0], "dp", axis=0, tiled=True),
    )
    cols_out, cols_down = (
        lax.all_gather(output_weight[0], "dp", axis=1, tiled=True),
        lax.all_gather(down_weight[0], "dp", axis=1, tiled=True),
    )
    return (rows_qkv.reshape(rows_qkv.shape[0], -1), cols_out, rows_up, cols_down)


def forward(source_rows, weights, factors, gain_rows, bias_rows, split_flag, tensor_place):
    qkv_weight_full, output_weight_full, up_weight_full, down_weight_full = weights
    (
        fac_a_qkv,
        qkv_output_factor,
        fac_a_out,
        out_output_factor,
        fac_a_up,
        up_output_factor,
        fac_a_down,
        down_output_factor,
    ) = factors
    first_normalized, second_normalized = layer_norms(source_rows, gain_rows, bias_rows)
    first_normalized, second_normalized = (
        lax.all_gather(first_normalized.astype(jnp.bfloat16), "tensor", axis=0, tiled=True),
        lax.all_gather(second_normalized.astype(jnp.bfloat16), "tensor", axis=0, tiled=True),
    )
    length = first_normalized.shape[0]
    qkv_reduced = matrix_product(first_normalized, fac_a_qkv).astype(jnp.bfloat16)
    up_reduced = matrix_product(second_normalized, fac_a_up).astype(jnp.bfloat16)
    joined_rows = matrix_product(
        first_normalized, qkv_weight_full
    ) + ADAPTER_SCALE * matrix_product(qkv_reduced, qkv_output_factor)
    hidden_rows = matrix_product(
        second_normalized, up_weight_full
    ) + ADAPTER_SCALE * matrix_product(up_reduced, up_output_factor)
    heads_view = joined_rows.reshape(length, 3, -1, HEAD)
    cosine_table, sine_table, allowed = geometry(split_flag, length)
    queries = rotate(heads_view[:, 0], cosine_table, sine_table).astype(jnp.bfloat16)
    key_heads = rotate(heads_view[:, 1], cosine_table, sine_table).astype(jnp.bfloat16)
    value_heads = heads_view[:, 2].astype(jnp.bfloat16)
    scores = (
        jnp.einsum("qhd,khd->hqk", queries, key_heads, preferred_element_type=jnp.float32) * 0.125
    )
    probabilities = weights_of(scores, allowed)
    probs_low = probabilities.astype(jnp.bfloat16)
    attention_result = jnp.einsum(
        "hqk,khd->qhd", probs_low, value_heads, preferred_element_type=jnp.float32
    )
    attention_result = attention_result.reshape(length, -1).astype(jnp.bfloat16)
    activated_rows = jax.nn.gelu(hidden_rows, approximate=False).astype(jnp.bfloat16)
    out_reduced, down_reduced = (
        lax.psum(matrix_product(attention_result, fac_a_out).astype(jnp.bfloat16), "tensor").astype(
            jnp.float32
        ),
        lax.psum(matrix_product(activated_rows, fac_a_down).astype(jnp.bfloat16), "tensor").astype(
            jnp.float32
        ),
    )
    out_reduced = out_reduced.astype(jnp.bfloat16)
    down_reduced = down_reduced.astype(jnp.bfloat16)
    partial_sum = matrix_product(attention_result, output_weight_full) + matrix_product(
        activated_rows, down_weight_full
    )
    branch_output = lax.psum_scatter(
        partial_sum.astype(jnp.bfloat16), "tensor", scatter_dimension=0, tiled=True
    ).astype(jnp.float32)
    row_count = source_rows.shape[0]
    row_start = tensor_place * row_count
    local_out_part = lax.dynamic_slice_in_dim(out_reduced, row_start, row_count, 0)
    local_down_part = lax.dynamic_slice_in_dim(down_reduced, row_start, row_count, 0)
    result = (
        source_rows
        + branch_output
        + ADAPTER_SCALE
        * (
            matrix_product(local_out_part, out_output_factor)
            + matrix_product(local_down_part, down_output_factor)
        )
    )
    saved = (
        source_rows,
        first_normalized,
        second_normalized,
        qkv_reduced,
        up_reduced,
        heads_view,
        cosine_table,
        sine_table,
        queries,
        key_heads,
        value_heads,
        probabilities,
        probs_low,
        attention_result,
        hidden_rows,
        activated_rows,
        out_reduced,
        down_reduced,
    )
    return (result, saved)


def backward(
    source_rows, upstream, weights, factors, gain_rows, bias_rows, split_flag, tensor_place
):
    unused_result, saved = forward(
        source_rows, weights, factors, gain_rows, bias_rows, split_flag, tensor_place
    )
    (
        source,
        first_normalized,
        second_normalized,
        qkv_reduced,
        up_reduced,
        heads_view,
        cosine_table,
        sine_table,
        queries,
        key_heads,
        value_heads,
        probabilities,
        probs_low,
        attention_result,
        hidden_rows,
        activated_rows,
        out_reduced,
        down_reduced,
    ) = saved
    qkv_weight_full, output_weight_full, up_weight_full, down_weight_full = weights
    (
        fac_a_qkv,
        qkv_output_factor,
        fac_a_out,
        out_output_factor,
        fac_a_up,
        up_output_factor,
        fac_a_down,
        down_output_factor,
    ) = factors
    length = first_normalized.shape[0]
    down_gradient = lax.all_gather(upstream.astype(jnp.bfloat16), "tensor", axis=0, tiled=True)
    out_reduced_gradient = (
        ADAPTER_SCALE * contracted_with(down_gradient, out_output_factor)
    ).astype(jnp.bfloat16)
    down_reduced_gradient = (
        ADAPTER_SCALE * contracted_with(down_gradient, down_output_factor)
    ).astype(jnp.bfloat16)
    out_adapter_gradient = ADAPTER_SCALE * inner_feature_rows(out_reduced, down_gradient)
    down_adapter_gradient = ADAPTER_SCALE * inner_feature_rows(down_reduced, down_gradient)
    grad_a_out = inner_feature_rows(attention_result, out_reduced_gradient)
    grad_a_down = inner_feature_rows(activated_rows, down_reduced_gradient)
    grad_attended = (
        contracted_with(down_gradient, output_weight_full)
        + contracted_with(out_reduced_gradient, fac_a_out)
    ).astype(jnp.bfloat16)
    grad_active = contracted_with(down_gradient, down_weight_full) + contracted_with(
        down_reduced_gradient, fac_a_down
    )
    unused_gelu, gelu_pull = jax.vjp(
        lambda argument: jax.nn.gelu(argument, approximate=False), hidden_rows
    )
    hidden_gradient = gelu_pull(grad_active)[0].astype(jnp.bfloat16)
    heads_grad = grad_attended.reshape(length, -1, HEAD)
    grad_probs = jnp.einsum(
        "qhd,khd->hqk", heads_grad, value_heads, preferred_element_type=jnp.float32
    )
    grad_scores = probabilities * (
        grad_probs - jnp.sum(probabilities * grad_probs, axis=-1, keepdims=True)
    )
    grad_scores = grad_scores.astype(jnp.bfloat16)
    grad_queries = (
        jnp.einsum("hqk,khd->qhd", grad_scores, key_heads, preferred_element_type=jnp.float32)
        * 0.125
    )
    grad_keys = (
        jnp.einsum("hqk,qhd->khd", grad_scores, queries, preferred_element_type=jnp.float32) * 0.125
    )
    grad_values = jnp.einsum(
        "hqk,qhd->khd", probs_low, heads_grad, preferred_element_type=jnp.float32
    )
    unused_turn, turn_pull = jax.vjp(
        lambda first_arg, second_arg: (
            rotate(first_arg, cosine_table, sine_table),
            rotate(second_arg, cosine_table, sine_table),
        ),
        heads_view[:, 0],
        heads_view[:, 1],
    )
    back_queries, back_keys = turn_pull((grad_queries, grad_keys))
    joined_gradient = (
        jnp.stack([back_queries, back_keys, grad_values], axis=1)
        .reshape(length, -1)
        .astype(jnp.bfloat16)
    )
    qkv_adapter_gradient = ADAPTER_SCALE * inner_feature_rows(qkv_reduced, joined_gradient)
    up_adapter_gradient = ADAPTER_SCALE * inner_feature_rows(up_reduced, hidden_gradient)
    grad_small_qkv, grad_small_up = (
        lax.psum(
            (ADAPTER_SCALE * contracted_with(joined_gradient, qkv_output_factor)).astype(
                jnp.bfloat16
            ),
            "tensor",
        ).astype(jnp.float32),
        lax.psum(
            (ADAPTER_SCALE * contracted_with(hidden_gradient, up_output_factor)).astype(
                jnp.bfloat16
            ),
            "tensor",
        ).astype(jnp.float32),
    )
    grad_small_qkv = grad_small_qkv.astype(jnp.bfloat16)
    grad_small_up = grad_small_up.astype(jnp.bfloat16)
    grad_a_qkv = inner_feature_rows(first_normalized, grad_small_qkv)
    grad_a_up = inner_feature_rows(second_normalized, grad_small_up)
    owner_flag = (tensor_place == 0).astype(jnp.float32)
    grad_one = contracted_with(joined_gradient, qkv_weight_full) + owner_flag * contracted_with(
        grad_small_qkv, fac_a_qkv
    )
    grad_two = contracted_with(hidden_gradient, up_weight_full) + owner_flag * contracted_with(
        grad_small_up, fac_a_up
    )
    grad_one, grad_two = (
        lax.psum_scatter(
            grad_one.astype(jnp.bfloat16), "tensor", scatter_dimension=0, tiled=True
        ).astype(jnp.float32),
        lax.psum_scatter(
            grad_two.astype(jnp.bfloat16), "tensor", scatter_dimension=0, tiled=True
        ).astype(jnp.float32),
    )
    unused_norm, norm_pull = jax.vjp(layer_norms, source, gain_rows, bias_rows)
    grad_source, grad_gain, grad_bias = norm_pull((grad_one, grad_two))
    result = upstream + grad_source
    gradients = (
        grad_a_qkv,
        qkv_adapter_gradient,
        grad_a_out,
        out_adapter_gradient,
        grad_a_up,
        up_adapter_gradient,
        grad_a_down,
        down_adapter_gradient,
        grad_gain,
        grad_bias,
    )
    return (result, gradients)


def per_device(
    inputs,
    cotangent,
    split,
    query_key_value_weight,
    output_weight,
    up_weight,
    down_weight,
    qkv_adapter_input,
    qkv_adapter_output,
    out_adapter_input,
    out_adapter_output,
    up_adapter_input,
    up_adapter_output,
    down_adapter_input,
    down_adapter_output,
    ln_gain,
    ln_bias,
):
    section_index = lax.axis_index("section")
    leading = section_index == 0
    tensor_place = lax.axis_index("tensor")
    micro_count = inputs.shape[0]
    trained = (
        qkv_adapter_input[0],
        qkv_adapter_output[0].reshape(qkv_adapter_output.shape[1], -1),
        out_adapter_input[0],
        out_adapter_output[0],
        up_adapter_input[0],
        up_adapter_output[0],
        down_adapter_input[0],
        down_adapter_output[0],
    )
    factors = tuple((member.astype(jnp.bfloat16) for member in trained))
    gain_rows = ln_gain[0]
    bias_rows = ln_bias[0]
    split_flags = split[:, 0]
    empty_rows = jnp.zeros_like(inputs[0])
    received = empty_rows
    kept_inputs = []
    produced = []
    for step_index in range(micro_count + 1):
        layer_input = jnp.where(leading, inputs[min(step_index, micro_count - 1)], received)
        split_flag = split_flags[jnp.clip(step_index - section_index, 0, micro_count - 1)]
        weights = collect(query_key_value_weight, output_weight, up_weight, down_weight)
        result, unused_saved = forward(
            layer_input, weights, factors, gain_rows, bias_rows, split_flag, tensor_place
        )
        kept_inputs.append(layer_input)
        produced.append(result)
        if step_index < micro_count:
            received = from_behind(result.astype(jnp.bfloat16), "section", 1).astype(result.dtype)
    activations = jnp.stack(
        [
            jnp.where(leading, produced[batch_index], produced[batch_index + 1])
            for batch_index in range(micro_count)
        ]
    )
    returned = empty_rows
    handed = []
    totals = None
    for step_index in range(micro_count + 1):
        upstream = jnp.where(leading, returned, cotangent[min(step_index, micro_count - 1)])
        earlier = kept_inputs[step_index - 1] if step_index >= 1 else empty_rows
        later_input = kept_inputs[step_index + 1] if step_index + 1 <= micro_count else empty_rows
        layer_input = jnp.where(leading, earlier, later_input)
        split_flag = split_flags[jnp.clip(step_index + section_index - 1, 0, micro_count - 1)]
        valid_flag = jnp.where(leading, step_index >= 1, step_index < micro_count).astype(
            jnp.float32
        )
        weights = collect(query_key_value_weight, output_weight, up_weight, down_weight)
        result, gradients = backward(
            layer_input, upstream, weights, factors, gain_rows, bias_rows, split_flag, tensor_place
        )
        gradients = tuple((valid_flag * member for member in gradients))
        totals = (
            gradients
            if totals is None
            else tuple((old_sum + new_term for old_sum, new_term in zip(totals, gradients)))
        )
        handed.append(result)
        if step_index < micro_count:
            returned = from_behind(result.astype(jnp.bfloat16), "section", -1).astype(result.dtype)
    input_grads = jnp.stack(
        [
            jnp.where(leading, handed[batch_index + 1], handed[batch_index])
            for batch_index in range(micro_count)
        ]
    )
    (
        sum_a_qkv,
        sum_b_qkv,
        sum_a_out,
        sum_b_out,
        sum_a_up,
        sum_b_up,
        sum_a_down,
        sum_b_down,
        sum_gain,
        sum_bias,
    ) = totals
    sum_a_qkv, sum_b_qkv, sum_a_out, sum_b_out, sum_a_up, sum_b_up, sum_a_down, sum_b_down = (
        lax.psum(sum_a_qkv.astype(jnp.bfloat16), "dp").astype(jnp.float32),
        lax.psum(sum_b_qkv.astype(jnp.bfloat16), "dp").astype(jnp.float32),
        lax.psum(sum_a_out.astype(jnp.bfloat16), "dp").astype(jnp.float32),
        lax.psum(sum_b_out.astype(jnp.bfloat16), "dp").astype(jnp.float32),
        lax.psum(sum_a_up.astype(jnp.bfloat16), "dp").astype(jnp.float32),
        lax.psum(sum_b_up.astype(jnp.bfloat16), "dp").astype(jnp.float32),
        lax.psum(sum_a_down.astype(jnp.bfloat16), "dp").astype(jnp.float32),
        lax.psum(sum_b_down.astype(jnp.bfloat16), "dp").astype(jnp.float32),
    )
    sum_gain, sum_bias = lax.psum((sum_gain, sum_bias), ("dp", "tensor"))
    dp_place = lax.axis_index("dp")
    row_count = query_key_value_weight.shape[1]
    col_count = output_weight.shape[2]
    part_qkv = lax.dynamic_slice_in_dim(qkv_adapter_input[0], dp_place * row_count, row_count, 0)
    combined_qkv_weight = query_key_value_weight[0].astype(
        jnp.float32
    ) + ADAPTER_SCALE * jnp.einsum(
        "dr,rcf->dcf", part_qkv, qkv_adapter_output[0], precision=FULL_PRECISION
    )
    part_out = lax.dynamic_slice_in_dim(out_adapter_output[0], dp_place * col_count, col_count, 1)
    combined_out_weight = output_weight[0].astype(jnp.float32) + ADAPTER_SCALE * jnp.dot(
        out_adapter_input[0], part_out, precision=FULL_PRECISION, preferred_element_type=jnp.float32
    )
    part_up = lax.dynamic_slice_in_dim(up_adapter_input[0], dp_place * row_count, row_count, 0)
    combined_up_weight = up_weight[0].astype(jnp.float32) + ADAPTER_SCALE * jnp.dot(
        part_up, up_adapter_output[0], precision=FULL_PRECISION, preferred_element_type=jnp.float32
    )
    part_down = lax.dynamic_slice_in_dim(down_adapter_output[0], dp_place * col_count, col_count, 1)
    combined_down_weight = down_weight[0].astype(jnp.float32) + ADAPTER_SCALE * jnp.dot(
        down_adapter_input[0],
        part_down,
        precision=FULL_PRECISION,
        preferred_element_type=jnp.float32,
    )
    return (
        activations[None],
        input_grads[None],
        sum_a_qkv[None],
        sum_b_qkv.reshape(qkv_adapter_output.shape),
        sum_a_out[None],
        sum_b_out[None],
        sum_a_up[None],
        sum_b_up[None],
        sum_a_down[None],
        sum_b_down[None],
        sum_gain[None],
        sum_bias[None],
        combined_qkv_weight[None],
        combined_out_weight[None],
        combined_up_weight[None],
        combined_down_weight[None],
    )


def solution(mesh):
    in_specs = (
        P(None, ("dp", "tensor"), None),
        P(None, ("dp", "tensor"), None),
        P(None, "dp"),
        P("section", "dp", None, "tensor"),
        P("section", "tensor", "dp"),
        P("section", "dp", "tensor"),
        P("section", "tensor", "dp"),
        P("section", None, None),
        P("section", None, None, "tensor"),
        P("section", "tensor", None),
        P("section", None, None),
        P("section", None, None),
        P("section", None, "tensor"),
        P("section", "tensor", None),
        P("section", None, None),
        P("section", None, None),
        P("section", None, None),
    )
    out_specs = (
        P("section", None, ("dp", "tensor"), None),
        P("section", None, ("dp", "tensor"), None),
        P("section", None, None),
        P("section", None, None, "tensor"),
        P("section", "tensor", None),
        P("section", None, None),
        P("section", None, None),
        P("section", None, "tensor"),
        P("section", "tensor", None),
        P("section", None, None),
        P("section", None, None),
        P("section", None, None),
        P("section", "dp", None, "tensor"),
        P("section", "tensor", "dp"),
        P("section", "dp", "tensor"),
        P("section", "tensor", "dp"),
    )
    return jax.shard_map(
        per_device, mesh=mesh, in_specs=in_specs, out_specs=out_specs, check_vma=False
    )
```

profile of v0, /device:TPU:0, one launch (start us, length us, event | category | flops | bytes accessed | tf_op | source)
XLA Modules:
  0.0 1699.9 jit_solution(10379596077979447974)
XLA Ops:
  28.7 25.6 %all-gather.1 = bf16[1,256,1024]{2,1,0:T(8,128)(2,1)S(1)} all-gather(bf16[1,256,256]{2,1,0:T(8,128)(2,1)S(1)} %copy-done.151), channel_id=3, replica_groups=mesh['section'=2,'dp'=4,'tensor'=4] {'dp'}, dimensions={2}, use_global_device_ids=true | all-gather | bytes 655360 | tf_op jit(solution)/shard_map/all_gather | solution.py:82
  59.1 37.4 %all-gather.23.cloned.1.call-done = bf16[1024,1024]{1,0:T(8,128)(2,1)} async-done(((bf16[256,1024]{1,0:T(8,128)(2,1)}), bf16[1024,1024]{1,0:T(8,128)(2,1)}) %all-gather.23.cloned.1.call-update) | async-done | bytes 2097168 | tf_op jit(solution)/shard_map/all_gather | solution.py:102
  144.0 36.3 %all-gather.25.cloned.1.call-done = bf16[1024,1024]{1,0:T(8,128)(2,1)} async-done(((bf16[256,1024]{1,0:T(8,128)(2,1)}), bf16[1024,1024]{1,0:T(8,128)(2,1)}) %all-gather.25.cloned.1.call-update) | async-done | bytes 2097168 | tf_op jit(solution)/shard_map/all_gather | solution.py:103
  187.9 13.9 fusion.35
  204.9 23.1 %all-gather.57.cloned.1.call-done = bf16[1,1024,1024]{2,1,0:T(8,128)(2,1)} async-done(((bf16[1,1024,256]{2,1,0:T(8,128)(2,1)}), bf16[1,1024,1024]{2,1,0:T(8,128)(2,1)}) %all-gather.57.cloned.1.call-update) | async-done | bytes 2097168 | tf_op jit(solution)/shard_map/all_gather | solution.py:83
  238.4 37.4 %all-reduce.58.cloned.1.call-done = (bf16[1024,128]{1,0:T(8,128)(2,1)}, bf16[1024,128]{1,0:T(8,128)(2,1)}) async-done(((bf16[1024,128]{1,0:T(8,128)(2,1)}, bf16[1024,128]{1,0:T(8,128)(2,1)}), (bf16[1024,128]{1,0:T(8,128)(2,1)}, bf16[1024,128]{1,0:T(8,128)(2,1)})) %all-reduce.58.cloned.1.call-update) | async-done | bytes 524304 | tf_op jit(solution)/shard_map/psum | solution.py:130
  277.9 36.7 %reduce-scatter.10.cloned.1.call-done = bf16[256,1024]{1,0:T(8,128)(2,1)} async-done(((bf16[1024,1024]{1,0:T(8,128)(2,1)}), bf16[256,1024]{1,0:T(8,128)(2,1)}) %reduce-scatter.10.cloned.1.call-update) | async-done | bytes 524304 | tf_op jit(solution)/shard_map/reduce_scatter | solution.py:142
  327.7 24.8 %all-gather.37.cloned.1.call-done = bf16[1024,1024]{1,0:T(8,128)(2,1)} async-done(((bf16[256,1024]{1,0:T(8,128)(2,1)}), bf16[1024,1024]{1,0:T(8,128)(2,1)}) %all-gather.37.cloned.1.call-update) | async-done | bytes 2097168 | tf_op jit(solution)/shard_map/all_gather | solution.py:219
  364.3 26.1 %all-gather.39.cloned.1.call-done = bf16[1024,1024]{1,0:T(8,128)(2,1)} async-done(((bf16[256,1024]{1,0:T(8,128)(2,1)}), bf16[1024,1024]{1,0:T(8,128)(2,1)}) %all-gather.39.cloned.1.call-update) | async-done | bytes 2097168 | tf_op jit(solution)/shard_map/all_gather | solution.py:102
  478.8 39.9 %all-reduce.56.cloned.1.call-done = (bf16[1024,128]{1,0:T(8,128)(2,1)}, bf16[1024,128]{1,0:T(8,128)(2,1)}) async-done(((bf16[1024,128]{1,0:T(8,128)(2,1)}, bf16[1024,128]{1,0:T(8,128)(2,1)}), (bf16[1024,128]{1,0:T(8,128)(2,1)}, bf16[1024,128]{1,0:T(8,128)(2,1)})) %all-reduce.56.cloned.1.call-update) | async-done | bytes 524304 | tf_op jit(solution)/shard_map/psum | solution.py:282
  529.3 29.1 %reduce-scatter.16.cloned.1.call-done = bf16[256,1024]{1,0:T(8,128)(2,1)} async-done(((bf16[1024,1024]{1,0:T(8,128)(2,1)}), bf16[256,1024]{1,0:T(8,128)(2,1)}) %reduce-scatter.16.cloned.1.call-update) | async-done | bytes 524304 | tf_op jit(solution)/shard_map/reduce_scatter | solution.py:304
  558.4 38.2 %reduce-scatter.18.cloned.1.call-done = bf16[256,1024]{1,0:T(8,128)(2,1)} async-done(((bf16[1024,1024]{1,0:T(8,128)(2,1)}), bf16[256,1024]{1,0:T(8,128)(2,1)}) %reduce-scatter.18.cloned.1.call-update) | async-done | bytes 524304 | tf_op jit(solution)/shard_map/reduce_scatter | solution.py:301
  605.8 33.1 %all-gather.27.cloned.1.call-done = bf16[1024,1024]{1,0:T(8,128)(2,1)} async-done(((bf16[256,1024]{1,0:T(8,128)(2,1)}), bf16[1024,1024]{1,0:T(8,128)(2,1)}) %all-gather.27.cloned.1.call-update) | async-done | bytes 2097168 | tf_op jit(solution)/shard_map/all_gather | solution.py:102
  653.6 23.1 %all-gather.29.cloned.1.call-done = bf16[1024,1024]{1,0:T(8,128)(2,1)} async-done(((bf16[256,1024]{1,0:T(8,128)(2,1)}), bf16[1024,1024]{1,0:T(8,128)(2,1)}) %all-gather.29.cloned.1.call-update) | async-done | bytes 2097168 | tf_op jit(solution)/shard_map/all_gather | solution.py:103
  683.2 13.9 fusion.38
  737.0 29.8 %all-reduce.54.cloned.1.call-done = (bf16[1024,128]{1,0:T(8,128)(2,1)}, bf16[1024,128]{1,0:T(8,128)(2,1)}) async-done(((bf16[1024,128]{1,0:T(8,128)(2,1)}, bf16[1024,128]{1,0:T(8,128)(2,1)}), (bf16[1024,128]{1,0:T(8,128)(2,1)}, bf16[1024,128]{1,0:T(8,128)(2,1)})) %all-reduce.54.cloned.1.call-update) | async-done | bytes 524304 | tf_op jit(solution)/shard_map/psum | solution.py:130
  769.0 36.1 %reduce-scatter.12.cloned.1.call-done = bf16[256,1024]{1,0:T(8,128)(2,1)} async-done(((bf16[1024,1024]{1,0:T(8,128)(2,1)}), bf16[256,1024]{1,0:T(8,128)(2,1)}) %reduce-scatter.12.cloned.1.call-update) | async-done | bytes 524304 | tf_op jit(solution)/shard_map/reduce_scatter | solution.py:142
  821.7 20.4 %all-gather.43.cloned.1.call-done = bf16[1024,1024]{1,0:T(8,128)(2,1)} async-done(((bf16[256,1024]{1,0:T(8,128)(2,1)}), bf16[1024,1024]{1,0:T(8,128)(2,1)}) %all-gather.43.cloned.1.call-update) | async-done | bytes 2097168 | tf_op jit(solution)/shard_map/all_gather | solution.py:219
  852.2 27.7 %all-gather.45.cloned.1.call-done = bf16[1024,1024]{1,0:T(8,128)(2,1)} async-done(((bf16[256,1024]{1,0:T(8,128)(2,1)}), bf16[1024,1024]{1,0:T(8,128)(2,1)}) %all-gather.45.cloned.1.call-update) | async-done | bytes 2097168 | tf_op jit(solution)/shard_map/all_gather | solution.py:102
  898.7 16.2 multiply_reduce_fusion.1
  985.9 22.7 %all-reduce.52.cloned.1.call-done = (bf16[1024,128]{1,0:T(8,128)(2,1)}, bf16[1024,128]{1,0:T(8,128)(2,1)}) async-done(((bf16[1024,128]{1,0:T(8,128)(2,1)}, bf16[1024,128]{1,0:T(8,128)(2,1)}), (bf16[1024,128]{1,0:T(8,128)(2,1)}, bf16[1024,128]{1,0:T(8,128)(2,1)})) %all-reduce.52.cloned.1.call-update) | async-done | bytes 524304 | tf_op jit(solution)/shard_map/psum | solution.py:276
  1016.6 29.7 %all-gather.51.cloned.1.call-done = bf16[1024,1024]{1,0:T(8,128)(2,1)} async-done(((bf16[256,1024]{1,0:T(8,128)(2,1)}), bf16[1024,1024]{1,0:T(8,128)(2,1)}) %all-gather.51.cloned.1.call-update) | async-done | bytes 2097168 | tf_op jit(solution)/shard_map/all_gather | solution.py:102
  1104.9 16.8 all-gather.31.cloned.1.call-done
  1163.5 35.2 %reduce-scatter.22.cloned.1.call-done = bf16[256,1024]{1,0:T(8,128)(2,1)} async-done(((bf16[1024,1024]{1,0:T(8,128)(2,1)}), bf16[256,1024]{1,0:T(8,128)(2,1)}) %reduce-scatter.22.cloned.1.call-update) | async-done | bytes 524304 | tf_op jit(solution)/shard_map/reduce_scatter | solution.py:301
  1208.6 27.8 %all-gather.33.cloned.1.call-done = bf16[1024,1024]{1,0:T(8,128)(2,1)} async-done(((bf16[256,1024]{1,0:T(8,128)(2,1)}), bf16[1024,1024]{1,0:T(8,128)(2,1)}) %all-gather.33.cloned.1.call-update) | async-done | bytes 2097168 | tf_op jit(solution)/shard_map/all_gather | solution.py:103
  1245.4 13.8 fusion.41
  1263.7 17.0 %all-gather.49.cloned.1.call-done = bf16[1024,1024]{1,0:T(8,128)(2,1)} async-done(((bf16[256,1024]{1,0:T(8,128)(2,1)}), bf16[1024,1024]{1,0:T(8,128)(2,1)}) %all-gather.49.cloned.1.call-update) | async-done | bytes 2097168 | tf_op jit(solution)/shard_map/all_gather | solution.py:219
  1366.2 44.8 %all-reduce.50.cloned.1.call-done = (bf16[1024,128]{1,0:T(8,128)(2,1)}, bf16[1024,128]{1,0:T(8,128)(2,1)}, bf16[1024,128]{1,0:T(8,128)(2,1)}, bf16[1024,128]{1,0...) async-done(((bf16[1024,128]{1,0:T(8,128)(2,1)}, ...) | async-done | bytes 2621456 | tf_op jit(solution)/shard_map/psum | solution.py:130
  1454.5 79.8 %all-reduce.60.cloned.1.call-done = (bf16[1,1024,128]{2,1,0:T(8,128)(2,1)}, bf16[1,128,3,256]{1,3,2,0:T(8,128)(2,1)}, bf16[1,256,128]{2,1,0:T(8,128)(2,1)}, bf16...) async-done(((bf16[1,1024,128]{2,1,0:T(8,128)(2,1)}, ...) | async-done | bytes 1835024 | tf_op jit(solution)/shard_map/psum | solution.py:428
  1548.5 22.8 %reduce-scatter.24.cloned.1.call-done = bf16[256,1024]{1,0:T(8,128)(2,1)} async-done(((bf16[1024,1024]{1,0:T(8,128)(2,1)}), bf16[256,1024]{1,0:T(8,128)(2,1)}) %reduce-scatter.24.cloned.1.call-update) | async-done | bytes 524304 | tf_op jit(solution)/shard_map/reduce_scatter | solution.py:304
  1571.3 38.3 %reduce-scatter.26.cloned.1.call-done = bf16[256,1024]{1,0:T(8,128)(2,1)} async-done(((bf16[1024,1024]{1,0:T(8,128)(2,1)}), bf16[256,1024]{1,0:T(8,128)(2,1)}) %reduce-scatter.26.cloned.1.call-update) | async-done | bytes 524304 | tf_op jit(solution)/shard_map/reduce_scatter | solution.py:301
  1613.5 75.8 %all-reduce.36 = (f32[1,2,1024]{2,1,0:T(2,128)}, f32[1,2,1024]{2,1,0:T(2,128)}) all-reduce(f32[1,2,1024]{2,1,0:T(2,128)S(1)} %add_bitcast_fusion.7, f32[1,2,1024]{2,1,0:T(2,128)S(1)} %add_bitcast_fusion.6), channel_id=1, replica_groups=mesh['section'=2,'dp'=4,'tensor'=4] {'dp','tensor'}, use_global_device_ids=true, to_apply=%region_74.75 | all-reduce | flops 4096 | bytes 32768 | tf_op jit(solution)/shard_map/psum | solution.py:437
  (866 shorter events, 688.4 us)
Async XLA Ops:
  9.3 87.2 %all-gather.23.cloned.1.call-start = ((), (), s32[]{:S(2)}) async-start(), calls=%async_computation.9 | async-start | bytes 2621440 | tf_op jit(solution)/shard_map/all_gather | solution.py:102
  16.5 127.5 %all-gather.55.cloned.1.call-start = ((), (), s32[]{:S(2)}) async-start(), calls=%async_computation.34 | async-start | bytes 2621440 | tf_op jit(solution)/shard_map/all_gather | solution.py:79
  17.3 163.1 %all-gather.25.cloned.1.call-start = ((), (), s32[]{:S(2)}) async-start(), calls=%async_computation.10 | async-start | bytes 2621440 | tf_op jit(solution)/shard_map/all_gather | solution.py:103
  17.9 210.2 %all-gather.57.cloned.1.call-start = ((), (), s32[]{:S(2)}) async-start(), calls=%async_computation.35 | async-start | bytes 2621440 | tf_op jit(solution)/shard_map/all_gather | solution.py:83
  18.4 257.3 %all-reduce.58.cloned.1.call-start = ((), (), s32[]{:S(2)}) async-start(), calls=%async_computation.40 | async-start | bytes 1048576 | tf_op jit(solution)/shard_map/psum | solution.py:130
  204.9 109.7 %reduce-scatter.10.cloned.1.call-start = ((), (), s32[]{:S(2)}) async-start(), calls=%async_computation.11 | async-start | bytes 2621440 | tf_op jit(solution)/shard_map/reduce_scatter | solution.py:142
  234.7 117.7 %all-gather.37.cloned.1.call-start = ((), (), s32[]{:S(2)}) async-start(), calls=%async_computation.19 | async-start | bytes 2621440 | tf_op jit(solution)/shard_map/all_gather | solution.py:219
  237.2 153.2 %all-gather.39.cloned.1.call-start = ((), (), s32[]{:S(2)}) async-start(), calls=%async_computation.21 | async-start | bytes 2621440 | tf_op jit(solution)/shard_map/all_gather | solution.py:102
  323.0 123.7 %all-gather.35.cloned.1.call-start = ((), (), s32[]{:S(2)}) async-start(), calls=%async_computation.18 | async-start | bytes 2621440 | tf_op jit(solution)/shard_map/all_gather | solution.py:103
  364.2 154.4 %all-reduce.56.cloned.1.call-start = ((), (), s32[]{:S(2)}) async-start(), calls=%async_computation.39 | async-start | bytes 1048576 | tf_op jit(solution)/shard_map/psum | solution.py:282
  472.2 86.2 %reduce-scatter.16.cloned.1.call-start = ((), (), s32[]{:S(2)}) async-start(), calls=%async_computation.20 | async-start | bytes 2621440 | tf_op jit(solution)/shard_map/reduce_scatter | solution.py:304
  523.0 73.5 %reduce-scatter.18.cloned.1.call-start = ((), (), s32[]{:S(2)}) async-start(), calls=%async_computation.22 | async-start | bytes 2621440 | tf_op jit(solution)/shard_map/reduce_scatter | solution.py:301
  529.0 109.9 %all-gather.27.cloned.1.call-start = ((), (), s32[]{:S(2)}) async-start(), calls=%async_computation.12 | async-start | bytes 2621440 | tf_op jit(solution)/shard_map/all_gather | solution.py:102
  603.4 73.2 %all-gather.29.cloned.1.call-start = ((), (), s32[]{:S(2)}) async-start(), calls=%async_computation.13 | async-start | bytes 2621440 | tf_op jit(solution)/shard_map/all_gather | solution.py:103
  604.0 162.7 %all-reduce.54.cloned.1.call-start = ((), (), s32[]{:S(2)}) async-start(), calls=%async_computation.38 | async-start | bytes 1048576 | tf_op jit(solution)/shard_map/psum | solution.py:130
  721.1 83.9 %reduce-scatter.12.cloned.1.call-start = ((), (), s32[]{:S(2)}) async-start(), calls=%async_computation.14 | async-start | bytes 2621440 | tf_op jit(solution)/shard_map/reduce_scatter | solution.py:142
  729.3 112.8 %all-gather.43.cloned.1.call-start = ((), (), s32[]{:S(2)}) async-start(), calls=%async_computation.24 | async-start | bytes 2621440 | tf_op jit(solution)/shard_map/all_gather | solution.py:219
  736.9 143.0 %all-gather.45.cloned.1.call-start = ((), (), s32[]{:S(2)}) async-start(), calls=%async_computation.26 | async-start | bytes 2621440 | tf_op jit(solution)/shard_map/all_gather | solution.py:102
  817.1 118.6 %all-gather.41.cloned.1.call-start = ((), (), s32[]{:S(2)}) async-start(), calls=%async_computation.23 | async-start | bytes 2621440 | tf_op jit(solution)/shard_map/all_gather | solution.py:103
  852.2 156.4 %all-reduce.52.cloned.1.call-start = ((), (), s32[]{:S(2)}) async-start(), calls=%async_computation.37 | async-start | bytes 1048576 | tf_op jit(solution)/shard_map/psum | solution.py:276
  962.8 83.5 %all-gather.51.cloned.1.call-start = ((), (), s32[]{:S(2)}) async-start(), calls=%async_computation.31 | async-start | bytes 2621440 | tf_op jit(solution)/shard_map/all_gather | solution.py:102
  963.6 120.5 %all-gather.47.cloned.1.call-start = ((), (), s32[]{:S(2)}) async-start(), calls=%async_computation.28 | async-start | bytes 2621440 | tf_op jit(solution)/shard_map/all_gather | solution.py:103
  964.3 157.4 %all-gather.31.cloned.1.call-start = ((), (), s32[]{:S(2)}) async-start(), calls=%async_computation.15 | async-start | bytes 2621440 | tf_op jit(solution)/shard_map/all_gather | solution.py:102
  969.9 193.7 %reduce-scatter.20.cloned.1.call-start = ((), (), s32[]{:S(2)}) async-start(), calls=%async_computation.25 | async-start | bytes 2621440 | tf_op jit(solution)/shard_map/reduce_scatter | solution.py:304
  1012.9 185.9 %reduce-scatter.22.cloned.1.call-start = ((), (), s32[]{:S(2)}) async-start(), calls=%async_computation.27 | async-start | bytes 2621440 | tf_op jit(solution)/shard_map/reduce_scatter | solution.py:301
  1071.9 164.5 %all-gather.33.cloned.1.call-start = ((), (), s32[]{:S(2)}) async-start(), calls=%async_computation.16 | async-start | bytes 2621440 | tf_op jit(solution)/shard_map/all_gather | solution.py:103
  1104.5 176.3 %all-gather.49.cloned.1.call-start = ((), (), s32[]{:S(2)}) async-start(), calls=%async_computation.29 | async-start | bytes 2621440 | tf_op jit(solution)/shard_map/all_gather | solution.py:219
  1245.3 165.6 %all-reduce.50.cloned.1.call-start = ((), (), s32[]{:S(2)}) async-start(), calls=%async_computation.36 | async-start | bytes 5242880 | tf_op jit(solution)/shard_map/psum | solution.py:130
  1330.4 119.5 %reduce-scatter.14.cloned.1.call-start = ((), (), s32[]{:S(2)}) async-start(), calls=%async_computation.17 | async-start | bytes 2621440 | tf_op jit(solution)/shard_map/reduce_scatter | solution.py:142
  1347.8 186.5 %all-reduce.60.cloned.1.call-start = ((), (), s32[]{:S(2)}) async-start(), calls=%async_computation.41 | async-start | bytes 3670016 | tf_op jit(solution)/shard_map/psum | solution.py:428
  1421.3 150.0 %reduce-scatter.24.cloned.1.call-start = ((), (), s32[]{:S(2)}) async-start(), calls=%async_computation.30 | async-start | bytes 2621440 | tf_op jit(solution)/shard_map/reduce_scatter | solution.py:304
  1427.6 182.0 %reduce-scatter.26.cloned.1.call-start = ((), (), s32[]{:S(2)}) async-start(), calls=%async_computation.32 | async-start | bytes 2621440 | tf_op jit(solution)/shard_map/reduce_scatter | solution.py:301
  (250 other events, 8632.5 us)
Sparse Core Ops, SparseCore 0:
  10.2 48.8 all-gather.52
  61.5 34.9 all-gather.22
  98.0 45.9 all-gather.54
  146.3 34.0 all-gather.24
  181.8 46.2 all-gather.56
  232.0 43.6 all-reduce.57
  279.3 35.1 reduce-scatter.9
  317.1 35.2 all-gather.36
  355.0 35.2 all-gather.38
  392.8 35.2 all-gather.34
  472.3 46.3 all-reduce.55
  523.2 35.1 reduce-scatter.15
  561.4 35.1 reduce-scatter.17
  603.5 35.2 all-gather.26
  641.3 35.2 all-gather.28
  721.2 45.4 all-reduce.53
  769.8 35.1 reduce-scatter.11
  806.8 35.2 all-gather.42
  844.5 35.2 all-gather.44
  882.1 35.2 all-gather.40
  962.9 45.5 all-reduce.51
  1010.9 35.2 all-gather.50
  1048.7 35.2 all-gather.46
  1086.3 35.2 all-gather.30
  1125.2 35.1 reduce-scatter.19
  1163.5 35.1 reduce-scatter.21
  1201.0 35.2 all-gather.32
  1245.4 35.3 all-gather.48
  1330.5 80.3 all-reduce.49
  1414.6 35.1 reduce-scatter.13
  1453.9 80.2 all-reduce.59
  1574.4 35.1 reduce-scatter.25
  (1 shorter events, 33.9 us)
where the time goes:
time: 1710 us; the launch traced here: 1700 us
  waiting for transfers between devices  864 us (51%)
  matrix products  547 us (32%)
  other arithmetic  119 us (7%)
  blocking collectives  101 us (6%)
  local copies, waits for them, and re-layouts  41.8 us (2%)
  between operations  18.3 us (1%)
    dot_general x54, matrix products, matrix_product(): return jnp.dot(left_side, right_side, preferred_element_type=jnp.float32)  221 us
    all_gather x6, waiting for transfers between devices, forward(): lax.all_gather(first_normalized.astype(jnp.bfloat16), 'tensor', axis=0, t...  171 us
    psum x3, waiting for transfers between devices, forward(): lax.psum(matrix_product(attention_result, fac_a_out).astype(jnp.bfloat16)...  112 us
    reduce_scatter x3, waiting for transfers between devices, backward(): lax.psum_scatter(grad_one.astype(jnp.bfloat16), 'tensor', scatter_dimensi...  112 us
    all_gather x6, waiting for transfers between devices, forward(): lax.all_gather(second_normalized.astype(jnp.bfloat16), 'tensor', axis=0,...  89.5 us
    dot_general x36, matrix products, contracted_with(): lax.dot_general(left_side, right_side, (((1,), (1,)), ((), ())), preferre...  87.9 us
    psum x1, waiting for transfers between devices, per_device(): lax.psum(sum_a_qkv.astype(jnp.bfloat16), 'dp').astype(jnp.float32)  79.8 us
    psum x1, blocking collectives, per_device(): sum_gain, sum_bias = lax.psum((sum_gain, sum_bias), ('dp', 'tensor'))  75.8 us
  transfers between devices with their start and end apart: 37, of which 33 were waited for; matrix products, arithmetic and copies ran while one was open for 31% of the time, Pallas kernels for 0%

commit v1 on v0

v1 whole, which is shorter than its diff:
```python
import functools

import jax
import jax.numpy as jnp
from jax import lax
from jax.experimental import pallas as pl
from jax.experimental.pallas import tpu as pltpu
from jax.sharding import PartitionSpec as P

HEAD = 64
ROT = 16
ADAPTER_SCALE = 0.25
EPSILON = 1e-05
MASKED = -1e30
BF = jnp.bfloat16
F32 = jnp.float32
MESH = pl.DeviceIdType.MESH


def nn(a, b):
    return lax.dot_general(a, b, (((1,), (0,)), ((), ())), preferred_element_type=F32)


def nt(a, b):
    return lax.dot_general(a, b, (((1,), (1,)), ((), ())), preferred_element_type=F32)


def make_kernel(T, DP, M, R, D, QC, FFL, RANK):
    L = R * T
    DR = D // DP
    W = D + 2 * RANK
    PAIRS = QC // 128
    HEADS = QC // HEAD
    TILE = 256
    HALF = L // 2

    def kernel(
        x_in, ct_in, wq_in, wup_in, wout_in, wdn_in,
        aq, bq, ao, bo, au, bu, ad, bd, gain, bias, cos_t, sin_t, negb,
        act, ig, ga_out, gr_out, gb_out, h_hbm, dg_hbm,
        wq, wup, wout, wdn, xh, t12t, qh, kp, vp, kT, vT, oT, lse, hw, dg,
        todt, sbuf, rbuf, sxr, sgr, sxs, dz, doh, delta, edot, dk, dv, dqt, dqkv,
        ga, gr, gb, xw, yw,
        w_ls, w_ss, w_rs, x_ss, x_rs, r_ss, r_rs, z_ss, z_rs, c_ss, c_rs, l_s,
    ):
        s = lax.axis_index("section")
        d = lax.axis_index("dp")
        t = lax.axis_index("tensor")
        other = 1 - s

        barrier = pltpu.get_barrier_semaphore()
        for k in range(1, T):
            pl.semaphore_signal(
                barrier, inc=1, device_id={"tensor": lax.rem(t + k, T)}, device_id_type=MESH
            )
        for k in range(1, DP):
            pl.semaphore_signal(
                barrier, inc=1, device_id={"dp": lax.rem(d + k, DP)}, device_id_type=MESH
            )
        pl.semaphore_signal(barrier, inc=1, device_id={"section": other}, device_id_type=MESH)
        pl.semaphore_wait(barrier, T + DP - 1)

        def weight_refs(index, owner):
            if index < 2:
                rows = pl.ds(pl.multiple_of(owner * DR, DR), DR)
                return (wq_in, wup_in)[index], (wq, wup)[index].at[rows]
            return (wout_in, wdn_in)[index - 2], (wout, wdn)[index - 2].at[owner]

        def weight_copy(index, k):
            src, dst = weight_refs(index, d)
            return pltpu.make_async_remote_copy(
                src_ref=src, dst_ref=dst,
                send_sem=w_ss.at[index, k - 1], recv_sem=w_rs.at[index, k - 1],
                device_id={"dp": lax.rem(d + k, DP)}, device_id_type=MESH,
            )

        def weight_local(index):
            src, dst = weight_refs(index, d)
            return pltpu.make_async_copy(src, dst, w_ls.at[index])

        for index in range(4):
            weight_local(index).start()
            for k in range(1, DP):
                weight_copy(index, k).start()

        def weights_ready(index):
            weight_local(index).wait()
            for k in range(1, DP):
                weight_copy(index, k).wait_recv()

        ga[...] = jnp.zeros_like(ga)
        gr[...] = jnp.zeros_like(gr)
        gb[...] = jnp.zeros_like(gb)

        def rows_copy(buf, m, k, ssem, rsem):
            place = m * T + t
            return pltpu.make_async_remote_copy(
                src_ref=buf.at[place], dst_ref=buf.at[place],
                send_sem=ssem.at[k - 1], recv_sem=rsem.at[m * (T - 1) + k - 1],
                device_id={"tensor": lax.rem(t + k, T)}, device_id_type=MESH,
            )

        def rows_wait(buf, m, c, ssem, rsem):
            place = m * T + lax.rem(t - c + T, T)
            pltpu.make_async_remote_copy(
                src_ref=buf.at[place], dst_ref=buf.at[place],
                send_sem=ssem.at[0], recv_sem=rsem.at[m * (T - 1) + c - 1],
                device_id={"tensor": lax.rem(t + 1, T)}, device_id_type=MESH,
            ).wait_recv()

        def block_copy(phase, i):
            k = lax.rem(i - t + T, T)
            slot = phase * (T - 1) + k - 1
            return pltpu.make_async_remote_copy(
                src_ref=sbuf.at[i], dst_ref=rbuf.at[slot],
                send_sem=r_ss.at[i], recv_sem=r_rs.at[slot],
                device_id={"tensor": i}, device_id_type=MESH,
            )

        def block_wait(phase, k):
            slot = phase * (T - 1) + k - 1
            pltpu.make_async_remote_copy(
                src_ref=sbuf.at[0], dst_ref=rbuf.at[slot],
                send_sem=r_ss.at[0], recv_sem=r_rs.at[slot],
                device_id={"tensor": lax.rem(t + k, T)}, device_id_type=MESH,
            ).wait_recv()

        def section_copy(m, phase):
            dst = (sxr, sgr)[phase]
            return pltpu.make_async_remote_copy(
                src_ref=sxs, dst_ref=dst.at[m],
                send_sem=c_ss.at[0], recv_sem=c_rs.at[phase * M + m],
                device_id={"section": other}, device_id_type=MESH,
            )

        def local_copy(src, dst, index):
            return pltpu.make_async_copy(src, dst, l_s.at[index])

        def norm_parts(x):
            mean = jnp.mean(x, axis=-1, keepdims=True)
            centred = x - mean
            spread = jnp.mean(centred * centred, axis=-1, keepdims=True)
            rstd = lax.rsqrt(spread + EPSILON)
            return centred * rstd, rstd

        def load_x(m):
            @pl.when(s == 0)
            def _():
                copy = local_copy(x_in.at[m], xw, 0)
                copy.start()
                copy.wait()

        lane = lax.broadcasted_iota(jnp.int32, (R, 128), 1)
        in_first = lax.rem(lane, HEAD) < ROT // 2
        head_low = lane < HEAD

        def turn(v, cosine, sine):
            swapped = jnp.where(in_first, pltpu.roll(v, 128 - ROT // 2, 1), pltpu.roll(v, ROT // 2, 1))
            return v * cosine + swapped * sine

        causal = lax.broadcasted_iota(jnp.int32, (R, R), 0) <= lax.broadcasted_iota(
            jnp.int32, (R, R), 1
        )

        def scores_t(m, p, i, j, q):
            keys = kp[m * PAIRS + p, j * R:(j + 1) * R, :]
            sc = nt(keys, q)
            if j == i:
                sc = jnp.where(causal, sc, MASKED)
            if i * R >= HALF and j * R < HALF:
                sc = sc + negb[m]
            return sc

        def forward(m, carry):
            load_x(m)

            @pl.when(s == 1)
            def _():
                section_copy(m, 0).wait_recv()
                xw[...] = sxr[m].astype(F32)

            xhat, _ = norm_parts(xw[...])
            xh[m * T + t] = xhat.astype(BF)
            for k in range(1, T):
                rows_copy(xh, m, k, x_ss, x_rs).start()

            @pl.when(m == 0)
            def _():
                weights_ready(0)
                weights_ready(1)

            def chunk(c, carry):
                src = lax.rem(t - c + T, T)

                @pl.when(c > 0)
                def _():
                    rows_wait(xh, m, c, x_ss, x_rs)

                rows = pl.ds(pl.multiple_of(src * R, R), R)
                xhc = xh[m * T + src].astype(F32)
                n1 = (xhc * gain[0:1] + bias[0:1]).astype(BF)
                n2 = (xhc * gain[1:2] + bias[1:2]).astype(BF)
                t1 = nn(n1, aq[...]).astype(BF)
                t2 = nn(n2, au[...]).astype(BF)
                t12t[m, 0:RANK, rows] = t1.T
                t12t[m, RANK:2 * RANK, rows] = t2.T
                cosine = cos_t[m, rows, :]
                sine = sin_t[m, rows, :]
                for part in range(3):
                    cols = slice(part * QC, (part + 1) * QC)
                    val = nn(n1, wq[:, cols]) + nn(t1, bq[:, cols])
                    if part == 2:
                        vb = val.astype(BF)
                        for p in range(PAIRS):
                            vp[m * PAIRS + p, rows, :] = vb[:, p * 128:(p + 1) * 128]
                        vT[:, rows] = vb.T
                    else:
                        for p in range(PAIRS):
                            v = turn(val[:, p * 128:(p + 1) * 128], cosine, sine)
                            if part == 0:
                                v = v * 0.125
                                qh[m * HEADS + 2 * p, rows, :] = jnp.where(head_low, v, 0.0).astype(BF)
                                qh[m * HEADS + 2 * p + 1, rows, :] = jnp.where(head_low, 0.0, v).astype(BF)
                            else:
                                vb = v.astype(BF)
                                kp[m * PAIRS + p, rows, :] = vb
                                kT[m, p * 128:(p + 1) * 128, rows] = vb.T
                for n0 in range(0, FFL, TILE):
                    cols = slice(n0, n0 + TILE)
                    u = nn(n2, wup[:, cols]) + nn(t2, bu[:, cols])
                    phi = 0.5 * (1.0 + lax.erf(u * 0.7071067811865476))
                    hw[rows, cols] = (u * phi).astype(BF)
                    dg[rows, cols] = (
                        phi + u * (0.3989422804014327 * jnp.exp(-0.5 * u * u))
                    ).astype(BF)
                return carry

            lax.fori_loop(0, T, chunk, 0)
            for k in range(1, T):
                rows_copy(xh, m, k, x_ss, x_rs).wait_send()
            local_copy(hw, h_hbm.at[m], 1).start()
            local_copy(dg, dg_hbm.at[m], 2).start()

            @pl.when(m == 0)
            def _():
                weights_ready(2)
                weights_ready(3)

            for i in range(T):
                icols = slice(i * R, (i + 1) * R)

                def pair(p, carry, i=i, icols=icols):
                    for hh in range(2):
                        h = 2 * p + hh
                        q = qh[m * HEADS + h, icols, :]
                        hrows = pl.ds(pl.multiple_of(h * HEAD, HEAD), HEAD)
                        blocks = [scores_t(m, p, i, j, q) for j in range(i + 1)]
                        top = functools.reduce(
                            jnp.maximum, [jnp.max(b, axis=0, keepdims=True) for b in blocks]
                        )
                        total = jnp.zeros_like(top)
                        acc = jnp.zeros((HEAD, R), F32)
                        for j in range(i + 1):
                            e = jnp.exp(blocks[j] - top)
                            total = total + jnp.sum(e, axis=0, keepdims=True)
                            acc = acc + nn(vT[hrows, j * R:(j + 1) * R], e.astype(BF))
                        oT[m, hrows, icols] = (acc * (1.0 / total)).astype(BF)
                        lse[pl.ds(m * HEADS + h, 1), icols] = top + jnp.log(total)
                    return carry

                lax.fori_loop(0, PAIRS, pair, 0)
                o = oT[m, :, icols].T
                hrow = hw[icols, :]
                for j in range(DP):
                    sbuf[i, :, j * DR:(j + 1) * DR] = (nn(o, wout[j]) + nn(hrow, wdn[j])).astype(BF)
                sbuf[i, :, D:D + RANK] = nn(o, ao[...]).astype(BF)
                sbuf[i, :, D + RANK:W] = nn(hrow, ad[...]).astype(BF)

                @pl.when(t != i)
                def _(i=i):
                    block_copy(m, i).start()

            for k in range(1, T):
                block_wait(m, k)

            def summed(lo, hi):
                v = sbuf[t, :, lo:hi].astype(F32)
                for k in range(T - 1):
                    v = v + rbuf[m * (T - 1) + k, :, lo:hi].astype(F32)
                return v

            to = summed(D, D + RANK).astype(BF)
            td = summed(D + RANK, W).astype(BF)
            todt[m, 0:RANK, :] = to.T
            todt[m, RANK:2 * RANK, :] = td.T
            for n0 in range(0, D, TILE):
                cols = slice(n0, n0 + TILE)
                y = xw[:, cols] + summed(n0, n0 + TILE) + nn(to, bo[:, cols]) + nn(td, bd[:, cols])
                xw[:, cols] = y
                sxs[:, cols] = y.astype(BF)

            @pl.when(s == 0)
            def _():
                section_copy(m, 0).start()

            out = local_copy(xw, act.at[m], 3)
            out.start()
            out.wait()
            for i in range(T):
                @pl.when(t != i)
                def _(i=i):
                    block_copy(m, i).wait_send()
            local_copy(hw, h_hbm.at[m], 1).wait()
            local_copy(dg, dg_hbm.at[m], 2).wait()

            @pl.when(s == 0)
            def _():
                section_copy(m, 0).wait_send()
            return carry

        lax.fori_loop(0, M, forward, 0)

        def backward(m, carry):
            local_copy(dg_hbm.at[m], dg, 2).start()
            local_copy(h_hbm.at[m], hw, 1).start()

            @pl.when(s == 1)
            def _():
                copy = local_copy(ct_in.at[m], yw, 3)
                copy.start()
                copy.wait()
                xw[...] = sxr[m].astype(F32)

            @pl.when(s == 0)
            def _():
                section_copy(m, 1).wait_recv()
                yw[...] = sgr[m].astype(F32)

            load_x(m)
            dz[m * T + t] = yw[...].astype(BF)
            for k in range(1, T):
                rows_copy(dz, m, k, z_ss, z_rs).start()
            dk[...] = jnp.zeros_like(dk)
            dv[...] = jnp.zeros_like(dv)
            local_copy(dg_hbm.at[m], dg, 2).wait()

            def chunk(c, carry):
                src = lax.rem(t - c + T, T)

                @pl.when(c > 0)
                def _():
                    rows_wait(dz, m, c, z_ss, z_rs)

                rows = pl.ds(pl.multiple_of(src * R, R), R)
                place = m * T + src
                full = dz[place]
                eo = nt(full, bo[...]).astype(BF)
                ed = nt(full, bd[...]).astype(BF)
                edot[0:RANK, rows] = eo.T
                edot[RANK:2 * RANK, rows] = ed.T
                do = nt(eo, ao[...])
                for j in range(DP):
                    do = do + nt(full[:, j * DR:(j + 1) * DR], wout[j])
                dob = do.astype(BF)
                for p in range(PAIRS):
                    v = dob[:, p * 128:(p + 1) * 128]
                    zero = jnp.zeros_like(v)
                    doh[2 * p, rows, :] = jnp.where(head_low, v, zero)
                    doh[2 * p + 1, rows, :] = jnp.where(head_low, zero, v)
                prod = dob.T.astype(F32) * oT[m, :, rows].astype(F32)
                for h in range(HEADS):
                    delta[h:h + 1, rows] = jnp.sum(
                        prod[h * HEAD:(h + 1) * HEAD], axis=0, keepdims=True
                    )
                for n0 in range(0, FFL, TILE):
                    cols = slice(n0, n0 + TILE)
                    v = nt(ed, ad[cols, :])
                    for j in range(DP):
                        v = v + nt(full[:, j * DR:(j + 1) * DR], wdn[j, cols, :])
                    dg[rows, cols] = (v * dg[rows, cols].astype(F32)).astype(BF)
                return carry

            lax.fori_loop(0, T, chunk, 0)
            for k in range(1, T):
                rows_copy(dz, m, k, z_ss, z_rs).wait_send()

            for i in range(T):
                icols = slice(i * R, (i + 1) * R)

                def pair(p, carry, i=i, icols=icols):
                    for hh in range(2):
                        h = 2 * p + hh
                        q = qh[m * HEADS + h, icols, :]
                        do = doh[h, icols, :]
                        hrows = pl.ds(pl.multiple_of(h * HEAD, HEAD), HEAD)
                        low = lse[pl.ds(m * HEADS + h, 1), icols]
                        dlt = delta[pl.ds(h, 1), icols]
                        acc = jnp.zeros((HEAD, R), F32)
                        for j in range(i + 1):
                            jrows = slice(j * R, (j + 1) * R)
                            prob = jnp.exp(scores_t(m, p, i, j, q) - low)
                            dp_t = nt(vp[m * PAIRS + p, jrows, :], do)
                            ds_t = (prob * (dp_t - dlt)).astype(BF)
                            dv[p, jrows, :] += nn(prob.astype(BF), do)
                            dk[p, jrows, :] += nn(ds_t, q)
                            acc = acc + nn(kT[m, hrows, jrows], ds_t)
                        dqt[hrows, icols] = acc
                    return carry

                lax.fori_loop(0, PAIRS, pair, 0)

            def tail(c, carry):
                i = lax.rem(t + c + 1, T)
                rows = pl.ds(pl.multiple_of(i * R, R), R)
                cosine = cos_t[m, rows, :]
                sine = -sin_t[m, rows, :]
                dq = dqt[:, rows].T * 0.125
                for p in range(PAIRS):
                    lanes = slice(p * 128, (p + 1) * 128)
                    dqkv[rows, p * 128:(p + 1) * 128] = turn(dq[:, lanes], cosine, sine).astype(BF)
                    dqkv[rows, QC + p * 128:QC + (p + 1) * 128] = turn(
                        dk[p, rows, :], cosine, sine
                    ).astype(BF)
                    dqkv[rows, 2 * QC + p * 128:2 * QC + (p + 1) * 128] = dv[p, rows, :].astype(BF)
                dj = dqkv[rows, :]
                du = dg[rows, :]
                for n0 in range(0, D, TILE):
                    cols = slice(n0, n0 + TILE)
                    dn1 = nt(dj, wq[cols, :])
                    dn2 = nt(du, wup[cols, :])
                    xhc = xh[m * T + i, :, cols].astype(F32)
                    gb[0:1, cols] += jnp.sum(dn1 * xhc, axis=0, keepdims=True)
                    gb[1:2, cols] += jnp.sum(dn2 * xhc, axis=0, keepdims=True)
                    gb[2:3, cols] += jnp.sum(dn1, axis=0, keepdims=True)
                    gb[3:4, cols] += jnp.sum(dn2, axis=0, keepdims=True)
                    sbuf[i, :, cols] = (dn1 * gain[0:1, cols] + dn2 * gain[1:2, cols]).astype(BF)
                sbuf[i, :, D:D + RANK] = nt(dj, bq[...]).astype(BF)
                sbuf[i, :, D + RANK:W] = nt(du, bu[...]).astype(BF)

                @pl.when(t != i)
                def _():
                    block_copy(M + m, i).start()
                return carry

            lax.fori_loop(0, T, tail, 0)

            local_copy(h_hbm.at[m], hw, 1).wait()
            base = 0
            ga[:, base:base + 3 * QC] += ADAPTER_SCALE * nn(t12t[m, 0:RANK, :], dqkv[...])
            base += 3 * QC
            ga[:, base:base + FFL] += ADAPTER_SCALE * nn(t12t[m, RANK:2 * RANK, :], dg[...])
            base += FFL
            ga[:, base:base + QC] += nt(edot[0:RANK, :], oT[m])
            base += QC
            ga[:, base:base + FFL] += nn(edot[RANK:2 * RANK, :], hw[...])
            own = dz[m * T + t]
            gr[:, 2 * D:3 * D] += ADAPTER_SCALE * nn(todt[m, 0:RANK, :], own)
            gr[:, 3 * D:4 * D] += ADAPTER_SCALE * nn(todt[m, RANK:2 * RANK, :], own)

            for k in range(1, T):
                block_wait(M + m, k)

            def summed(lo, hi):
                v = sbuf[t, :, lo:hi].astype(F32)
                for k in range(T - 1):
                    v = v + rbuf[(M + m) * (T - 1) + k, :, lo:hi].astype(F32)
                return v

            e1 = summed(D, D + RANK).astype(BF)
            e2 = summed(D + RANK, W).astype(BF)
            xhat, rstd = norm_parts(xw[...])
            xw[...] = xhat
            n1 = (xhat * gain[0:1] + bias[0:1]).astype(BF)
            n2 = (xhat * gain[1:2] + bias[1:2]).astype(BF)
            gr[:, 0:D] += nn(e1.T, n1)
            gr[:, D:2 * D] += nn(e2.T, n2)
            pieces = []
            mean_g = jnp.zeros((R, 1), F32)
            mean_gx = jnp.zeros((R, 1), F32)
            for n0 in range(0, D, TILE):
                cols = slice(n0, n0 + TILE)
                dn1 = nt(e1, aq[cols, :])
                dn2 = nt(e2, au[cols, :])
                xhc = xw[:, cols]
                gb[0:1, cols] += jnp.sum(dn1 * xhc, axis=0, keepdims=True)
                gb[1:2, cols] += jnp.sum(dn2 * xhc, axis=0, keepdims=True)
                gb[2:3, cols] += jnp.sum(dn1, axis=0, keepdims=True)
                gb[3:4, cols] += jnp.sum(dn2, axis=0, keepdims=True)
                g = summed(n0, n0 + TILE) + dn1 * gain[0:1, cols] + dn2 * gain[1:2, cols]
                mean_g = mean_g + jnp.sum(g, axis=1, keepdims=True)
                mean_gx = mean_gx + jnp.sum(g * xhc, axis=1, keepdims=True)
                pieces.append(g)
            mean_g = mean_g * (1.0 / D)
            mean_gx = mean_gx * (1.0 / D)
            for n, n0 in enumerate(range(0, D, TILE)):
                cols = slice(n0, n0 + TILE)
                v = yw[:, cols] + (pieces[n] - mean_g - xw[:, cols] * mean_gx) * rstd
                yw[:, cols] = v
                sxs[:, cols] = v.astype(BF)

            @pl.when(s == 1)
            def _():
                section_copy(m, 1).start()

            out = local_copy(yw, ig.at[m], 3)
            out.start()
            out.wait()
            for i in range(T):
                @pl.when(t != i)
                def _(i=i):
                    block_copy(M + m, i).wait_send()

            @pl.when(s == 1)
            def _():
                section_copy(m, 1).wait_send()
            return carry

        lax.fori_loop(0, M, backward, 0)

        outs = [local_copy(ga, ga_out, 1), local_copy(gr, gr_out, 2), local_copy(gb, gb_out, 3)]
        for copy in outs:
            copy.start()
        for copy in outs:
            copy.wait()
        for index in range(4):
            for k in range(1, DP):
                weight_copy(index, k).wait_send()

    any_spec = pl.BlockSpec(memory_space=pl.ANY)
    vmem_spec = pl.BlockSpec(memory_space=pltpu.VMEM)
    smem_spec = pl.BlockSpec(memory_space=pltpu.SMEM)
    GA = 3 * QC + QC + 2 * FFL
    shapes = jax.ShapeDtypeStruct
    return pl.pallas_call(
        kernel,
        out_shape=(
            shapes((M, R, D), F32), shapes((M, R, D), F32),
            shapes((RANK, GA), F32), shapes((RANK, 4 * D), F32), shapes((8, D), F32),
            shapes((M, L, FFL), BF), shapes((M, L, FFL), BF),
        ),
        in_specs=[any_spec] * 6 + [vmem_spec] * 12 + [smem_spec],
        out_specs=(any_spec,) * 7,
        scratch_shapes=[
            pltpu.VMEM((D, 3 * QC), BF), pltpu.VMEM((D, FFL), BF),
            pltpu.VMEM((DP, QC, DR), BF), pltpu.VMEM((DP, FFL, DR), BF),
            pltpu.VMEM((M * T, R, D), BF),
            pltpu.VMEM((M, 2 * RANK, L), BF),
            pltpu.VMEM((M * HEADS, L, 128), BF),
            pltpu.VMEM((M * PAIRS, L, 128), BF),
            pltpu.VMEM((M * PAIRS, L, 128), BF),
            pltpu.VMEM((M, QC, L), BF),
            pltpu.VMEM((QC, L), BF),
            pltpu.VMEM((M, QC, L), BF),
            pltpu.VMEM((M * HEADS, L), F32),
            pltpu.VMEM((L, FFL), BF),
            pltpu.VMEM((L, FFL), BF),
            pltpu.VMEM((M, 2 * RANK, R), BF),
            pltpu.VMEM((T, R, W), BF),
            pltpu.VMEM((2 * M * (T - 1), R, W), BF),
            pltpu.VMEM((M, R, D), BF),
            pltpu.VMEM((M, R, D), BF),
            pltpu.VMEM((R, D), BF),
            pltpu.VMEM((M * T, R, D), BF),
            pltpu.VMEM((HEADS, L, 128), BF),
            pltpu.VMEM((8, L), F32),
            pltpu.VMEM((2 * RANK, L), BF),
            pltpu.VMEM((PAIRS, L, 128), F32),
            pltpu.VMEM((PAIRS, L, 128), F32),
            pltpu.VMEM((QC, L), F32),
            pltpu.VMEM((L, 3 * QC), BF),
            pltpu.VMEM((RANK, GA), F32),
            pltpu.VMEM((RANK, 4 * D), F32),
            pltpu.VMEM((8, D), F32),
            pltpu.VMEM((R, D), F32),
            pltpu.VMEM((R, D), F32),
            pltpu.SemaphoreType.DMA((4,)),
            pltpu.SemaphoreType.DMA((4, DP - 1)),
            pltpu.SemaphoreType.DMA((4, DP - 1)),
            pltpu.SemaphoreType.DMA((T - 1,)),
            pltpu.SemaphoreType.DMA((M * (T - 1),)),
            pltpu.SemaphoreType.DMA((T,)),
            pltpu.SemaphoreType.DMA((2 * M * (T - 1),)),
            pltpu.SemaphoreType.DMA((T - 1,)),
            pltpu.SemaphoreType.DMA((M * (T - 1),)),
            pltpu.SemaphoreType.DMA((1,)),
            pltpu.SemaphoreType.DMA((2 * M,)),
            pltpu.SemaphoreType.DMA((4,)),
        ],
        compiler_params=pltpu.CompilerParams(
            collective_id=0, has_side_effects=True, vmem_limit_bytes=63 * 2**20
        ),
    )


def rope_tables(split_flags, length):
    half = ROT // 2
    place = jnp.arange(length, dtype=jnp.int32)
    flags = split_flags.astype(jnp.int32)[:, None]
    places = (place[None] - length // 2 * jnp.where(place[None] >= length // 2, flags, 0)).astype(F32)
    inverse = 10000.0 ** (-jnp.arange(half, dtype=F32) * 2.0 / ROT)
    angles = places[:, :, None] * inverse
    cosine, sine = jnp.cos(angles), jnp.sin(angles)
    pad = HEAD - ROT
    rest = angles.shape[:2] + (pad,)
    cos_head = jnp.concatenate([cosine, cosine, jnp.ones(rest, F32)], axis=-1)
    sin_head = jnp.concatenate([-sine, sine, jnp.zeros(rest, F32)], axis=-1)
    return jnp.tile(cos_head, (1, 1, 2)), jnp.tile(sin_head, (1, 1, 2))


def solution(mesh):
    T = mesh.shape["tensor"]
    DP = mesh.shape["dp"]

    def per_device(
        inputs, cotangent, split,
        query_key_value_weight, output_weight, up_weight, down_weight,
        qkv_adapter_input, qkv_adapter_output, out_adapter_input, out_adapter_output,
        up_adapter_input, up_adapter_output, down_adapter_input, down_adapter_output,
        ln_gain, ln_bias,
    ):
        M, R, D = inputs.shape
        QC = output_weight.shape[1]
        FFL = up_weight.shape[2]
        RANK = qkv_adapter_input.shape[2]
        L = R * T
        wq = query_key_value_weight[0].reshape(-1, 3 * QC)
        aq = qkv_adapter_input[0].astype(BF)
        bq = (ADAPTER_SCALE * qkv_adapter_output[0].reshape(RANK, -1)).astype(BF)
        ao = out_adapter_input[0].astype(BF)
        bo = (ADAPTER_SCALE * out_adapter_output[0]).astype(BF)
        au = up_adapter_input[0].astype(BF)
        bu = (ADAPTER_SCALE * up_adapter_output[0]).astype(BF)
        ad = down_adapter_input[0].astype(BF)
        bd = (ADAPTER_SCALE * down_adapter_output[0]).astype(BF)
        flags = split[:, 0]
        cos_t, sin_t = rope_tables(flags, L)
        negb = MASKED * flags.astype(F32)
        kernel = make_kernel(T, DP, M, R, D, QC, FFL, RANK)
        act, ig, ga, gr, gb, _, _ = kernel(
            inputs, cotangent, wq, up_weight[0], output_weight[0], down_weight[0],
            aq, bq, ao, bo, au, bu, ad, bd, ln_gain[0], ln_bias[0], cos_t, sin_t, negb,
        )
        ga = lax.psum(ga.astype(BF), "dp").astype(F32)
        gr = lax.psum(gr.astype(BF), ("dp", "tensor")).astype(F32)
        gb = lax.psum(gb, ("dp", "tensor"))
        cuts = [3 * QC, 3 * QC + FFL, 4 * QC + FFL]
        b_qkv, b_up, a_out, a_down = jnp.split(ga, cuts, axis=1)
        a_qkv, a_up, b_out, b_down = jnp.split(gr, 4, axis=1)

        dp_place = lax.axis_index("dp")
        DR = D // DP
        sl = lax.dynamic_slice_in_dim
        c_qkv = wq.astype(F32) + nn(sl(aq, dp_place * DR, DR, 0), bq)
        c_out = output_weight[0].astype(F32) + nn(ao, sl(bo, dp_place * DR, DR, 1))
        c_up = up_weight[0].astype(F32) + nn(sl(au, dp_place * DR, DR, 0), bu)
        c_down = down_weight[0].astype(F32) + nn(ad, sl(bd, dp_place * DR, DR, 1))
        return (
            act[None], ig[None],
            a_qkv.T[None], b_qkv.reshape(qkv_adapter_output.shape),
            a_out.T[None], b_out[None], a_up.T[None], b_up[None], a_down.T[None], b_down[None],
            gb[0:2][None], gb[2:4][None],
            c_qkv.reshape(query_key_value_weight.shape), c_out[None], c_up[None], c_down[None],
        )

    rows = P(None, ("dp", "tensor"), None)
    whole = P("section", None, None)
    in_specs = (
        rows, rows, P(None, "dp"),
        P("section", "dp", None, "tensor"), P("section", "tensor", "dp"),
        P("section", "dp", "tensor"), P("section", "tensor", "dp"),
        whole, P("section", None, None, "tensor"), P("section", "tensor", None), whole,
        whole, P("section", None, "tensor"), P("section", "tensor", None), whole,
        whole, whole,
    )
    layer_rows = P("section", None, ("dp", "tensor"), None)
    out_specs = (
        layer_rows, layer_rows,
        whole, P("section", None, None, "tensor"), P("section", "tensor", None), whole,
        whole, P("section", None, "tensor"), P("section", "tensor", None), whole,
        whole, whole,
        P("section", "dp", None, "tensor"), P("section", "tensor", "dp"),
        P("section", "dp", "tensor"), P("section", "tensor", "dp"),
    )
    return jax.shard_map(
        per_device, mesh=mesh, in_specs=in_specs, out_specs=out_specs, check_vma=False
    )
```

time: 1710 us -> 674 us (0.39)
  waiting for transfers between devices: 864 us -> 71.1 us
  matrix products: 547 us -> 3.66 us
  Pallas kernels: 0 us -> 465 us
  other arithmetic: 119 us -> 14.9 us
  local copies, waits for them, and re-layouts: 41.8 us -> 19.1 us
    dot_general x136 -> x4, matrix products: 482 us -> 3.66 us  [nn(): lax.dot_general(a, b, (((1,), (0,)), ((), ())), preferred_element_type=F32)]
    pallas_call x0 -> x1, Pallas kernels: none -> 465 us  [per_device(): kernel(inputs, cotangent, wq, up_weight[0], output_weight[0], down_weight...]
    all_gather x18 -> x0, waiting for transfers between devices: 364 us -> none  [the longest x6 171 us: forward(): lax.all_gather(first_normalized.astype(jnp.bfloat16), 'tensor', axis=0, t...]
    reduce_scatter x9 -> x0, waiting for transfers between devices: 237 us -> none  [the longest x3 112 us: backward(): lax.psum_scatter(grad_one.astype(jnp.bfloat16), 'tensor', scatter_dimensi...]
    psum x6 -> x2, waiting for transfers between devices: 254 us -> 71 us  [the longest x1 71 us: per_device(): gr = lax.psum(gr.astype(BF), ('dp', 'tensor')).astype(F32)]
    sub x6 -> x0, matrix products: 65.1 us -> none  [weights_of(): exponent = jnp.exp(masked_scores - row_max)]
    convert_element_type x25 -> x17, other arithmetic: 53.7 us -> 13.3 us  [the longest x2 3.82 us: per_device(): ga = lax.psum(ga.astype(BF), 'dp').astype(F32)]
    all_gather x1 -> x0, blocking collectives: 25.6 us -> none  [collect(): lax.all_gather(output_weight[0], 'dp', axis=1, tiled=True)]
  transfers between devices with their start and end apart: 37 -> 2, of which waited for: 33 -> 1; matrix products, arithmetic and copies ran while one was open for 31% -> 2% of each run, Pallas kernels for 0% -> 0%
where the time goes in v1:
time: 674 us
  Pallas kernels  465 us (69%)
  blocking collectives  85.6 us (13%)
  waiting for transfers between devices  71.1 us (11%)
  local copies, waits for them, and re-layouts  19.1 us (3%)
  other arithmetic  14.9 us (2%)
  between operations  14.3 us (2%)
    pallas_call x1, Pallas kernels, per_device(): kernel(inputs, cotangent, wq, up_weight[0], output_weight[0], down_weight...  465 us
    psum x1, blocking collectives, per_device(): gb = lax.psum(gb, ('dp', 'tensor'))  85.6 us
    psum x1, waiting for transfers between devices, per_device(): gr = lax.psum(gr.astype(BF), ('dp', 'tensor')).astype(F32)  71 us
  transfers between devices with their start and end apart: 2, of which 1 were waited for; matrix products, arithmetic and copies ran while one was open for 2% of the time, Pallas kernels for 0%

profile of v1, /device:TPU:0, one launch (start us, length us, event | category | flops | bytes accessed | tf_op | source)
XLA Modules:
  0.0 673.9 jit_solution(6094189766477684238)
XLA Ops:
  7.4 1.2 convert_multiply_fusion.negb
  9.9 1.3 copy.47.cos_t
  11.3 1.3 copy.48.sin_t
  12.9 0.9 copy.45.wq_in
  14.0 0.8 copy.46.bq
  14.8 0.7 convert_bitcast_fusion.ad
  15.6 1.8 fusion.5.bu
  18.7 0.7 convert_bitcast_fusion.3.aq
  19.5 0.7 fusion.23.bd
  20.2 0.7 fusion.24.bo
  20.9 465.1 %shard_map.291 = (f32[2,256,1024]{2,1,0:T(8,128)}, f32[2,256,1024]{2,1,0:T(8,128)}, f32[128,3072]{1,0:T(8,128)}, f32[128,4096]{1,0:T(8,128)}, f32[8,1024]{1,0:T(...) custom-call(f32[2,256,1024]{2,1,0:T(8,128)} %x_in.1, f32[2,256,1024]{2,1,0:T(8,128)} %ct_in.1, ...), custom_call_target="tpu_custom_call" | custom-call | tf_op jit(solution)/shard_map/pallas_call | solution.py:639
  486.0 2.5 convert_element_type.94
  488.7 1.1 convert_element_type.92
  489.8 1.0 copy-done.6
  491.8 1.1 copy.59
  493.0 0.9 fusion.4
  493.9 85.6 %psum.23 = f32[8,1024]{1,0:T(8,128)S(1)} all-reduce(f32[8,1024]{1,0:T(8,128)S(1)} %copy-done.22), channel_id=1, replica_groups=mesh['section'=2,'dp'=4,'tensor'=4] {'dp','tensor'}, use_global_device_ids=true, to_apply=%region_2.3 | all-reduce | flops 8192 | bytes 65536 | tf_op jit(solution)/shard_map/psum | solution.py:645
  579.5 1.3 fusion.1
  580.8 1.3 fusion.2
  582.6 1.3 convert_element_type.95
  583.9 0.9 slice_bitcast_fusion.1
  584.9 1.0 copy.58
  585.9 0.8 copy.56
  586.8 0.9 copy.55
  587.7 71.0 %all-reduce.3.cloned.1.call-done = bf16[128,4096]{1,0:T(8,128)(2,1)} async-done(((bf16[128,4096]{1,0:T(8,128)(2,1)}), bf16[128,4096]{1,0:T(8,128)(2,1)}) %all-reduce.3.cloned.1.call-update) | async-done | bytes 1048592 | tf_op jit(solution)/shard_map/psum | solution.py:644
  658.8 1.4 convert_element_type.93
  660.2 1.2 slice_bitcast_fusion
  661.4 1.0 copy.54
  662.4 1.0 copy.57
  663.4 1.3 copy.66
  664.7 1.0 copy-done.11
  665.7 1.3 copy.67
  (75 shorter events, 5.3 us)
Async XLA Ops:
  7.2 575.5 %all-reduce.5.cloned.1.call-start = ((), (), s32[]{:S(2)}) async-start(), calls=%async_computation.1 | async-start | bytes 1572864 | tf_op jit(solution)/shard_map/psum | solution.py:643
  11.2 1.4 copy-start.19
  11.3 2.4 copy-start.20
  12.7 2.2 copy-start.18
  12.8 4.5 copy-start.21
  12.8 5.1 copy-start.7
  13.8 4.9 copy-start.4
  13.9 5.5 copy-start.5
  14.8 5.4 copy-start.9
  486.0 2.6 copy-start.3
  488.6 170.2 %all-reduce.3.cloned.1.call-start = ((), (), s32[]{:S(2)}) async-start(), calls=%async_computation | async-start | bytes 2097152 | tf_op jit(solution)/shard_map/psum | solution.py:644
  489.8 1.0 copy-start.6
  489.8 1.2 copy-start.8
  489.8 1.4 copy-start.10
  489.8 1.5 copy-start
  491.2 1.8 copy-start.16
  491.2 1.8 copy-start.17
  491.5 2.4 copy-start.22
  491.5 88.0 %copy-start.2 = (bf16[1024,128]{1,0:T(8,128)(2,1)S(1)}, bf16[1024,128]{1,0:T(8,128)(2,1)}, u32[]{:S(2)}) copy-start(bf16[1024,128]{1,0:T(8,128)(2,1)} %convert_bitcast_fusion.ad) | copy-start | bytes 786436
  491.5 88.0 %copy-start.13 = (bf16[1,1024,256]{2,1,0:T(8,128)(2,1)S(1)}, bf16[1,1024,256]{2,1,0:T(8,128)(2,1)}, u32[]{:S(2)}) copy-start(bf16[1,1024,256]{2,1,0:T(8,128)(2,1)} %param.23) | copy-start | bytes 1572868
  491.8 89.0 %copy-start.1 = (bf16[128,1024]{1,0:T(8,128)(2,1)S(1)}, bf16[128,1024]{1,0:T(8,128)(2,1)}, u32[]{:S(2)}) copy-start(bf16[128,1024]{1,0:T(8,128)(2,1)} %fusion.5.bu) | copy-start | bytes 786436
  491.8 88.9 %copy-start.14 = (bf16[1,256,1024]{2,1,0:T(8,128)(2,1)S(1)}, bf16[1,256,1024]{2,1,0:T(8,128)(2,1)}, u32[]{:S(2)}) copy-start(bf16[1,256,1024]{2,1,0:T(8,128)(2,1)} %param.22) | copy-start | bytes 1572868
  583.9 2.7 copy-start.15
  661.4 2.0 copy-start.12
  663.4 2.3 copy-start.11
Sparse Core Ops, SparseCore 0:
  488.7 53.1 all-reduce.4
  547.7 111.0 all-reduce.2

commit v2 on v1

--- a/solution.py
+++ b/solution.py
@@ -33,15 +33,20 @@
     HEADS = QC // HEAD
     TILE = 256
     HALF = L // 2
+    GA = 4 * QC + 2 * FFL
+    GRW = 4 * D // T
+    PW = -(-GA // (DP * 128)) * 128
+    SW = -(-GRW // (DP * 128)) * 128
 
     def kernel(
         x_in, ct_in, wq_in, wup_in, wout_in, wdn_in,
-        aq, bq, ao, bo, au, bu, ad, bd, gain, bias, cos_t, sin_t, negb,
+        aq, bq, ao, bo, au, bu, ad, bd, gain, bias, rope, negb,
         act, ig, ga_out, gr_out, gb_out, h_hbm, dg_hbm,
         wq, wup, wout, wdn, xh, t12t, qh, kp, vp, kT, vT, oT, lse, hw, dg,
         todt, sbuf, rbuf, sxr, sgr, sxs, dz, doh, delta, edot, dk, dv, dqt, dqkv,
-        ga, gr, gb, xw, yw,
+        ga, gr, gb, xw, yw, pa, pa_in, pa_all, pb, pb_in, pb_all, gb_sum, gb_t, gb_d,
         w_ls, w_ss, w_rs, x_ss, x_rs, r_ss, r_rs, z_ss, z_rs, c_ss, c_rs, l_s,
+        go, at_ss, at_rs, ad_ss, ad_rs,
     ):
         s = lax.axis_index("section")
         d = lax.axis_index("dp")
@@ -60,33 +65,73 @@
         pl.semaphore_signal(barrier, inc=1, device_id={"section": other}, device_id_type=MESH)
         pl.semaphore_wait(barrier, T + DP - 1)
 
-        def weight_refs(index, owner):
+        def gathered(index, owner):
             if index < 2:
-                rows = pl.ds(pl.multiple_of(owner * DR, DR), DR)
-                return (wq_in, wup_in)[index], (wq, wup)[index].at[rows]
-            return (wout_in, wdn_in)[index - 2], (wout, wdn)[index - 2].at[owner]
-
-        def weight_copy(index, k):
-            src, dst = weight_refs(index, d)
+                return (wq, wup)[index].at[pl.ds(pl.multiple_of(owner * DR, DR), DR)]
+            return (wout, wdn)[index - 2].at[owner]
+
+        def weight_copy(index, way, hop, owner, own):
+            place = gathered(index, owner)
             return pltpu.make_async_remote_copy(
-                src_ref=src, dst_ref=dst,
-                send_sem=w_ss.at[index, k - 1], recv_sem=w_rs.at[index, k - 1],
-                device_id={"dp": lax.rem(d + k, DP)}, device_id_type=MESH,
+                src_ref=(wq_in, wup_in, wout_in, wdn_in)[index] if own else place, dst_ref=place,
+                send_sem=w_ss.at[index, way, hop], recv_sem=w_rs.at[index, way, hop],
+                device_id={"dp": d + 1 if way == 0 else d - 1}, device_id_type=MESH,
             )
 
+        has_next = (d < DP - 1, d > 0)
+
+        def holds(way, hop):
+            return d >= hop + 1 if way == 0 else d + hop + 1 <= DP - 1
+
+        def owner_of(way, hop):
+            return d - hop - 1 if way == 0 else d + hop + 1
+
         def weight_local(index):
-            src, dst = weight_refs(index, d)
-            return pltpu.make_async_copy(src, dst, w_ls.at[index])
+            return pltpu.make_async_copy(
+                (wq_in, wup_in, wout_in, wdn_in)[index], gathered(index, d), w_ls.at[index]
+            )
+
+        def weights_start():
+            for index in range(4):
+                for way in range(2):
+                    @pl.when(has_next[way])
+                    def _(index=index, way=way):
+                        weight_copy(index, way, 0, d, True).start()
+
+        def weights_pass(indices):
+            def step(hop, carry):
+                for index in indices:
+                    for way in range(2):
+                        @pl.when(holds(way, hop))
+                        def _(index=index, way=way):
+                            weight_copy(index, way, hop, owner_of(way, hop), False).wait_recv()
+
+                            @pl.when(has_next[way])
+                            def _():
+                                weight_copy(index, way, hop + 1, owner_of(way, hop), False).start()
+                return carry
+
+            lax.fori_loop(0, DP - 1, step, 0)
+
+        def weights_sent():
+            for index in range(4):
+                for way in range(2):
+                    @pl.when(has_next[way])
+                    def _(index=index, way=way):
+                        weight_copy(index, way, 0, d, True).wait_send()
+
+            def step(hop, carry):
+                for index in range(4):
+                    for way in range(2):
+                        @pl.when(jnp.logical_and(has_next[way], holds(way, hop)))
+                        def _(index=index, way=way):
+                            weight_copy(index, way, hop + 1, owner_of(way, hop), False).wait_send()
+                return carry
+
+            lax.fori_loop(0, DP - 1, step, 0)
 
         for index in range(4):
             weight_local(index).start()
-            for k in range(1, DP):
-                weight_copy(index, k).start()
-
-        def weights_ready(index):
-            weight_local(index).wait()
-            for k in range(1, DP):
-                weight_copy(index, k).wait_recv()
 
         ga[...] = jnp.zeros_like(ga)
         gr[...] = jnp.zeros_like(gr)
@@ -96,7 +141,7 @@
             place = m * T + t
             return pltpu.make_async_remote_copy(
                 src_ref=buf.at[place], dst_ref=buf.at[place],
-                send_sem=ssem.at[k - 1], recv_sem=rsem.at[m * (T - 1) + k - 1],
+                send_sem=ssem.at[m * (T - 1) + k - 1], recv_sem=rsem.at[m * (T - 1) + k - 1],
                 device_id={"tensor": lax.rem(t + k, T)}, device_id_type=MESH,
             )
 
@@ -107,6 +152,12 @@
                 send_sem=ssem.at[0], recv_sem=rsem.at[m * (T - 1) + c - 1],
                 device_id={"tensor": lax.rem(t + 1, T)}, device_id_type=MESH,
             ).wait_recv()
+
+        def to_peer(axis, size, me, k, src, dst, ssem, rsem):
+            return pltpu.make_async_remote_copy(
+                src_ref=src, dst_ref=dst, send_sem=ssem, recv_sem=rsem,
+                device_id={axis: lax.rem(me + k, size)}, device_id_type=MESH,
+            )
 
         def block_copy(phase, i):
             k = lax.rem(i - t + T, T)
@@ -143,12 +194,20 @@
             rstd = lax.rsqrt(spread + EPSILON)
             return centred * rstd, rstd
 
-        def load_x(m):
-            @pl.when(s == 0)
-            def _():
-                copy = local_copy(x_in.at[m], xw, 0)
-                copy.start()
-                copy.wait()
+        def send_normed(m):
+            xhat, _ = norm_parts(xw[m])
+            xh[m * T + t] = xhat.astype(BF)
+            for k in range(1, T):
+                rows_copy(xh, m, k, x_ss, x_rs).start()
+
+        def send_gradient(m):
+            for k in range(1, T):
+                rows_copy(dz, m, k, z_ss, z_rs).start()
+
+        def take_x(m):
+            section_copy(m, 0).wait_recv()
+            xw[m] = sxr[m].astype(F32)
+            send_normed(m)
 
         lane = lax.broadcasted_iota(jnp.int32, (R, 128), 1)
         in_first = lax.rem(lane, HEAD) < ROT // 2
@@ -157,6 +216,11 @@
         def turn(v, cosine, sine):
             swapped = jnp.where(in_first, pltpu.roll(v, 128 - ROT // 2, 1), pltpu.roll(v, ROT // 2, 1))
             return v * cosine + swapped * sine
+
+        def rope_of(m, rows):
+            table = rope[m, rows, :]
+            crossed = pltpu.roll(table, HEAD, 1)
+            return jnp.where(head_low, table, crossed), jnp.where(head_low, crossed, table)
 
         causal = lax.broadcasted_iota(jnp.int32, (R, R), 0) <= lax.broadcasted_iota(
             jnp.int32, (R, R), 1
@@ -171,23 +235,43 @@
                 sc = sc + negb[m]
             return sc
 
-        def forward(m, carry):
-            load_x(m)
-
-            @pl.when(s == 1)
-            def _():
-                section_copy(m, 0).wait_recv()
-                xw[...] = sxr[m].astype(F32)
-
-            xhat, _ = norm_parts(xw[...])
-            xh[m * T + t] = xhat.astype(BF)
-            for k in range(1, T):
-                rows_copy(xh, m, k, x_ss, x_rs).start()
-
-            @pl.when(m == 0)
-            def _():
-                weights_ready(0)
-                weights_ready(1)
+        @pl.when(s == 0)
+        def _():
+            weights_start()
+            loads = [local_copy(x_in.at[m], xw.at[m], m) for m in range(M)]
+            for copy in loads:
+                copy.start()
+            for m in range(M):
+                loads[m].wait()
+                send_normed(m)
+            weights_pass((0, 1, 2, 3))
+            weights_sent()
+            pl.semaphore_signal(go, inc=1, device_id={"section": other}, device_id_type=MESH)
+
+        @pl.when(s == 1)
+        def _():
+            loads = [local_copy(ct_in.at[m], xw.at[m], m) for m in range(M)]
+            for copy in loads:
+                copy.start()
+            for m in range(M):
+                loads[m].wait()
+                dz[m * T + t] = xw[m].astype(BF)
+                send_gradient(m)
+            pl.semaphore_wait(go, 1)
+            weights_start()
+            weights_pass((0, 1))
+            take_x(0)
+            weights_pass((2, 3))
+            weights_sent()
+
+        for index in range(4):
+            weight_local(index).wait()
+
+        def normed_to_hidden(m):
+            @pl.when(m > 0)
+            def _():
+                local_copy(hw, h_hbm.at[m - 1], 1).wait()
+                local_copy(dg, dg_hbm.at[m - 1], 2).wait()
 
             def chunk(c, carry):
                 src = lax.rem(t - c + T, T)
@@ -204,8 +288,7 @@
                 t2 = nn(n2, au[...]).astype(BF)
                 t12t[m, 0:RANK, rows] = t1.T
                 t12t[m, RANK:2 * RANK, rows] = t2.T
-                cosine = cos_t[m, rows, :]
-                sine = sin_t[m, rows, :]
+                cosine, sine = rope_of(m, rows)
                 for part in range(3):
                     cols = slice(part * QC, (part + 1) * QC)
                     val = nn(n1, wq[:, cols]) + nn(t1, bq[:, cols])
@@ -236,16 +319,10 @@
                 return carry
 
             lax.fori_loop(0, T, chunk, 0)
-            for k in range(1, T):
-                rows_copy(xh, m, k, x_ss, x_rs).wait_send()
             local_copy(hw, h_hbm.at[m], 1).start()
             local_copy(dg, dg_hbm.at[m], 2).start()
 
-            @pl.when(m == 0)
-            def _():
-                weights_ready(2)
-                weights_ready(3)
-
+        def attend_and_project(m):
             for i in range(T):
                 icols = slice(i * R, (i + 1) * R)
 
@@ -280,6 +357,11 @@
                 def _(i=i):
                     block_copy(m, i).start()
 
+        def finish_forward(m):
+            @pl.when(m > 0)
+            def _():
+                local_copy(yw, act.at[m - 1], 3).wait()
+
             for k in range(1, T):
                 block_wait(m, k)
 
@@ -295,53 +377,59 @@
             todt[m, RANK:2 * RANK, :] = td.T
             for n0 in range(0, D, TILE):
                 cols = slice(n0, n0 + TILE)
-                y = xw[:, cols] + summed(n0, n0 + TILE) + nn(to, bo[:, cols]) + nn(td, bd[:, cols])
-                xw[:, cols] = y
+                y = xw[m, :, cols] + summed(n0, n0 + TILE) + nn(to, bo[:, cols]) + nn(td, bd[:, cols])
+                yw[:, cols] = y
                 sxs[:, cols] = y.astype(BF)
 
             @pl.when(s == 0)
             def _():
                 section_copy(m, 0).start()
 
-            out = local_copy(xw, act.at[m], 3)
-            out.start()
-            out.wait()
+            local_copy(yw, act.at[m], 3).start()
+            for k in range(1, T):
+                rows_copy(xh, m, k, x_ss, x_rs).wait_send()
             for i in range(T):
                 @pl.when(t != i)
                 def _(i=i):
                     block_copy(m, i).wait_send()
-            local_copy(hw, h_hbm.at[m], 1).wait()
-            local_copy(dg, dg_hbm.at[m], 2).wait()
 
             @pl.when(s == 0)
             def _():
                 section_copy(m, 0).wait_send()
+
+        def forward(step, carry):
+            @pl.when(step < M)
+            def _():
+                normed_to_hidden(step)
+
+            @pl.when(step > 0)
+            def _():
+                finish_forward(step - 1)
+
+            @pl.when(jnp.logical_and(s == 1, step < M - 1))
+            def _():
+                take_x(step + 1)
+
+            @pl.when(step < M)
+            def _():
+                attend_and_project(step)
             return carry
 
-        lax.fori_loop(0, M, forward, 0)
-
-        def backward(m, carry):
+        lax.fori_loop(0, M + 1, forward, 0)
+        local_copy(hw, h_hbm.at[M - 1], 1).wait()
+        local_copy(dg, dg_hbm.at[M - 1], 2).wait()
+        local_copy(yw, act.at[M - 1], 3).wait()
+
+        def gradient_to_hidden(m):
             local_copy(dg_hbm.at[m], dg, 2).start()
             local_copy(h_hbm.at[m], hw, 1).start()
 
-            @pl.when(s == 1)
-            def _():
-                copy = local_copy(ct_in.at[m], yw, 3)
-                copy.start()
-                copy.wait()
-                xw[...] = sxr[m].astype(F32)
-
             @pl.when(s == 0)
             def _():
                 section_copy(m, 1).wait_recv()
-                yw[...] = sgr[m].astype(F32)
-
-            load_x(m)
-            dz[m * T + t] = yw[...].astype(BF)
-            for k in range(1, T):
-                rows_copy(dz, m, k, z_ss, z_rs).start()
-            dk[...] = jnp.zeros_like(dk)
-            dv[...] = jnp.zeros_like(dv)
+                dz[m * T + t] = sgr[m]
+                send_gradient(m)
+
             local_copy(dg_hbm.at[m], dg, 2).wait()
 
             def chunk(c, carry):
@@ -381,9 +469,10 @@
                 return carry
 
             lax.fori_loop(0, T, chunk, 0)
-            for k in range(1, T):
-                rows_copy(dz, m, k, z_ss, z_rs).wait_send()
-
+
+        def attention_back(m):
+            dk[...] = jnp.zeros_like(dk)
+            dv[...] = jnp.zeros_like(dv)
             for i in range(T):
                 icols = slice(i * R, (i + 1) * R)
 
@@ -412,8 +501,8 @@
             def tail(c, carry):
                 i = lax.rem(t + c + 1, T)
                 rows = pl.ds(pl.multiple_of(i * R, R), R)
-                cosine = cos_t[m, rows, :]
-                sine = -sin_t[m, rows, :]
+                cosine, sine = rope_of(m, rows)
+                sine = -sine
                 dq = dqt[:, rows].T * 0.125
                 for p in range(PAIRS):
                     lanes = slice(p * 128, (p + 1) * 128)
@@ -444,6 +533,14 @@
 
             lax.fori_loop(0, T, tail, 0)
 
+            @pl.when(m > 0)
+            def _():
+                local_copy(yw, ig.at[m - 1], 3).wait()
+
+            @pl.when(s == 1)
+            def _():
+                local_copy(ct_in.at[m], yw, 0).start()
+
             local_copy(h_hbm.at[m], hw, 1).wait()
             base = 0
             ga[:, base:base + 3 * QC] += ADAPTER_SCALE * nn(t12t[m, 0:RANK, :], dqkv[...])
@@ -457,6 +554,15 @@
             gr[:, 2 * D:3 * D] += ADAPTER_SCALE * nn(todt[m, 0:RANK, :], own)
             gr[:, 3 * D:4 * D] += ADAPTER_SCALE * nn(todt[m, RANK:2 * RANK, :], own)
 
+        def finish_backward(m):
+            @pl.when(s == 1)
+            def _():
+                local_copy(ct_in.at[m], yw, 0).wait()
+
+            @pl.when(s == 0)
+            def _():
+                yw[...] = sgr[m].astype(F32)
+
             for k in range(1, T):
                 block_wait(M + m, k)
 
@@ -468,8 +574,8 @@
 
             e1 = summed(D, D + RANK).astype(BF)
             e2 = summed(D + RANK, W).astype(BF)
-            xhat, rstd = norm_parts(xw[...])
-            xw[...] = xhat
+            xhat, rstd = norm_parts(xw[m])
+            xw[m] = xhat
             n1 = (xhat * gain[0:1] + bias[0:1]).astype(BF)
             n2 = (xhat * gain[1:2] + bias[1:2]).astype(BF)
             gr[:, 0:D] += nn(e1.T, n1)
@@ -481,7 +587,7 @@
                 cols = slice(n0, n0 + TILE)
                 dn1 = nt(e1, aq[cols, :])
                 dn2 = nt(e2, au[cols, :])
-                xhc = xw[:, cols]
+                xhc = xw[m, :, cols]
                 gb[0:1, cols] += jnp.sum(dn1 * xhc, axis=0, keepdims=True)
                 gb[1:2, cols] += jnp.sum(dn2 * xhc, axis=0, keepdims=True)
                 gb[2:3, cols] += jnp.sum(dn1, axis=0, keepdims=True)
@@ -494,7 +600,7 @@
             mean_gx = mean_gx * (1.0 / D)
             for n, n0 in enumerate(range(0, D, TILE)):
                 cols = slice(n0, n0 + TILE)
-                v = yw[:, cols] + (pieces[n] - mean_g - xw[:, cols] * mean_gx) * rstd
+                v = yw[:, cols] + (pieces[n] - mean_g - xw[m, :, cols] * mean_gx) * rstd
                 yw[:, cols] = v
                 sxs[:, cols] = v.astype(BF)
 
@@ -502,9 +608,9 @@
             def _():
                 section_copy(m, 1).start()
 
-            out = local_copy(yw, ig.at[m], 3)
-            out.start()
-            out.wait()
+            local_copy(yw, ig.at[m], 3).start()
+            for k in range(1, T):
+                rows_copy(dz, m, k, z_ss, z_rs).wait_send()
             for i in range(T):
                 @pl.when(t != i)
                 def _(i=i):
@@ -513,23 +619,154 @@
             @pl.when(s == 1)
             def _():
                 section_copy(m, 1).wait_send()
+
+        def backward(step, carry):
+            @pl.when(step < M)
+            def _():
+                gradient_to_hidden(step)
+
+            @pl.when(step > 0)
+            def _():
+                finish_backward(step - 1)
+
+            @pl.when(step < M)
+            def _():
+                attention_back(step)
             return carry
 
-        lax.fori_loop(0, M, backward, 0)
-
-        outs = [local_copy(ga, ga_out, 1), local_copy(gr, gr_out, 2), local_copy(gb, gb_out, 3)]
-        for copy in outs:
-            copy.start()
+        lax.fori_loop(0, M + 1, backward, 0)
+        local_copy(yw, ig.at[M - 1], 3).wait()
+
+        def scatter_dp(buf, landing, base):
+            for k in range(1, DP):
+                yield to_peer("dp", DP, d, k, buf.at[lax.rem(d + k, DP)], landing.at[k - 1],
+                              ad_ss.at[base, k - 1], ad_rs.at[base, k - 1])
+
+        def gather_dp(buf, base):
+            for k in range(1, DP):
+                yield to_peer("dp", DP, d, k, buf.at[d], buf.at[d],
+                              ad_ss.at[base, k - 1], ad_rs.at[base, k - 1])
+
+        def gather_dp_wait(buf, base):
+            for k in range(1, DP):
+                place = buf.at[lax.rem(d - k + DP, DP)]
+                to_peer("dp", DP, d, k, place, place,
+                        ad_ss.at[base, k - 1], ad_rs.at[base, k - 1]).wait_recv()
+
+        def fill(buf, value, width):
+            total = value.shape[1]
+            for j in range(DP):
+                lo, hi = min(j * width, total), min((j + 1) * width, total)
+                if hi > lo:
+                    buf[j, :, 0:hi - lo] = value[:, lo:hi].astype(BF)
+                if hi - lo < width:
+                    buf[j, :, hi - lo:width] = jnp.zeros((RANK, width - hi + lo), BF)
+
+        def added(buf, landing):
+            v = buf[d].astype(F32)
+            for k in range(DP - 1):
+                v = v + landing[k].astype(F32)
+            return v.astype(BF)
+
+        def tensor_scatter():
+            for k in range(1, T):
+                yield to_peer("tensor", T, t, k, sbuf.at[lax.rem(t + k, T), 0:RANK, 0:GRW],
+                              rbuf.at[k - 1, 0:RANK, 0:GRW], at_ss.at[0, k - 1], at_rs.at[0, k - 1])
+
+        def tensor_gather():
+            for k in range(1, T):
+                yield to_peer("tensor", T, t, k, sbuf.at[t, 0:RANK, 0:GRW],
+                              rbuf.at[T - 1 + k - 1, 0:RANK, 0:GRW],
+                              at_ss.at[1, k - 1], at_rs.at[1, k - 1])
+
+        def gb_over_tensor():
+            for k in range(1, T):
+                yield to_peer("tensor", T, t, k, gb, gb_t.at[k - 1], at_ss.at[2, k - 1], at_rs.at[2, k - 1])
+
+        def gb_over_dp():
+            for k in range(1, DP):
+                yield to_peer("dp", DP, d, k, gb_sum, gb_d.at[k - 1], ad_ss.at[4, k - 1], ad_rs.at[4, k - 1])
+
+        def start_all(copies):
+            for copy in copies:
+                copy.start()
+
+        def arrive_all(copies):
+            for copy in copies:
+                copy.wait_recv()
+
+        def sent_all(copies):
+            for copy in copies:
+                copy.wait_send()
+
+        for j in range(T):
+            sbuf[j, 0:RANK, 0:GRW] = gr[:, j * GRW:(j + 1) * GRW].astype(BF)
+        start_all(tensor_scatter())
+        start_all(gb_over_tensor())
+        fill(pa, ga, PW)
+        start_all(scatter_dp(pa, pa_in, 0))
+
+        arrive_all(tensor_scatter())
+        part = sbuf[t, 0:RANK, 0:GRW].astype(F32)
+        for k in range(T - 1):
+            part = part + rbuf[k, 0:RANK, 0:GRW].astype(F32)
+        fill(pb, part, SW)
+        start_all(scatter_dp(pb, pb_in, 1))
+        arrive_all(gb_over_tensor())
+        total = gb[...]
+        for k in range(T - 1):
+            total = total + gb_t[k]
+        gb_sum[...] = total
+        start_all(gb_over_dp())
+
+        arrive_all(scatter_dp(pb, pb_in, 1))
+        pb_all[d] = added(pb, pb_in)
+        start_all(gather_dp(pb_all, 3))
+        arrive_all(scatter_dp(pa, pa_in, 0))
+        pa_all[d] = added(pa, pa_in)
+        start_all(gather_dp(pa_all, 2))
+
+        gather_dp_wait(pb_all, 3)
+        for j in range(DP):
+            lo, hi = min(j * SW, GRW), min((j + 1) * SW, GRW)
+            if hi > lo:
+                sbuf[t, 0:RANK, lo:hi] = pb_all[j, :, 0:hi - lo]
+        start_all(tensor_gather())
+
+        arrive_all(gb_over_dp())
+        sent_all(gb_over_tensor())
+        total = gb_sum[...]
+        for k in range(DP - 1):
+            total = total + gb_d[k]
+        gb[...] = total
+        outs = [local_copy(gb, gb_out, 3)]
+        outs[0].start()
+
+        gather_dp_wait(pa_all, 2)
+        for j in range(DP):
+            lo, hi = min(j * PW, GA), min((j + 1) * PW, GA)
+            if hi > lo:
+                ga[:, lo:hi] = pa_all[j, :, 0:hi - lo].astype(F32)
+        outs.append(local_copy(ga, ga_out, 1))
+        outs[1].start()
+
+        arrive_all(tensor_gather())
+        gr[:, pl.ds(pl.multiple_of(t * GRW, 128), GRW)] = sbuf[t, 0:RANK, 0:GRW].astype(F32)
+        for k in range(1, T):
+            place = pl.ds(pl.multiple_of(lax.rem(t - k + T, T) * GRW, 128), GRW)
+            gr[:, place] = rbuf[T - 1 + k - 1, 0:RANK, 0:GRW].astype(F32)
+        outs.append(local_copy(gr, gr_out, 2))
+        outs[2].start()
+        for copies in (tensor_scatter(), tensor_gather(), scatter_dp(pa, pa_in, 0),
+                       scatter_dp(pb, pb_in, 1), gather_dp(pa_all, 2), gather_dp(pb_all, 3),
+                       gb_over_dp()):
+            sent_all(copies)
         for copy in outs:
             copy.wait()
-        for index in range(4):
-            for k in range(1, DP):
-                weight_copy(index, k).wait_send()
 
     any_spec = pl.BlockSpec(memory_space=pl.ANY)
     vmem_spec = pl.BlockSpec(memory_space=pltpu.VMEM)
     smem_spec = pl.BlockSpec(memory_space=pltpu.SMEM)
-    GA = 3 * QC + QC + 2 * FFL
     shapes = jax.ShapeDtypeStruct
     return pl.pallas_call(
         kernel,
@@ -538,7 +775,7 @@
             shapes((RANK, GA), F32), shapes((RANK, 4 * D), F32), shapes((8, D), F32),
             shapes((M, L, FFL), BF), shapes((M, L, FFL), BF),
         ),
-        in_specs=[any_spec] * 6 + [vmem_spec] * 12 + [smem_spec],
+        in_specs=[any_spec] * 6 + [vmem_spec] * 11 + [smem_spec],
         out_specs=(any_spec,) * 7,
         scratch_shapes=[
             pltpu.VMEM((D, 3 * QC), BF), pltpu.VMEM((D, FFL), BF),
@@ -571,20 +808,34 @@
             pltpu.VMEM((RANK, GA), F32),
             pltpu.VMEM((RANK, 4 * D), F32),
             pltpu.VMEM((8, D), F32),
+            pltpu.VMEM((M, R, D), F32),
             pltpu.VMEM((R, D), F32),
-            pltpu.VMEM((R, D), F32),
+            pltpu.VMEM((DP, RANK, PW), BF),
+            pltpu.VMEM((DP - 1, RANK, PW), BF),
+            pltpu.VMEM((DP, RANK, PW), BF),
+            pltpu.VMEM((DP, RANK, SW), BF),
+            pltpu.VMEM((DP - 1, RANK, SW), BF),
+            pltpu.VMEM((DP, RANK, SW), BF),
+            pltpu.VMEM((8, D), F32),
+            pltpu.VMEM((T - 1, 8, D), F32),
+            pltpu.VMEM((DP - 1, 8, D), F32),
             pltpu.SemaphoreType.DMA((4,)),
-            pltpu.SemaphoreType.DMA((4, DP - 1)),
-            pltpu.SemaphoreType.DMA((4, DP - 1)),
-            pltpu.SemaphoreType.DMA((T - 1,)),
+            pltpu.SemaphoreType.DMA((4, 2, DP)),
+            pltpu.SemaphoreType.DMA((4, 2, DP)),
+            pltpu.SemaphoreType.DMA((M * (T - 1),)),
             pltpu.SemaphoreType.DMA((M * (T - 1),)),
             pltpu.SemaphoreType.DMA((T,)),
             pltpu.SemaphoreType.DMA((2 * M * (T - 1),)),
-            pltpu.SemaphoreType.DMA((T - 1,)),
+            pltpu.SemaphoreType.DMA((M * (T - 1),)),
             pltpu.SemaphoreType.DMA((M * (T - 1),)),
             pltpu.SemaphoreType.DMA((1,)),
             pltpu.SemaphoreType.DMA((2 * M,)),
             pltpu.SemaphoreType.DMA((4,)),
+            pltpu.SemaphoreType.REGULAR,
+            pltpu.SemaphoreType.DMA((3, T - 1)),
+            pltpu.SemaphoreType.DMA((3, T - 1)),
+            pltpu.SemaphoreType.DMA((5, DP - 1)),
+            pltpu.SemaphoreType.DMA((5, DP - 1)),
         ],
         compiler_params=pltpu.CompilerParams(
             collective_id=0, has_side_effects=True, vmem_limit_bytes=63 * 2**20
@@ -592,7 +843,7 @@
     )
 
 
-def rope_tables(split_flags, length):
+def rope_table(split_flags, length):
     half = ROT // 2
     place = jnp.arange(length, dtype=jnp.int32)
     flags = split_flags.astype(jnp.int32)[:, None]
@@ -604,7 +855,7 @@
     rest = angles.shape[:2] + (pad,)
     cos_head = jnp.concatenate([cosine, cosine, jnp.ones(rest, F32)], axis=-1)
     sin_head = jnp.concatenate([-sine, sine, jnp.zeros(rest, F32)], axis=-1)
-    return jnp.tile(cos_head, (1, 1, 2)), jnp.tile(sin_head, (1, 1, 2))
+    return jnp.concatenate([cos_head, sin_head], axis=-1)
 
 
 def solution(mesh):
@@ -633,16 +884,13 @@
         ad = down_adapter_input[0].astype(BF)
         bd = (ADAPTER_SCALE * down_adapter_output[0]).astype(BF)
         flags = split[:, 0]
-        cos_t, sin_t = rope_tables(flags, L)
+        rope = rope_table(flags, L)
         negb = MASKED * flags.astype(F32)
         kernel = make_kernel(T, DP, M, R, D, QC, FFL, RANK)
         act, ig, ga, gr, gb, _, _ = kernel(
             inputs, cotangent, wq, up_weight[0], output_weight[0], down_weight[0],
-            aq, bq, ao, bo, au, bu, ad, bd, ln_gain[0], ln_bias[0], cos_t, sin_t, negb,
+            aq, bq, ao, bo, au, bu, ad, bd, ln_gain[0], ln_bias[0], rope, negb,
         )
-        ga = lax.psum(ga.astype(BF), "dp").astype(F32)
-        gr = lax.psum(gr.astype(BF), ("dp", "tensor")).astype(F32)
-        gb = lax.psum(gb, ("dp", "tensor"))
         cuts = [3 * QC, 3 * QC + FFL, 4 * QC + FFL]
         b_qkv, b_up, a_out, a_down = jnp.split(ga, cuts, axis=1)
         a_qkv, a_up, b_out, b_down = jnp.split(gr, 4, axis=1)

time: 674 us -> 406 us (0.60)
  Pallas kernels: 465 us -> 364 us
  blocking collectives: 85.6 us -> 0 us
  waiting for transfers between devices: 71.1 us -> 0 us
  between operations: 14.3 us -> 0.89 us
    pallas_call x1, Pallas kernels: 465 us -> 364 us  [per_device(): kernel(inputs, cotangent, wq, up_weight[0], output_weight[0], down_weight...]
    psum x1 -> x0, blocking collectives: 85.6 us -> none  [per_device(): gb = lax.psum(gb, ('dp', 'tensor'))]
    psum x2 -> x0, waiting for transfers between devices: 71 us -> none  [the longest x1 71 us: per_device(): gr = lax.psum(gr.astype(BF), ('dp', 'tensor')).astype(F32)]
  transfers between devices with their start and end apart: 2 -> 0, of which waited for: 1 -> 0; matrix products, arithmetic and copies ran while one was open for 2% -> 0% of each run, Pallas kernels for 0% -> 0%
where the time goes in v2:
time: 406 us; the launch traced here: 405 us
  Pallas kernels  364 us (90%)
  local copies, waits for them, and re-layouts  25.3 us (6%)
  other arithmetic  11.2 us (3%)
    pallas_call x1, Pallas kernels, per_device(): kernel(inputs, cotangent, wq, up_weight[0], output_weight[0], down_weight...  364 us
    unnamed x52, local copies, waits for them, and re-layouts  10.9 us

profile of v2, /device:TPU:0, one launch (start us, length us, event | category | flops | bytes accessed | tf_op | source)
XLA Modules:
  0.0 405.2 jit_solution(11263894095020769141)
XLA Ops:
  0.7 0.7 subtract_convert_fusion
  1.4 3.7 multiply_sine_fusion
  5.1 1.0 broadcast_in_dim.75
  6.2 1.0 broadcast_in_dim.76
  7.2 4.4 %concatenate.3.rope = f32[2,1024,128]{2,1,0:T(8,128)} concatenate(f32[2,1024,8]{2,1,0:T(8,128)S(1)} %get-tuple-element.84, f32[2,1024,8]{2,1,0:T(8,128)S(1)} %get-tuple-element.84, f32[2,1024,48]{2,1,0:T(8,128)} %broadcast_in_dim.75, f32[2,1024,8]{2,1,0:T(8,128)S(1)} %get-tuple-element.83, f32[2,1024,8]{2,1,0:T(8,128)S(1)} %get-tuple-element.82, f32[2,1024,48]{2,1,0:T(8,128)} %broadcast_in_dim.76), dimensions={2} | concatenate | bytes 2097152 | tf_op jit(solution)/shard_map/concatenate | solution.py:858
  11.8 0.9 copy.61.wq_in
  12.8 1.2 copy.59
  14.0 0.8 copy.62.bq
  14.9 0.7 convert_bitcast_fusion.ad
  15.6 1.8 fusion.6.bu
  17.4 0.6 convert_bitcast_fusion.1.ao
  18.0 0.7 convert_bitcast_fusion.2.au
  18.8 0.7 convert_bitcast_fusion.3.aq
  19.5 0.7 fusion.23.bd
  20.2 0.7 fusion.24.bo
  21.5 364.1 %shard_map.291 = (f32[2,256,1024]{2,1,0:T(8,128)}, f32[2,256,1024]{2,1,0:T(8,128)}, f32[128,3072]{1,0:T(8,128)}, f32[128,4096]{1,0:T(8,128)}, f32[8,1024]{1,0:T(...) custom-call(f32[2,256,1024]{2,1,0:T(8,128)} %x_in.1, f32[2,256,1024]{2,1,0:T(8,128)} %ct_in.1, ...), custom_call_target="tpu_custom_call" | custom-call | tf_op jit(solution)/shard_map/pallas_call | solution.py:890
  385.6 3.1 slice_bitcast_fusion
  388.7 1.0 copy.68
  389.7 1.0 copy.71
  390.7 1.0 copy.72
  391.7 1.1 split.25
  392.9 0.9 copy.69
  393.8 0.9 slice_bitcast_fusion.6
  394.7 0.8 copy.70
  395.5 0.6 slice_bitcast_fusion.7
  396.7 1.1 copy.73
  398.0 1.3 fusion.1
  399.3 1.3 fusion.2
  400.6 0.9 fusion.4
  401.5 1.3 copy.78
  402.8 1.0 copy-done.10
  403.9 1.3 copy.79
  (53 shorter events, 1.6 us)
Async XLA Ops:
  7.2 4.4 %copy-start.17 = (bf16[1,256,3,256]{3,1,2,0:T(8,128)(2,1)S(1)}, bf16[1,256,3,256]{3,1,2,0:T(8,128)(2,1)}, u32[]{:S(2)}) copy-start(bf16[1,256,3,256]{3,1,2,0:T(8,128)(2,1)} %param.20) | copy-start | bytes 1179652
  11.6 3.2 copy-start.16
  11.8 5.6 %copy-start.18 = (f32[1,256,128]{2,1,0:T(8,128)S(1)}, f32[1,256,128]{2,1,0:T(8,128)}, u32[]{:S(2)}) copy-start(f32[1,256,128]{2,1,0:T(8,128)} %param.26) | copy-start | bytes 393220
  11.8 6.2 %copy-start.6 = (f32[1,1024,128]{2,1,0:T(8,128)S(1)}, f32[1,1024,128]{2,1,0:T(8,128)}, u32[]{:S(2)}) copy-start(f32[1,1024,128]{2,1,0:T(8,128)} %param.28) | copy-start | bytes 1572868
  12.8 6.0 %copy-start.3 = (f32[1,1024,128]{2,1,0:T(8,128)S(1)}, f32[1,1024,128]{2,1,0:T(8,128)}, u32[]{:S(2)}) copy-start(f32[1,1024,128]{2,1,0:T(8,128)} %param.24) | copy-start | bytes 1572868
  14.0 5.5 %copy-start.4 = (f32[1,128,1024]{2,1,0:T(8,128)S(1)}, f32[1,128,1024]{2,1,0:T(8,128)}, u32[]{:S(2)}) copy-start(f32[1,128,1024]{2,1,0:T(8,128)} %param.31) | copy-start | bytes 1572868
  14.9 5.4 %copy-start.8 = (f32[1,128,1024]{2,1,0:T(8,128)S(1)}, f32[1,128,1024]{2,1,0:T(8,128)}, u32[]{:S(2)}) copy-start(f32[1,128,1024]{2,1,0:T(8,128)} %param.27) | copy-start | bytes 1572868
  15.6 5.4 %copy-start.20 = (s32[2,1]{0,1:T(1,128)S(1)}, s32[2,1]{0,1:T(1,128)}, u32[]{:S(2)}) copy-start(s32[2,1]{0,1:T(1,128)} %param.19) | copy-start | bytes 28
  390.7 4.8 %copy-start.19 = (f32[8,1024]{1,0:T(8,128)S(1)}, f32[8,1024]{1,0:T(8,128)}, u32[]{:S(2)}) copy-start(f32[8,1024]{1,0:T(8,128)} %get-tuple-element.25) | copy-start | bytes 98308
  391.7 4.5 %copy-start = (bf16[256,768]{1,0:T(8,128)(2,1)S(1)}, bf16[256,768]{1,0:T(8,128)(2,1)}, u32[]{:S(2)}) copy-start(bf16[256,768]{1,0:T(8,128)(2,1)} %copy.61.wq_in) | copy-start | bytes 1179652
  396.1 1.7 copy-start.5
  396.4 1.5 copy-start.2
  396.4 1.5 copy-start.12
  396.7 2.5 copy-start.7
  397.9 1.4 copy-start.1
  397.9 1.4 copy-start.13
  397.9 2.6 copy-start.9
  399.2 1.4 copy-start.14
  399.2 1.4 copy-start.15
  399.2 2.3 copy-start.11
  401.5 2.3 copy-start.10

commit v3 on v2

v3 whole, which is shorter than its diff:
```python
import functools

import jax
import jax.numpy as jnp
import numpy as np
from jax import lax
from jax.experimental import pallas as pl
from jax.experimental.pallas import tpu as pltpu
from jax.sharding import PartitionSpec as P

HEAD = 64
ROT = 16
ADAPTER_SCALE = 0.25
EPSILON = 1e-05
MASKED = -1e30
BF = jnp.bfloat16
F32 = jnp.float32
MESH = pl.DeviceIdType.MESH


def nn(a, b):
    return lax.dot_general(a, b, (((1,), (0,)), ((), ())), preferred_element_type=F32)


def nt(a, b):
    return lax.dot_general(a, b, (((1,), (1,)), ((), ())), preferred_element_type=F32)


def make_kernel(T, DP, M, R, D, QC, FFL, RANK):
    L = R * T
    DR = D // DP
    B = R // 2
    PAIRS = QC // 128
    HEADS = QC // HEAD
    TILE = 256
    HALF = L // 2
    GA = 4 * QC + 2 * FFL
    GRW = 2 * D // T
    PW = -(-GA // (DP * 128)) * 128
    SW = -(-GRW // (DP * 128)) * 128

    def kernel(
        x_in, ct_in, wq_in, wup_in, wout_in, wdn_in,
        aq_in, bq_in, ao_in, bo_in, au_in, bu_in, ad_in, bd_in, gain, bias, rope, split,
        act, ig, ga_out, gr_out, gb_out, dg_hbm,
        aq, bq, ao, bo, au, bu, ad, bd,
        wq, wup, wout, wdn, xh, t12t, qp, kp, vp, kT, vT, oT, lse, hw, dg,
        todt, sbuf, rbuf, srec, sxs, dz, dop, delta, edot, dk, dv, dqt, dqkv,
        ga, gr, gb, xw, yw, pa, pa_in, pa_all, pt, pt_in, pt_all, pb, pb_in, pb_all,
        gb_sum, gb_t, gb_d,
        w_ls, w_ss, w_rs, x_ss, x_rs, r_ss, r_rs, z_ss, z_rs, c_ss, c_rs, l_s, f_s,
        go, at_ss, at_rs, ad_ss, ad_rs,
    ):
        s = lax.axis_index("section")
        d = lax.axis_index("dp")
        t = lax.axis_index("tensor")
        other = 1 - s

        barrier = pltpu.get_barrier_semaphore()
        for k in range(1, T):
            pl.semaphore_signal(
                barrier, inc=1, device_id={"tensor": lax.rem(t + k, T)}, device_id_type=MESH
            )
        for k in range(1, DP):
            pl.semaphore_signal(
                barrier, inc=1, device_id={"dp": lax.rem(d + k, DP)}, device_id_type=MESH
            )
        pl.semaphore_signal(barrier, inc=1, device_id={"section": other}, device_id_type=MESH)
        pl.semaphore_wait(barrier, T + DP - 1)

        def gathered(index, owner):
            if index < 2:
                return (wq, wup)[index].at[pl.ds(pl.multiple_of(owner * DR, DR), DR)]
            return (wout, wdn)[index - 2].at[owner]

        def weight_copy(index, way, hop, owner, own):
            place = gathered(index, owner)
            return pltpu.make_async_remote_copy(
                src_ref=(wq_in, wup_in, wout_in, wdn_in)[index] if own else place, dst_ref=place,
                send_sem=w_ss.at[index, way, hop], recv_sem=w_rs.at[index, way, hop],
                device_id={"dp": d + 1 if way == 0 else d - 1}, device_id_type=MESH,
            )

        has_next = (d < DP - 1, d > 0)

        def holds(way, hop):
            return d >= hop + 1 if way == 0 else d + hop + 1 <= DP - 1

        def owner_of(way, hop):
            return d - hop - 1 if way == 0 else d + hop + 1

        def weight_local(index):
            return pltpu.make_async_copy(
                (wq_in, wup_in, wout_in, wdn_in)[index], gathered(index, d), w_ls.at[index]
            )

        def weights_start(indices):
            for index in indices:
                for way in range(2):
                    @pl.when(has_next[way])
                    def _(index=index, way=way):
                        weight_copy(index, way, 0, d, True).start()

        def weights_hop(indices, hop):
            for index in indices:
                for way in range(2):
                    @pl.when(holds(way, hop))
                    def _(index=index, way=way):
                        weight_copy(index, way, hop, owner_of(way, hop), False).wait_recv()

                        @pl.when(has_next[way])
                        def _():
                            weight_copy(index, way, hop + 1, owner_of(way, hop), False).start()

        def weights_pass(indices, first):
            def step(hop, carry):
                weights_hop(indices, hop)
                return carry

            lax.fori_loop(first, DP - 1, step, 0)

        def weights_sent():
            for index in range(4):
                for way in range(2):
                    @pl.when(has_next[way])
                    def _(index=index, way=way):
                        weight_copy(index, way, 0, d, True).wait_send()

            def step(hop, carry):
                for index in range(4):
                    for way in range(2):
                        @pl.when(jnp.logical_and(has_next[way], holds(way, hop)))
                        def _(index=index, way=way):
                            weight_copy(index, way, hop + 1, owner_of(way, hop), False).wait_send()
                return carry

            lax.fori_loop(0, DP - 1, step, 0)

        for index in range(4):
            weight_local(index).start()

        down, wide = 3 * QC, 3 * QC + FFL
        factors = (
            (aq_in, dk.at[0], aq, 1.0), (au_in, dk.at[1], au, 1.0),
            (ad_in, dv.at[0], ad, 1.0), (ao_in, dv.at[1, 0:QC], ao, 1.0),
            (bq_in, ga.at[:, 0:down], bq, ADAPTER_SCALE), (bu_in, ga.at[:, down:wide], bu, ADAPTER_SCALE),
            (bo_in, gr.at[:, 0:D], bo, ADAPTER_SCALE), (bd_in, gr.at[:, D:2 * D], bd, ADAPTER_SCALE),
        )

        def factor_load(index):
            source, stage, _, _ = factors[index]
            return pltpu.make_async_copy(source, stage, f_s.at[index])

        def factors_take():
            for index in range(8):
                factor_load(index).wait()
            for _, stage, place, scale in factors:
                v = stage[...]
                place[...] = (v if scale == 1.0 else v * scale).astype(BF)
            ga[...] = jnp.zeros_like(ga)
            gr[...] = jnp.zeros_like(gr)
            gb[...] = jnp.zeros_like(gb)

        for index in range(8):
            factor_load(index).start()

        def across(c):
            return lax.rem(t + c, 2) + 2 * lax.rem(t // 2 + c // 2, 2)

        def block(i):
            return pl.ds(pl.multiple_of(i * R, R), R)

        def half(i, low):
            return pl.ds(pl.multiple_of(i * R + (B if low else 0), B), B)

        def rows_copy(buf, m, kind, ssem, rsem):
            if kind < 2:
                place = buf.at[m, block(t)]
            elif kind == 2:
                place = buf.at[m, half(across(1), False)]
            else:
                place = buf.at[m, half(across(2), True)]
            return pltpu.make_async_remote_copy(
                src_ref=place, dst_ref=place,
                send_sem=ssem.at[m * 4 + kind], recv_sem=rsem.at[m * 4 + kind],
                device_id={"tensor": across((1, 2, 2, 1)[kind])}, device_id_type=MESH,
            )

        def rows_wait(buf, m, kind, ssem, rsem):
            if kind < 2:
                place = buf.at[m, block(across(1 + kind))]
            else:
                place = buf.at[m, half(across(3), kind == 3)]
            pltpu.make_async_remote_copy(
                src_ref=place, dst_ref=place,
                send_sem=ssem.at[m * 4 + kind], recv_sem=rsem.at[m * 4 + kind],
                device_id={"tensor": across(1)}, device_id_type=MESH,
            ).wait_recv()

        def rows_start(buf, m, ssem, rsem):
            for kind in range(2):
                rows_copy(buf, m, kind, ssem, rsem).start()

        def rows_next(buf, m, c, ssem, rsem):
            @pl.when(c == 1)
            def _():
                for kind in range(2):
                    rows_wait(buf, m, kind, ssem, rsem)
                    rows_copy(buf, m, 2 + kind, ssem, rsem).start()

            @pl.when(c == 3)
            def _():
                for kind in range(2, 4):
                    rows_wait(buf, m, kind, ssem, rsem)

        def rows_sent(buf, m, ssem, rsem):
            for kind in range(4):
                rows_copy(buf, m, kind, ssem, rsem).wait_send()

        def to_peer(axis, size, me, k, src, dst, ssem, rsem):
            return pltpu.make_async_remote_copy(
                src_ref=src, dst_ref=dst, send_sem=ssem, recv_sem=rsem,
                device_id={axis: lax.rem(me + k, size)}, device_id_type=MESH,
            )

        def block_copy(phase, kind):
            place = (
                sbuf.at[across(1), 0:B], sbuf.at[across(3), 0:B],
                sbuf.at[across(2), B:R], sbuf.at[across(3), B:R],
                sbuf.at[across(2), 0:B], sbuf.at[across(1), B:R],
            )[kind]
            return pltpu.make_async_remote_copy(
                src_ref=place, dst_ref=rbuf.at[lax.rem(phase, M) * 6 + kind],
                send_sem=r_ss.at[kind], recv_sem=r_rs.at[phase * 6 + kind],
                device_id={"tensor": across((1, 1, 2, 2, 2, 1)[kind])}, device_id_type=MESH,
            )

        def blocks_next(phase, m, c):
            @pl.when(c == 3)
            def _():
                block_copy(phase, 1).start()
                block_copy(phase, 3).start()

            @pl.when(c == 2)
            def _():
                block_copy(phase, 2).start()

            @pl.when(c == 1)
            def _():
                block_copy(phase, 0).start()
                block_copy(phase, 1).wait_recv()
                place = across(2)
                sbuf[place, 0:B] = (
                    sbuf[place, 0:B].astype(F32) + rbuf[m * 6 + 1].astype(F32)
                ).astype(BF)
                block_copy(phase, 4).start()
                block_copy(phase, 3).wait_recv()
                place = across(1)
                sbuf[place, B:R] = (
                    sbuf[place, B:R].astype(F32) + rbuf[m * 6 + 3].astype(F32)
                ).astype(BF)
                block_copy(phase, 5).start()

        def block_sum(m, low, cols=slice(None)):
            if low:
                own, first, second = sbuf[t, B:R, cols], rbuf[m * 6 + 2, :, cols], rbuf[m * 6 + 5, :, cols]
            else:
                own, first, second = sbuf[t, 0:B, cols], rbuf[m * 6, :, cols], rbuf[m * 6 + 4, :, cols]
            return own.astype(F32) + (first.astype(F32) + second.astype(F32))

        def blocks_arrive(phase):
            for kind in (0, 2, 4, 5):
                block_copy(phase, kind).wait_recv()

        def blocks_sent(phase):
            for kind in range(6):
                block_copy(phase, kind).wait_send()

        def section_copy(m, phase):
            return pltpu.make_async_remote_copy(
                src_ref=sxs, dst_ref=srec.at[m],
                send_sem=c_ss.at[0], recv_sem=c_rs.at[phase * M + m],
                device_id={"section": other}, device_id_type=MESH,
            )

        def local_copy(src, dst, index):
            return pltpu.make_async_copy(src, dst, l_s.at[index])

        def norm_parts(x):
            mean = jnp.mean(x, axis=-1, keepdims=True)
            centred = x - mean
            spread = jnp.mean(centred * centred, axis=-1, keepdims=True)
            rstd = lax.rsqrt(spread + EPSILON)
            return centred * rstd, rstd

        def send_normed(m):
            xhat, _ = norm_parts(xw[m])
            xh[m, block(t)] = xhat.astype(BF)
            rows_start(xh, m, x_ss, x_rs)

        def take_gradient(m):
            section_copy(m, 1).wait_recv()
            dz[m, block(t)] = srec[m]
            rows_start(dz, m, z_ss, z_rs)

        def take_x(m):
            section_copy(m, 0).wait_recv()
            xw[m] = srec[m].astype(F32)
            send_normed(m)

        lane = lax.broadcasted_iota(jnp.int32, (R, 128), 1)
        in_first = lax.rem(lane, HEAD) < ROT // 2
        head_low = lane < HEAD

        def turn(v, cosine, sine):
            swapped = jnp.where(in_first, pltpu.roll(v, 128 - ROT // 2, 1), pltpu.roll(v, ROT // 2, 1))
            return v * cosine + swapped * sine

        def rope_of(m, chunk):
            again = jnp.where(chunk * R >= HALF, chunk * R - HALF, chunk * R)
            plain = rope[pl.ds(pl.multiple_of(chunk * R, R), R), :]
            restarted = rope[pl.ds(pl.multiple_of(again, R), R), :]
            table = jnp.where(split[m] > 0, restarted, plain)
            crossed = pltpu.roll(table, HEAD, 1)
            return jnp.where(head_low, table, crossed), jnp.where(head_low, crossed, table)

        def head_part(v, hh):
            zero = jnp.zeros_like(v)
            return jnp.where(head_low, v, zero) if hh == 0 else jnp.where(head_low, zero, v)

        causal = lax.broadcasted_iota(jnp.int32, (R, R), 0) <= lax.broadcasted_iota(
            jnp.int32, (R, R), 1
        )

        def scores_t(m, p, i, j, q):
            keys = kp[m * PAIRS + p, j * R:(j + 1) * R, :]
            sc = nt(keys, q)
            if j == i:
                sc = jnp.where(causal, sc, MASKED)
            if i * R >= HALF and j * R < HALF:
                sc = sc + MASKED * split[m].astype(F32)
            return sc

        @pl.when(s == 0)
        def _():
            weights_start((0, 1))
            loads = [local_copy(x_in.at[m], xw.at[m], m) for m in range(M)]
            for copy in loads:
                copy.start()
            for m in range(M):
                loads[m].wait()
                send_normed(m)
            factors_take()
            weights_pass((0, 1), 0)
            weights_start((2, 3))

        @pl.when(s == 1)
        def _():
            loads = [local_copy(ct_in.at[m], xw.at[m], m) for m in range(M)]
            for copy in loads:
                copy.start()
            for m in range(M):
                loads[m].wait()
                dz[m, block(t)] = xw[m].astype(BF)
                rows_start(dz, m, z_ss, z_rs)
            factors_take()
            pl.semaphore_wait(go, 1)
            weights_start((0, 1))
            weights_pass((0, 1), 0)
            weights_start((2, 3))
            take_x(0)

        for index in range(4):
            weight_local(index).wait()

        def normed_to_hidden(m):
            @pl.when(m > 0)
            def _():
                local_copy(dg, dg_hbm.at[m - 1], 2).wait()

            def chunk(c, carry):
                src = across(c)
                rows_next(xh, m, c, x_ss, x_rs)

                @pl.when(jnp.logical_and(c == T - 2, m < DP - 1))
                def _():
                    weights_hop((2, 3), 2 * m)

                rows = block(src)
                xhc = xh[m, rows, :].astype(F32)
                n1 = (xhc * gain[0:1] + bias[0:1]).astype(BF)
                n2 = (xhc * gain[1:2] + bias[1:2]).astype(BF)
                t1 = nn(n1, aq[...]).astype(BF)
                t2 = nn(n2, au[...]).astype(BF)
                t12t[m, 0:RANK, rows] = t1.T
                t12t[m, RANK:2 * RANK, rows] = t2.T
                cosine, sine = rope_of(m, src)
                for part in range(3):
                    cols = slice(part * QC, (part + 1) * QC)
                    val = nn(n1, wq[:, cols]) + nn(t1, bq[:, cols])
                    if part == 2:
                        vb = val.astype(BF)
                        for p in range(PAIRS):
                            vp[m * PAIRS + p, rows, :] = vb[:, p * 128:(p + 1) * 128]
                        vT[m, :, rows] = vb.T
                    else:
                        for p in range(PAIRS):
                            v = turn(val[:, p * 128:(p + 1) * 128], cosine, sine)
                            if part == 0:
                                qp[m * PAIRS + p, rows, :] = (v * 0.125).astype(BF)
                            else:
                                vb = v.astype(BF)
                                kp[m * PAIRS + p, rows, :] = vb
                                kT[m, p * 128:(p + 1) * 128, rows] = vb.T
                for n0 in range(0, FFL, TILE):
                    cols = slice(n0, n0 + TILE)
                    u = nn(n2, wup[:, cols]) + nn(t2, bu[:, cols])
                    phi = 0.5 * (1.0 + lax.erf(u * 0.7071067811865476))
                    hw[m, rows, cols] = (u * phi).astype(BF)
                    dg[rows, cols] = (
                        phi + u * (0.3989422804014327 * jnp.exp(-0.5 * u * u))
                    ).astype(BF)
                return carry

            lax.fori_loop(0, T, chunk, 0)
            local_copy(dg, dg_hbm.at[m], 2).start()

        def attend(m):
            for i in range(T):
                icols = slice(i * R, (i + 1) * R)

                def pair(p, carry, i=i, icols=icols):
                    for hh in range(2):
                        h = 2 * p + hh
                        q = head_part(qp[m * PAIRS + p, icols, :], hh)
                        hrows = pl.ds(pl.multiple_of(h * HEAD, HEAD), HEAD)
                        blocks = [scores_t(m, p, i, j, q) for j in range(i + 1)]
                        top = functools.reduce(
                            jnp.maximum, [jnp.max(b, axis=0, keepdims=True) for b in blocks]
                        )
                        total = jnp.zeros_like(top)
                        acc = jnp.zeros((HEAD, R), F32)
                        for j in range(i + 1):
                            e = jnp.exp(blocks[j] - top)
                            total = total + jnp.sum(e, axis=0, keepdims=True)
                            acc = acc + nn(vT[m, hrows, j * R:(j + 1) * R], e.astype(BF))
                        oT[m, hrows, icols] = (acc * (1.0 / total)).astype(BF)
                        lse[pl.ds(m * HEADS + h, 1), icols] = top + jnp.log(total)
                    return carry

                lax.fori_loop(0, PAIRS, pair, 0)

        def project(m):
            def step(n, carry):
                c = T - 1 - n
                i = across(c)
                rows = block(i)
                o = oT[m, :, rows].T
                hrow = hw[m, rows, :]
                to = nn(o, ao[...]).astype(BF)
                td = nn(hrow, ad[...]).astype(BF)
                todt[m, 0:RANK, rows] = to.T
                todt[m, RANK:2 * RANK, rows] = td.T
                for j in range(DP):
                    cols = slice(j * DR, (j + 1) * DR)
                    sbuf[i, :, cols] = (
                        nn(o, wout[j]) + nn(hrow, wdn[j]) + nn(to, bo[:, cols]) + nn(td, bd[:, cols])
                    ).astype(BF)
                blocks_next(m, m, c)
                return carry

            lax.fori_loop(0, T, step, 0)

        def finish_forward(m):
            @pl.when(m > 0)
            def _():
                local_copy(yw, act.at[m - 1], 3).wait()

            blocks_arrive(m)
            for low in range(2):
                rows = slice(low * B, (low + 1) * B)
                y = xw[m, rows, :] + block_sum(m, low)
                yw[rows, :] = y
                sxs[rows, :] = y.astype(BF)

            @pl.when(s == 0)
            def _():
                section_copy(m, 0).start()

            local_copy(yw, act.at[m], 3).start()
            rows_sent(xh, m, x_ss, x_rs)
            blocks_sent(m)

            @pl.when(s == 0)
            def _():
                section_copy(m, 0).wait_send()

        def forward(step, carry):
            @pl.when(step < M)
            def _():
                normed_to_hidden(step)

            @pl.when(step == 1)
            def _():
                weights_pass((2, 3), 3)
                weights_sent()

                @pl.when(s == 0)
                def _():
                    pl.semaphore_signal(go, inc=1, device_id={"section": other}, device_id_type=MESH)

            @pl.when(step > 0)
            def _():
                project(step - 1)

            @pl.when(jnp.logical_and(s == 1, step < M - 1))
            def _():
                take_x(step + 1)

            @pl.when(step < M)
            def _():
                attend(step)

            @pl.when(step == 0)
            def _():
                if DP > 2:
                    weights_hop((2, 3), 1)

            @pl.when(jnp.logical_or(jnp.logical_and(step > 0, step < M), jnp.logical_and(step == M, s == 0)))
            def _():
                finish_forward(step - 1)
            return carry

        lax.fori_loop(0, M + 1, forward, 0)
        local_copy(dg, dg_hbm.at[M - 1], 2).wait()
        local_copy(dg_hbm.at[0], dg, 2).start()

        def gradient_to_hidden(m):
            local_copy(dg_hbm.at[m], dg, 2).wait()

            def chunk(c, carry):
                src = across(c)
                rows_next(dz, m, c, z_ss, z_rs)
                rows = block(src)
                full = dz[m, rows, :]
                eo = nt(full, bo[...]).astype(BF)
                ed = nt(full, bd[...]).astype(BF)
                edot[0:RANK, rows] = eo.T
                edot[RANK:2 * RANK, rows] = ed.T
                do = nt(eo, ao[...])
                for j in range(DP):
                    do = do + nt(full[:, j * DR:(j + 1) * DR], wout[j])
                dob = do.astype(BF)
                for p in range(PAIRS):
                    v = dob[:, p * 128:(p + 1) * 128]
                    dop[p, rows, :] = v
                prod = dob.T.astype(F32) * oT[m, :, rows].astype(F32)
                for h in range(HEADS):
                    delta[h:h + 1, rows] = jnp.sum(
                        prod[h * HEAD:(h + 1) * HEAD], axis=0, keepdims=True
                    )
                for n0 in range(0, FFL, TILE):
                    cols = slice(n0, n0 + TILE)
                    v = nt(ed, ad[cols, :])
                    for j in range(DP):
                        v = v + nt(full[:, j * DR:(j + 1) * DR], wdn[j, cols, :])
                    dg[rows, cols] = (v * dg[rows, cols].astype(F32)).astype(BF)
                return carry

            lax.fori_loop(0, T, chunk, 0)

        def attention_back(m):
            dk[...] = jnp.zeros_like(dk)
            dv[...] = jnp.zeros_like(dv)
            for i in range(T):
                icols = slice(i * R, (i + 1) * R)

                def pair(p, carry, i=i, icols=icols):
                    for hh in range(2):
                        h = 2 * p + hh
                        q = head_part(qp[m * PAIRS + p, icols, :], hh)
                        do = head_part(dop[p, icols, :], hh)
                        hrows = pl.ds(pl.multiple_of(h * HEAD, HEAD), HEAD)
                        low = lse[pl.ds(m * HEADS + h, 1), icols]
                        dlt = delta[pl.ds(h, 1), icols]
                        acc = jnp.zeros((HEAD, R), F32)
                        for j in range(i + 1):
                            jrows = slice(j * R, (j + 1) * R)
                            prob = jnp.exp(scores_t(m, p, i, j, q) - low)
                            dp_t = nt(vp[m * PAIRS + p, jrows, :], do)
                            ds_t = (prob * (dp_t - dlt)).astype(BF)
                            dv[p, jrows, :] += nn(prob.astype(BF), do)
                            dk[p, jrows, :] += nn(ds_t, q)
                            acc = acc + nn(kT[m, hrows, jrows], ds_t)
                        dqt[hrows, icols] = acc
                    return carry

                lax.fori_loop(0, PAIRS, pair, 0)

        def turn_back(m):
            def step(i, carry):
                rows = block(i)
                cosine, sine = rope_of(m, i)
                sine = -sine
                dq = dqt[:, rows].T * 0.125
                for p in range(PAIRS):
                    lanes = slice(p * 128, (p + 1) * 128)
                    dqkv[rows, p * 128:(p + 1) * 128] = turn(dq[:, lanes], cosine, sine).astype(BF)
                    dqkv[rows, QC + p * 128:QC + (p + 1) * 128] = turn(
                        dk[p, rows, :], cosine, sine
                    ).astype(BF)
                    dqkv[rows, 2 * QC + p * 128:2 * QC + (p + 1) * 128] = dv[p, rows, :].astype(BF)
                dop[0, rows, :] = nt(dqkv[rows, :], bq[...]).astype(BF)
                dop[1, rows, :] = nt(dg[rows, :], bu[...]).astype(BF)
                return carry

            lax.fori_loop(0, T, step, 0)

        def project_back(m):
            def tail(n, carry):
                c = T - 1 - n
                i = across(c)
                rows = block(i)
                dj = dqkv[rows, :]
                du = dg[rows, :]
                e1 = dop[0, rows, :]
                e2 = dop[1, rows, :]
                for n0 in range(0, D, TILE):
                    cols = slice(n0, n0 + TILE)
                    dn1 = nt(dj, wq[cols, :]) + nt(e1, aq[cols, :])
                    dn2 = nt(du, wup[cols, :]) + nt(e2, au[cols, :])
                    xhc = xh[m, rows, cols].astype(F32)
                    gb[0:1, cols] += jnp.sum(dn1 * xhc, axis=0, keepdims=True)
                    gb[1:2, cols] += jnp.sum(dn2 * xhc, axis=0, keepdims=True)
                    gb[2:3, cols] += jnp.sum(dn1, axis=0, keepdims=True)
                    gb[3:4, cols] += jnp.sum(dn2, axis=0, keepdims=True)
                    sbuf[i, :, cols] = (dn1 * gain[0:1, cols] + dn2 * gain[1:2, cols]).astype(BF)
                blocks_next(M + m, m, c)
                return carry

            lax.fori_loop(0, T, tail, 0)

            @pl.when(m == 0)
            def _():
                local_copy(yw, act.at[M - 1], 3).wait()

            @pl.when(m > 0)
            def _():
                local_copy(yw, ig.at[m - 1], 3).wait()

            @pl.when(s == 1)
            def _():
                local_copy(ct_in.at[m], yw, 0).start()

        def factor_gradients(m):
            base = 0
            ga[:, base:base + 3 * QC] += ADAPTER_SCALE * nn(t12t[m, 0:RANK, :], dqkv[...])
            base += 3 * QC
            ga[:, base:base + FFL] += ADAPTER_SCALE * nn(t12t[m, RANK:2 * RANK, :], dg[...])
            base += FFL
            ga[:, base:base + QC] += nt(edot[0:RANK, :], oT[m])
            base += QC
            ga[:, base:base + FFL] += nn(edot[RANK:2 * RANK, :], hw[m])
            gr[:, 2 * D:3 * D] += ADAPTER_SCALE * nn(todt[m, 0:RANK, :], dz[m])
            gr[:, 3 * D:4 * D] += ADAPTER_SCALE * nn(todt[m, RANK:2 * RANK, :], dz[m])

            def step(i, carry):
                rows = block(i)
                xhc = xh[m, rows, :].astype(F32)
                n1 = (xhc * gain[0:1] + bias[0:1]).astype(BF)
                gr[:, 0:D] += nn(dop[0, rows, :].T, n1)
                n2 = (xhc * gain[1:2] + bias[1:2]).astype(BF)
                gr[:, D:2 * D] += nn(dop[1, rows, :].T, n2)
                return carry

            lax.fori_loop(0, T, step, 0)

        def next_hidden(m):
            @pl.when(m < M - 1)
            def _():
                local_copy(dg_hbm.at[m + 1], dg, 2).start()

        def finish_backward(m):
            @pl.when(s == 1)
            def _():
                local_copy(ct_in.at[m], yw, 0).wait()

            @pl.when(s == 0)
            def _():
                yw[...] = srec[m].astype(F32)

            blocks_arrive(M + m)
            for low in range(2):
                rows = slice(low * B, (low + 1) * B)
                xhat, rstd = norm_parts(xw[m, rows, :])
                g = block_sum(m, low)
                mean_g = jnp.mean(g, axis=1, keepdims=True)
                mean_gx = jnp.mean(g * xhat, axis=1, keepdims=True)
                v = yw[rows, :] + (g - mean_g - xhat * mean_gx) * rstd
                yw[rows, :] = v
                sxs[rows, :] = v.astype(BF)

            @pl.when(s == 1)
            def _():
                section_copy(m, 1).start()

            local_copy(yw, ig.at[m], 3).start()
            rows_sent(dz, m, z_ss, z_rs)
            blocks_sent(M + m)

            @pl.when(s == 1)
            def _():
                section_copy(m, 1).wait_send()

        def over_dp(index, source, landing):
            for k in range(1, DP):
                yield to_peer("dp", DP, d, k, source(lax.rem(d + k, DP)), landing(k - 1),
                              ad_ss.at[index, k - 1], ad_rs.at[index, k - 1])

        def over_tensor(index, source, landing):
            for k in range(1, T):
                yield to_peer("tensor", T, t, k, source(lax.rem(t + k, T)), landing(k - 1),
                              at_ss.at[index, k - 1], at_rs.at[index, k - 1])

        def pa_scatter():
            return over_dp(0, lambda j: pa.at[j], lambda k: pa_in.at[k])

        def pa_gather():
            return over_dp(1, lambda j: pa_all.at[d], lambda k: pa_all.at[d])

        def pb_scatter(part):
            return over_dp(2 + part, lambda j: pb.at[part * DP + j], lambda k: pb_in.at[part * (DP - 1) + k])

        def pb_gather(part):
            place = pb_all.at[part * DP + d]
            return over_dp(4 + part, lambda j: place, lambda k: place)

        def pt_scatter(part):
            return over_tensor(part, lambda j: pt.at[part * T + j], lambda k: pt_in.at[part * (T - 1) + k])

        def pt_gather(part):
            return over_tensor(2 + part, lambda j: pt.at[part * T + t], lambda k: pt_all.at[part * (T - 1) + k])

        def gb_tensor():
            return over_tensor(4, lambda j: gb, lambda k: gb_t.at[k])

        def gb_dp():
            return over_dp(6, lambda j: gb_sum, lambda k: gb_d.at[k])

        def gathered_wait(index, buf, base):
            for k in range(1, DP):
                place = buf.at[base + lax.rem(d - k + DP, DP)]
                to_peer("dp", DP, d, k, place, place,
                        ad_ss.at[index, k - 1], ad_rs.at[index, k - 1]).wait_recv()

        def start_all(copies):
            for copy in copies:
                copy.start()

        def arrive_all(copies):
            for copy in copies:
                copy.wait_recv()

        def sent_all(copies):
            for copy in copies:
                copy.wait_send()

        def fill(buf, base, value, width):
            total = value.shape[1]
            for j in range(DP):
                lo, hi = min(j * width, total), min((j + 1) * width, total)
                if hi > lo:
                    buf[base + j, :, 0:hi - lo] = value[:, lo:hi].astype(BF)
                if hi - lo < width:
                    buf[base + j, :, hi - lo:width] = jnp.zeros((RANK, width - hi + lo), BF)

        def pt_fill(part):
            for j in range(T):
                lo = part * 2 * D + j * GRW
                pt[part * T + j] = gr[:, lo:lo + GRW].astype(BF)

        def pt_to_pb(part):
            arrive_all(pt_scatter(part))
            v = pt[part * T + t].astype(F32)
            for k in range(T - 1):
                v = v + pt_in[part * (T - 1) + k].astype(F32)
            fill(pb, part * DP, v, SW)
            start_all(pb_scatter(part))

        def pb_add(part):
            arrive_all(pb_scatter(part))
            v = pb[part * DP + d].astype(F32)
            for k in range(DP - 1):
                v = v + pb_in[part * (DP - 1) + k].astype(F32)
            pb_all[part * DP + d] = v.astype(BF)
            start_all(pb_gather(part))

        def pb_to_pt(part):
            gathered_wait(4 + part, pb_all, part * DP)
            for j in range(DP):
                lo, hi = min(j * SW, GRW), min((j + 1) * SW, GRW)
                if hi > lo:
                    pt[part * T + t, :, lo:hi] = pb_all[part * DP + j, :, 0:hi - lo]
            start_all(pt_gather(part))

        def gr_place(part, owner):
            return gr_out.at[:, pl.ds(pl.multiple_of(part * 2 * D + owner * GRW, 128), GRW)]

        def gr_store(part, k):
            if k == 0:
                return pltpu.make_async_copy(pt.at[part * T + t], gr_place(part, t), f_s.at[part * T])
            return pltpu.make_async_copy(
                pt_all.at[part * (T - 1) + k - 1], gr_place(part, lax.rem(t - k + T, T)),
                f_s.at[part * T + k],
            )

        def backward(step, carry):
            gradient_to_hidden(step)

            @pl.when(jnp.logical_and(s == 1, step == 0))
            def _():
                finish_forward(M - 1)

            @pl.when(jnp.logical_and(s == 0, step > 0))
            def _():
                finish_backward(step - 1)

            attention_back(step)
            turn_back(step)

            @pl.when(step < M - 1)
            def _():
                project_back(step)

                @pl.when(s == 0)
                def _():
                    take_gradient(step + 1)

                factor_gradients(step)
                next_hidden(step)

            @pl.when(step == M - 1)
            def _():
                factor_gradients(step)
                for part in range(2):
                    pt_fill(part)
                    start_all(pt_scatter(part))
                fill(pa, 0, ga, PW)
                start_all(pa_scatter())
                project_back(step)
                start_all(gb_tensor())
                for part in range(2):
                    pt_to_pb(part)
                arrive_all(pa_scatter())
                v = pa[d].astype(F32)
                for k in range(DP - 1):
                    v = v + pa_in[k].astype(F32)
                pa_all[d] = v.astype(BF)
                start_all(pa_gather())
                for part in range(2):
                    pb_add(part)

            @pl.when(jnp.logical_or(s == 1, step == M - 1))
            def _():
                finish_backward(step)
            return carry

        @pl.when(s == 0)
        def _():
            take_gradient(0)

        lax.fori_loop(0, M, backward, 0)

        arrive_all(gb_tensor())
        total = gb[...]
        for k in range(T - 1):
            total = total + gb_t[k]
        gb_sum[...] = total
        start_all(gb_dp())
        for part in range(2):
            pb_to_pt(part)
        arrive_all(gb_dp())
        sent_all(gb_tensor())
        total = gb_sum[...]
        for k in range(DP - 1):
            total = total + gb_d[k]
        gb[...] = total
        outs = [local_copy(gb, gb_out, 0)]
        outs[0].start()
        gathered_wait(1, pa_all, 0)
        for j in range(DP):
            copy = pltpu.make_async_copy(
                pa_all.at[j], ga_out.at[:, j * PW:(j + 1) * PW], w_ls.at[4 + j]
            )
            copy.start()
            outs.append(copy)
        for part in range(2):
            arrive_all(pt_gather(part))
            for k in range(T):
                copy = gr_store(part, k)
                copy.start()
                outs.append(copy)
        for copies in (pa_scatter(), pa_gather(), gb_dp(), pt_scatter(0), pt_scatter(1),
                       pt_gather(0), pt_gather(1), pb_scatter(0), pb_scatter(1),
                       pb_gather(0), pb_gather(1)):
            sent_all(copies)
        for copy in outs:
            copy.wait()
        local_copy(yw, ig.at[M - 1], 3).wait()

    any_spec = pl.BlockSpec(memory_space=pl.ANY)
    vmem_spec = pl.BlockSpec(memory_space=pltpu.VMEM)
    smem_spec = pl.BlockSpec(memory_space=pltpu.SMEM)
    shapes = jax.ShapeDtypeStruct
    return pl.pallas_call(
        kernel,
        out_shape=(
            shapes((M, R, D), F32), shapes((M, R, D), F32),
            shapes((RANK, DP * PW), BF), shapes((RANK, 4 * D), BF), shapes((8, D), F32),
            shapes((M, L, FFL), BF),
        ),
        in_specs=[any_spec] * 14 + [vmem_spec] * 3 + [smem_spec],
        out_specs=(any_spec,) * 6,
        scratch_shapes=[
            pltpu.VMEM((D, RANK), BF), pltpu.VMEM((RANK, 3 * QC), BF),
            pltpu.VMEM((QC, RANK), BF), pltpu.VMEM((RANK, D), BF),
            pltpu.VMEM((D, RANK), BF), pltpu.VMEM((RANK, FFL), BF),
            pltpu.VMEM((FFL, RANK), BF), pltpu.VMEM((RANK, D), BF),
            pltpu.VMEM((D, 3 * QC), BF), pltpu.VMEM((D, FFL), BF),
            pltpu.VMEM((DP, QC, DR), BF), pltpu.VMEM((DP, FFL, DR), BF),
            pltpu.VMEM((M, L, D), BF),
            pltpu.VMEM((M, 2 * RANK, L), BF),
            pltpu.VMEM((M * PAIRS, L, 128), BF),
            pltpu.VMEM((M * PAIRS, L, 128), BF),
            pltpu.VMEM((M * PAIRS, L, 128), BF),
            pltpu.VMEM((M, QC, L), BF),
            pltpu.VMEM((M, QC, L), BF),
            pltpu.VMEM((M, QC, L), BF),
            pltpu.VMEM((M * HEADS, L), F32),
            pltpu.VMEM((M, L, FFL), BF),
            pltpu.VMEM((L, FFL), BF),
            pltpu.VMEM((M, 2 * RANK, L), BF),
            pltpu.VMEM((T, R, D), BF),
            pltpu.VMEM((M * 6, B, D), BF),
            pltpu.VMEM((M, R, D), BF),
            pltpu.VMEM((R, D), BF),
            pltpu.VMEM((M, L, D), BF),
            pltpu.VMEM((PAIRS, L, 128), BF),
            pltpu.VMEM((8, L), F32),
            pltpu.VMEM((2 * RANK, L), BF),
            pltpu.VMEM((PAIRS, L, 128), F32),
            pltpu.VMEM((PAIRS, L, 128), F32),
            pltpu.VMEM((QC, L), F32),
            pltpu.VMEM((L, 3 * QC), BF),
            pltpu.VMEM((RANK, GA), F32),
            pltpu.VMEM((RANK, 4 * D), F32),
            pltpu.VMEM((8, D), F32),
            pltpu.VMEM((M, R, D), F32),
            pltpu.VMEM((R, D), F32),
            pltpu.VMEM((DP, RANK, PW), BF),
            pltpu.VMEM((DP - 1, RANK, PW), BF),
            pltpu.VMEM((DP, RANK, PW), BF),
            pltpu.VMEM((2 * T, RANK, GRW), BF),
            pltpu.VMEM((2 * (T - 1), RANK, GRW), BF),
            pltpu.VMEM((2 * (T - 1), RANK, GRW), BF),
            pltpu.VMEM((2 * DP, RANK, SW), BF),
            pltpu.VMEM((2 * (DP - 1), RANK, SW), BF),
            pltpu.VMEM((2 * DP, RANK, SW), BF),
            pltpu.VMEM((8, D), F32),
            pltpu.VMEM((T - 1, 8, D), F32),
            pltpu.VMEM((DP - 1, 8, D), F32),
            pltpu.SemaphoreType.DMA((4 + DP,)),
            pltpu.SemaphoreType.DMA((4, 2, DP)),
            pltpu.SemaphoreType.DMA((4, 2, DP)),
            pltpu.SemaphoreType.DMA((M * 4,)),
            pltpu.SemaphoreType.DMA((M * 4,)),
            pltpu.SemaphoreType.DMA((6,)),
            pltpu.SemaphoreType.DMA((2 * M * 6,)),
            pltpu.SemaphoreType.DMA((M * 4,)),
            pltpu.SemaphoreType.DMA((M * 4,)),
            pltpu.SemaphoreType.DMA((1,)),
            pltpu.SemaphoreType.DMA((2 * M,)),
            pltpu.SemaphoreType.DMA((4,)),
            pltpu.SemaphoreType.DMA((2 * max(T, 4),)),
            pltpu.SemaphoreType.REGULAR,
            pltpu.SemaphoreType.DMA((5, T - 1)),
            pltpu.SemaphoreType.DMA((5, T - 1)),
            pltpu.SemaphoreType.DMA((7, DP - 1)),
            pltpu.SemaphoreType.DMA((7, DP - 1)),
        ],
        compiler_params=pltpu.CompilerParams(
            collective_id=0, has_side_effects=True, vmem_limit_bytes=63 * 2**20
        ),
    )


def rope_table(length):
    half = ROT // 2
    inverse = np.float32(10000.0) ** (-np.arange(half, dtype=np.float32) * np.float32(2.0 / ROT))
    angles = np.arange(length, dtype=np.float32)[:, None] * inverse[None, :]
    cosine, sine = np.cos(angles.astype(np.float64)), np.sin(angles.astype(np.float64))
    rest = np.zeros((length, HEAD - ROT))
    return np.concatenate(
        [cosine, cosine, rest + 1.0, -sine, sine, rest], axis=-1
    ).astype(np.float32)


def solution(mesh):
    T = mesh.shape["tensor"]
    DP = mesh.shape["dp"]

    def per_device(
        inputs, cotangent, split,
        query_key_value_weight, output_weight, up_weight, down_weight,
        qkv_adapter_input, qkv_adapter_output, out_adapter_input, out_adapter_output,
        up_adapter_input, up_adapter_output, down_adapter_input, down_adapter_output,
        ln_gain, ln_bias,
    ):
        M, R, D = inputs.shape
        QC = output_weight.shape[1]
        FFL = up_weight.shape[2]
        RANK = qkv_adapter_input.shape[2]
        L = R * T
        wq = query_key_value_weight[0].reshape(-1, 3 * QC)
        aq = qkv_adapter_input[0].astype(BF)
        bq = (ADAPTER_SCALE * qkv_adapter_output[0].reshape(RANK, -1)).astype(BF)
        ao = out_adapter_input[0].astype(BF)
        bo = (ADAPTER_SCALE * out_adapter_output[0]).astype(BF)
        au = up_adapter_input[0].astype(BF)
        bu = (ADAPTER_SCALE * up_adapter_output[0]).astype(BF)
        ad = down_adapter_input[0].astype(BF)
        bd = (ADAPTER_SCALE * down_adapter_output[0]).astype(BF)
        kernel = make_kernel(T, DP, M, R, D, QC, FFL, RANK)
        act, ig, ga, gr, gb, _ = kernel(
            inputs, cotangent, wq, up_weight[0], output_weight[0], down_weight[0],
            qkv_adapter_input[0], qkv_adapter_output[0].reshape(RANK, -1),
            out_adapter_input[0], out_adapter_output[0],
            up_adapter_input[0], up_adapter_output[0],
            down_adapter_input[0], down_adapter_output[0],
            ln_gain[0], ln_bias[0], jnp.asarray(rope_table(L)), split[:, 0],
        )
        ga = ga.astype(F32)
        gr = gr.astype(F32)
        cuts = [3 * QC, 3 * QC + FFL, 4 * QC + FFL, 4 * QC + 2 * FFL]
        b_qkv, b_up, a_out, a_down, _ = jnp.split(ga, cuts, axis=1)
        a_qkv, a_up, b_out, b_down = jnp.split(gr, 4, axis=1)

        dp_place = lax.axis_index("dp")
        DR = D // DP
        sl = lax.dynamic_slice_in_dim
        c_qkv = wq.astype(F32) + nn(sl(aq, dp_place * DR, DR, 0), bq)
        c_out = output_weight[0].astype(F32) + nn(ao, sl(bo, dp_place * DR, DR, 1))
        c_up = up_weight[0].astype(F32) + nn(sl(au, dp_place * DR, DR, 0), bu)
        c_down = down_weight[0].astype(F32) + nn(ad, sl(bd, dp_place * DR, DR, 1))
        return (
            act[None], ig[None],
            a_qkv.T[None], b_qkv.reshape(qkv_adapter_output.shape),
            a_out.T[None], b_out[None], a_up.T[None], b_up[None], a_down.T[None], b_down[None],
            gb[0:2][None], gb[2:4][None],
            c_qkv.reshape(query_key_value_weight.shape), c_out[None], c_up[None], c_down[None],
        )

    rows = P(None, ("dp", "tensor"), None)
    whole = P("section", None, None)
    in_specs = (
        rows, rows, P(None, "dp"),
        P("section", "dp", None, "tensor"), P("section", "tensor", "dp"),
        P("section", "dp", "tensor"), P("section", "tensor", "dp"),
        whole, P("section", None, None, "tensor"), P("section", "tensor", None), whole,
        whole, P("section", None, "tensor"), P("section", "tensor", None), whole,
        whole, whole,
    )
    layer_rows = P("section", None, ("dp", "tensor"), None)
    out_specs = (
        layer_rows, layer_rows,
        whole, P("section", None, None, "tensor"), P("section", "tensor", None), whole,
        whole, P("section", None, "tensor"), P("section", "tensor", None), whole,
        whole, whole,
        P("section", "dp", None, "tensor"), P("section", "tensor", "dp"),
        P("section", "dp", "tensor"), P("section", "tensor", "dp"),
    )
    return jax.shard_map(
        per_device, mesh=mesh, in_specs=in_specs, out_specs=out_specs, check_vma=False
    )
```

time: 406 us -> 351 us (0.86)
  Pallas kernels: 364 us -> 323 us
  other arithmetic: 11.2 us -> 1.57 us
  local copies, waits for them, and re-layouts: 25.3 us -> 17.3 us
    pallas_call x1, Pallas kernels: 364 us -> 323 us  [per_device(): kernel(inputs, cotangent, wq, up_weight[0], output_weight[0], down_weight...]
    convert_element_type x13 -> x2, other arithmetic: 6.99 us -> 1.57 us  [the longest x1 1.37 us: per_device(): ga = ga.astype(F32)]
    concatenate x1 -> x0, local copies, waits for them, and re-layouts: 4.42 us -> none  [rope_table(): return jnp.concatenate([cos_head, sin_head], axis=-1)]
    unnamed x52 -> x34, local copies, waits for them, and re-layouts: 10.9 us -> 13 us
where the time goes in v3:
time: 351 us; the launch traced here: 350 us
  Pallas kernels  323 us (92%)
  local copies, waits for them, and re-layouts  17.3 us (5%)
  matrix products  7.42 us (2%)
    pallas_call x1, Pallas kernels, per_device(): kernel(inputs, cotangent, wq, up_weight[0], output_weight[0], down_weight...  323 us
    unnamed x34, local copies, waits for them, and re-layouts  13 us
    dot_general x4, matrix products, nn(): lax.dot_general(a, b, (((1,), (0,)), ((), ())), preferred_element_type=F32)  7.42 us

profile of v3, /device:TPU:0, one launch (start us, length us, event | category | flops | bytes accessed | tf_op | source)
XLA Modules:
  0.0 349.9 jit_solution(15776396890970701943)
XLA Ops:
  0.6 1.2 copy.44
  1.8 0.9 copy.46.wq_in
  2.7 1.1 copy.45
  3.9 0.9 copy.47.bq_in
  4.8 322.8 %shard_map.297 = (f32[2,256,1024]{2,1,0:T(8,128)}, f32[2,256,1024]{2,1,0:T(8,128)}, bf16[128,3072]{1,0:T(8,128)(2,1)}, bf16[128,4096]{1,0:T(8,128)(2,1)}, f32[8,...) custom-call(f32[2,256,1024]{2,1,0:T(8,128)} %x_in.1, f32[2,256,1024]{2,1,0:T(8,128)} %ct_in.1, bf16[256,768]{1,0:T(8,128)(2,1)} %copy.46.wq_in, ...), custom_call_target="tpu_custom_call" | custom-call | tf_op jit(solution)/shard_map/pallas_call | solution.py:1034
  327.6 0.0 copy-start.8
  327.6 1.4 convert_element_type.43
  329.0 0.1 copy-done.8
  329.1 0.2 convert_element_type.42
  329.3 1.4 slice_bitcast_fusion
  330.7 2.1 copy.53
  332.8 1.0 copy.56
  333.8 1.0 copy.57
  334.8 0.8 copy.55
  335.6 1.2 convolution_add_fusion.1
  336.8 0.3 copy.50
  337.0 0.0 copy-start.1
  337.1 0.0 copy-start.2
  337.1 1.1 copy.58
  338.2 0.0 copy-start.3
  338.3 0.0 copy-start.4
  338.3 0.2 copy.48
  338.4 0.9 copy.54
  339.4 0.6 slice_bitcast_fusion.7
  340.0 0.0 copy-start.10
  340.0 0.0 copy-start.6
  340.0 2.3 fusion.1
  342.3 2.2 fusion.2
  344.5 1.8 fusion.4
  346.3 1.3 copy.63
  347.6 1.0 copy-done.5
  348.6 1.3 copy.64
  (17 shorter events, 0.1 us)
Async XLA Ops:
  327.6 1.5 copy-start.8
  330.7 4.8 %copy-start = (bf16[256,768]{1,0:T(8,128)(2,1)S(1)}, bf16[256,768]{1,0:T(8,128)(2,1)}, u32[]{:S(2)}) copy-start(bf16[256,768]{1,0:T(8,128)(2,1)} %copy.46.wq_in) | copy-start | bytes 1179652
  336.7 1.5 copy-start.7
  337.0 2.3 copy-start.11
  337.0 2.9 copy-start.1
  337.1 2.9 copy-start.2
  338.2 4.1 %copy-start.3 = (bf16[1,256,1024]{2,1,0:T(8,128)(2,1)S(1)}, bf16[1,256,1024]{2,1,0:T(8,128)(2,1)}, u32[]{:S(2)}) copy-start(bf16[1,256,1024]{2,1,0:T(8,128)(2,1)} %param.23) | copy-start | bytes 1572868
  338.3 4.1 %copy-start.4 = (f32[1,128,1024]{2,1,0:T(8,128)S(1)}, f32[1,128,1024]{2,1,0:T(8,128)}, u32[]{:S(2)}) copy-start(f32[1,128,1024]{2,1,0:T(8,128)} %param.30) | copy-start | bytes 1572868
  340.0 4.5 %copy-start.9 = (bf16[1,256,256]{2,1,0:T(8,128)(2,1)S(1)}, bf16[1,256,256]{2,1,0:T(8,128)(2,1)}, u32[]{:S(2)}) copy-start(bf16[1,256,256]{2,1,0:T(8,128)(2,1)} %param.22) | copy-start | bytes 393220
  340.0 4.5 %copy-start.10 = (f32[1,256,128]{2,1,0:T(8,128)S(1)}, f32[1,256,128]{2,1,0:T(8,128)}, u32[]{:S(2)}) copy-start(f32[1,256,128]{2,1,0:T(8,128)} %param.27) | copy-start | bytes 393220
  340.0 6.3 %copy-start.6 = (f32[2,256,1024]{2,1,0:T(8,128)S(1)}, f32[2,256,1024]{2,1,0:T(8,128)}, u32[]{:S(2)}) copy-start(f32[2,256,1024]{2,1,0:T(8,128)} %get-tuple-element.21) | copy-start | bytes 6291460
  346.3 2.3 copy-start.5

commit v4 on v3

v4 whole, which is shorter than its diff:
```python
import functools

import jax
import jax.numpy as jnp
import numpy as np
from jax import lax
from jax.experimental import pallas as pl
from jax.experimental.pallas import tpu as pltpu
from jax.sharding import PartitionSpec as P

HEAD = 64
ROT = 16
ADAPTER_SCALE = 0.25
EPSILON = 1e-05
MASKED = -1e30
BF = jnp.bfloat16
F32 = jnp.float32
MESH = pl.DeviceIdType.MESH


def nn(a, b):
    return lax.dot_general(a, b, (((1,), (0,)), ((), ())), preferred_element_type=F32)


def nt(a, b):
    return lax.dot_general(a, b, (((1,), (1,)), ((), ())), preferred_element_type=F32)


def make_kernel(T, DP, M, R, D, QC, FFL, RANK):
    L = R * T
    DR = D // DP
    B = R // 2
    PAIRS = QC // 128
    HEADS = QC // HEAD
    TILE = 256
    HALF = L // 2
    GA = 4 * QC + 2 * FFL
    GRW = 2 * D // T
    PW = -(-GA // (DP * 128)) * 128
    SW = -(-GRW // (DP * 128)) * 128
    NA, NB = -(-GA // PW), -(-GRW // SW)

    def kernel(
        x_in, ct_in, wq_in, wup_in, wout_in, wdn_in,
        aq_in, bq_in, ao_in, bo_in, au_in, bu_in, ad_in, bd_in, gain_in, bias_in, rope, split,
        act, ig, ga_out, gr_out, gb_out, h_hbm, dg_hbm,
        aq, bq, ao, bo, au, bu, ad, bd, norms,
        wq, wup, wout, wdn, xh, t12t, qp, kp, vp, kT, vT, oT, lse, hw, dg,
        todt, sbuf, rbuf, dz, dop, delta, edot, dk, dv, dqt, dqkv,
        acc, gb, xw, yw, pa, pa_x, pa_in, pa_sum, pt, pt_x, pt_in, pb, pb_in, pb_all,
        gb_x, gb_sum, gb_t, gb_d,
        w_ls, w_ss, w_rs, v_ss, v_rs, x_ss, x_rs, r_ss, r_rs, z_ss, z_rs, c_ss, c_rs, l_s, f_s,
        go, at_ss, at_rs, ad_ss, ad_rs,
    ):
        s = lax.axis_index("section")
        d = lax.axis_index("dp")
        t = lax.axis_index("tensor")
        other = 1 - s

        barrier = pltpu.get_barrier_semaphore()
        for k in range(1, T):
            pl.semaphore_signal(
                barrier, inc=1, device_id={"tensor": lax.rem(t + k, T)}, device_id_type=MESH
            )
        for k in range(1, DP):
            pl.semaphore_signal(
                barrier, inc=1, device_id={"dp": lax.rem(d + k, DP)}, device_id_type=MESH
            )
        pl.semaphore_signal(barrier, inc=1, device_id={"section": other}, device_id_type=MESH)
        pl.semaphore_wait(barrier, T + DP - 1)

        def to_other(src, dst, ssem, rsem):
            return pltpu.make_async_remote_copy(
                src_ref=src, dst_ref=dst, send_sem=ssem, recv_sem=rsem,
                device_id={"section": other}, device_id_type=MESH,
            )

        shards = (wq_in, wup_in, wout_in, wdn_in)

        def gathered(index, layer, owner):
            return (wq, wup, wout, wdn)[index].at[layer, pl.ds(pl.multiple_of(owner * DR, DR), DR)]

        def weight_copy(index, way, hop, owner, own):
            place = gathered(index, s, owner)
            return pltpu.make_async_remote_copy(
                src_ref=shards[index] if own else place, dst_ref=place,
                send_sem=w_ss.at[index, way, hop], recv_sem=w_rs.at[index, way, hop],
                device_id={"dp": d + 1 if way == 0 else d - 1}, device_id_type=MESH,
            )

        def weight_over(index, layer, owner, own):
            place = gathered(index, layer, owner)
            return to_other(
                shards[index] if own else place, place, v_ss.at[index, owner], v_rs.at[index, owner]
            )

        has_next = (d < DP - 1, d > 0)

        def holds(way, hop):
            return d >= hop + 1 if way == 0 else d + hop + 1 <= DP - 1

        def owner_of(way, hop):
            return d - hop - 1 if way == 0 else d + hop + 1

        def weight_local(index):
            return pltpu.make_async_copy(shards[index], gathered(index, s, d), w_ls.at[index])

        def weights_start(indices):
            for index in indices:
                for way in range(2):
                    @pl.when(has_next[way])
                    def _(index=index, way=way):
                        weight_copy(index, way, 0, d, True).start()
                weight_over(index, s, d, True).start()

        def weights_hop(indices, hop):
            for index in indices:
                for way in range(2):
                    @pl.when(holds(way, hop))
                    def _(index=index, way=way):
                        owner = owner_of(way, hop)
                        weight_copy(index, way, hop, owner, False).wait_recv()

                        @pl.when(has_next[way])
                        def _():
                            weight_copy(index, way, hop + 1, owner, False).start()

                        weight_over(index, s, owner, False).start()

        def weights_pass(indices, first, last):
            if last > first:
                def step(hop, carry):
                    weights_hop(indices, hop)
                    return carry

                lax.fori_loop(first, last, step, 0)

        def weights_sent():
            for index in range(4):
                for way in range(2):
                    @pl.when(has_next[way])
                    def _(index=index, way=way):
                        weight_copy(index, way, 0, d, True).wait_send()

            def step(hop, carry):
                for index in range(4):
                    for way in range(2):
                        @pl.when(jnp.logical_and(has_next[way], holds(way, hop)))
                        def _(index=index, way=way):
                            weight_copy(index, way, hop + 1, owner_of(way, hop), False).wait_send()
                return carry

            lax.fori_loop(0, DP - 1, step, 0)

        def weights_from_other(indices, layer):
            def step(owner, carry):
                for index in indices:
                    weight_over(index, layer, owner, False).wait_recv()
                return carry

            lax.fori_loop(0, DP, step, 0)

        for index in range(4):
            weight_local(index).start()

        factors = (
            (aq_in, dk.at[0], aq, 1.0), (au_in, dk.at[1], au, 1.0),
            (ad_in, dv.at[0], ad, 1.0), (ao_in, dv.at[1, 0:QC], ao, 1.0),
            (bq_in, acc.at[0:RANK, 0:3 * QC], bq, ADAPTER_SCALE), (bu_in, acc.at[RANK:, 0:FFL], bu, ADAPTER_SCALE),
            (bo_in, dqt.at[0:RANK, 0:D], bo, ADAPTER_SCALE), (bd_in, dqt.at[RANK:2 * RANK, 0:D], bd, ADAPTER_SCALE),
        )

        def factor_load(index):
            source, stage, _, _ = factors[index]
            return pltpu.make_async_copy(source, stage, f_s.at[index])

        def factor_over(index, layer):
            place = norms.at[layer] if index == 8 else factors[index][2].at[layer]
            return to_other(place, place, c_ss.at[index], c_rs.at[index])

        def factors_give():
            norms[s, 0:2, :] = gain_in[...]
            norms[s, 2:4, :] = bias_in[...]
            factor_over(8, s).start()
            for index, (_, stage, place, scale) in enumerate(factors):
                factor_load(index).wait()
                v = stage[...]
                place[s] = (v if scale == 1.0 else v * scale).astype(BF)
                factor_over(index, s).start()

        for index in range(8):
            factor_load(index).start()

        def across(c):
            return lax.rem(t + c, 2) + 2 * lax.rem(t // 2 + c // 2, 2)

        def block(i):
            return pl.ds(pl.multiple_of(i * R, R), R)

        def half(i, low):
            return pl.ds(pl.multiple_of(i * R + (B if low else 0), B), B)

        def rows_copy(buf, m, kind, ssem, rsem):
            if kind < 2:
                place = buf.at[m, block(t)]
            elif kind == 2:
                place = buf.at[m, half(across(1), False)]
            else:
                place = buf.at[m, half(across(2), True)]
            return pltpu.make_async_remote_copy(
                src_ref=place, dst_ref=place,
                send_sem=ssem.at[m * 4 + kind], recv_sem=rsem.at[m * 4 + kind],
                device_id={"tensor": across((1, 2, 2, 1)[kind])}, device_id_type=MESH,
            )

        def rows_wait(buf, m, kind, ssem, rsem):
            if kind < 2:
                place = buf.at[m, block(across(1 + kind))]
            else:
                place = buf.at[m, half(across(3), kind == 3)]
            pltpu.make_async_remote_copy(
                src_ref=place, dst_ref=place,
                send_sem=ssem.at[m * 4 + kind], recv_sem=rsem.at[m * 4 + kind],
                device_id={"tensor": across(1)}, device_id_type=MESH,
            ).wait_recv()

        def rows_start(buf, m, ssem, rsem):
            for kind in range(2):
                rows_copy(buf, m, kind, ssem, rsem).start()

        def rows_next(buf, m, c, ssem, rsem):
            @pl.when(c == 1)
            def _():
                for kind in range(2):
                    rows_wait(buf, m, kind, ssem, rsem)
                    rows_copy(buf, m, 2 + kind, ssem, rsem).start()

            @pl.when(c == 3)
            def _():
                for kind in range(2, 4):
                    rows_wait(buf, m, kind, ssem, rsem)

        def rows_sent(buf, m, ssem, rsem):
            for kind in range(4):
                rows_copy(buf, m, kind, ssem, rsem).wait_send()

        def to_peer(axis, size, me, k, src, dst, ssem, rsem):
            return pltpu.make_async_remote_copy(
                src_ref=src, dst_ref=dst, send_sem=ssem, recv_sem=rsem,
                device_id={axis: lax.rem(me + k, size)}, device_id_type=MESH,
            )

        def block_copy(phase, kind):
            place = (
                sbuf.at[across(1), 0:B], sbuf.at[across(3), 0:B],
                sbuf.at[across(2), B:R], sbuf.at[across(3), B:R],
                sbuf.at[across(2), 0:B], sbuf.at[across(1), B:R],
            )[kind]
            return pltpu.make_async_remote_copy(
                src_ref=place, dst_ref=rbuf.at[lax.rem(phase, 2) * 6 + kind],
                send_sem=r_ss.at[kind], recv_sem=r_rs.at[phase * 6 + kind],
                device_id={"tensor": across((1, 1, 2, 2, 2, 1)[kind])}, device_id_type=MESH,
            )

        def blocks_next(phase, c):
            @pl.when(c == 3)
            def _():
                block_copy(phase, 1).start()
                block_copy(phase, 3).start()

            @pl.when(c == 2)
            def _():
                block_copy(phase, 2).start()

            @pl.when(c == 1)
            def _():
                block_copy(phase, 0).start()
                block_copy(phase, 1).wait_recv()
                place = across(2)
                sbuf[place, 0:B] = (
                    sbuf[place, 0:B].astype(F32) + rbuf[lax.rem(phase, 2) * 6 + 1].astype(F32)
                ).astype(BF)
                block_copy(phase, 4).start()
                block_copy(phase, 3).wait_recv()
                place = across(1)
                sbuf[place, B:R] = (
                    sbuf[place, B:R].astype(F32) + rbuf[lax.rem(phase, 2) * 6 + 3].astype(F32)
                ).astype(BF)
                block_copy(phase, 5).start()

        def block_sum(phase, low):
            base = lax.rem(phase, 2) * 6
            if low:
                own, first, second = sbuf[t, B:R], rbuf[base + 2], rbuf[base + 5]
            else:
                own, first, second = sbuf[t, 0:B], rbuf[base], rbuf[base + 4]
            return own.astype(F32) + (first.astype(F32) + second.astype(F32))

        def blocks_arrive(phase):
            for kind in (0, 2, 4, 5):
                block_copy(phase, kind).wait_recv()

        def blocks_sent(phase):
            for kind in range(6):
                block_copy(phase, kind).wait_send()

        def rows_out(src, out, layer, index):
            class Out:
                def start(self):
                    @pl.when(s == layer)
                    def _():
                        local_copy(src, out.at[s], 3 + index).start()

                    @pl.when(s != layer)
                    def _():
                        to_other(src, out.at[s], c_ss.at[9 + index], c_rs.at[9 + index]).start()

                def sent(self):
                    @pl.when(s == layer)
                    def _():
                        local_copy(src, out.at[s], 3 + index).wait()

                    @pl.when(s != layer)
                    def _():
                        to_other(src, out.at[s], c_ss.at[9 + index], c_rs.at[9 + index]).wait_send()

                def arrive(self):
                    @pl.when(s == layer)
                    def _():
                        to_other(src, out.at[other], c_ss.at[9 + index], c_rs.at[9 + index]).wait_recv()

            return Out()

        def act_out(layer):
            return rows_out(yw if layer else xw.at[1], act, layer, layer)

        def ig_out(layer):
            return rows_out(yw, ig, layer, 2 + layer)

        def local_copy(src, dst, index):
            return pltpu.make_async_copy(src, dst, l_s.at[index])

        def norm_parts(x):
            mean = jnp.mean(x, axis=-1, keepdims=True)
            centred = x - mean
            spread = jnp.mean(centred * centred, axis=-1, keepdims=True)
            rstd = lax.rsqrt(spread + EPSILON)
            return centred * rstd, rstd

        def send_normed(layer):
            xhat, _ = norm_parts(xw[layer])
            xh[layer, block(t)] = xhat.astype(BF)
            rows_start(xh, layer, x_ss, x_rs)

        lane = lax.broadcasted_iota(jnp.int32, (R, 128), 1)
        in_first = lax.rem(lane, HEAD) < ROT // 2
        head_low = lane < HEAD

        def turn(v, cosine, sine):
            swapped = jnp.where(in_first, pltpu.roll(v, 128 - ROT // 2, 1), pltpu.roll(v, ROT // 2, 1))
            return v * cosine + swapped * sine

        def rope_of(chunk):
            again = jnp.where(chunk * R >= HALF, chunk * R - HALF, chunk * R)
            plain = rope[pl.ds(pl.multiple_of(chunk * R, R), R), :]
            restarted = rope[pl.ds(pl.multiple_of(again, R), R), :]
            table = jnp.where(split[s] > 0, restarted, plain)
            crossed = pltpu.roll(table, HEAD, 1)
            return jnp.where(head_low, table, crossed), jnp.where(head_low, crossed, table)

        def head_part(v, hh):
            zero = jnp.zeros_like(v)
            return jnp.where(head_low, v, zero) if hh == 0 else jnp.where(head_low, zero, v)

        causal = lax.broadcasted_iota(jnp.int32, (R, R), 0) <= lax.broadcasted_iota(
            jnp.int32, (R, R), 1
        )

        def scores_t(m, p, i, j, q):
            keys = kp[m * PAIRS + p, j * R:(j + 1) * R, :]
            sc = nt(keys, q)
            if j == i:
                sc = jnp.where(causal, sc, MASKED)
            if i * R >= HALF and j * R < HALF:
                sc = sc + MASKED * split[s].astype(F32)
            return sc

        loads = [local_copy(x_in.at[s], xw.at[0], 0), local_copy(ct_in.at[s], yw, 1)]
        for copy in loads:
            copy.start()

        @pl.when(s == 0)
        def _():
            weights_start((0, 1))

        loads[0].wait()
        send_normed(0)
        loads[1].wait()
        dz[1, block(t)] = yw[...].astype(BF)
        rows_start(dz, 1, z_ss, z_rs)
        factors_give()
        gb[...] = jnp.zeros_like(gb)

        @pl.when(s == 0)
        def _():
            weights_pass((0, 1), 0, DP - 2)
            weights_start((2, 3))
            weights_pass((0, 1), DP - 2, DP - 1)

        for index in range(9):
            factor_over(index, other).wait_recv()
        for index in range(4):
            weight_local(index).wait()

        def gain_of(layer, j, cols=slice(None)):
            return norms[layer, j:j + 1, cols]

        def bias_of(layer, j):
            return norms[layer, 2 + j:3 + j, :]

        def normed_to_hidden(m):
            @pl.when(s != m)
            def _():
                weights_from_other((0, 1), m)

            @pl.when(m > 0)
            def _():
                local_copy(hw, h_hbm, 1).wait()
                local_copy(dg, dg_hbm, 2).wait()

            def chunk(c, carry):
                src = across(c)
                rows_next(xh, m, c, x_ss, x_rs)

                @pl.when(jnp.logical_and(c == 2, s == m))
                def _():
                    weights_hop((2, 3), 0)

                rows = block(src)
                xhc = xh[m, rows, :].astype(F32)
                n1 = (xhc * gain_of(m, 0) + bias_of(m, 0)).astype(BF)
                n2 = (xhc * gain_of(m, 1) + bias_of(m, 1)).astype(BF)
                t1 = nn(n1, aq[m]).astype(BF)
                t2 = nn(n2, au[m]).astype(BF)
                t12t[m, 0:RANK, rows] = t1.T
                t12t[m, RANK:2 * RANK, rows] = t2.T
                cosine, sine = rope_of(src)
                for part in range(3):
                    cols = slice(part * QC, (part + 1) * QC)
                    val = nn(n1, wq[m, :, cols]) + nn(t1, bq[m, :, cols])
                    if part == 2:
                        vb = val.astype(BF)
                        for p in range(PAIRS):
                            vp[m * PAIRS + p, rows, :] = vb[:, p * 128:(p + 1) * 128]
                        vT[:, rows] = vb.T
                    else:
                        for p in range(PAIRS):
                            v = turn(val[:, p * 128:(p + 1) * 128], cosine, sine)
                            if part == 0:
                                qp[m * PAIRS + p, rows, :] = (v * 0.125).astype(BF)
                            else:
                                vb = v.astype(BF)
                                kp[m * PAIRS + p, rows, :] = vb
                                kT[m, p * 128:(p + 1) * 128, rows] = vb.T
                for n0 in range(0, FFL, TILE):
                    cols = slice(n0, n0 + TILE)
                    u = nn(n2, wup[m, :, cols]) + nn(t2, bu[m, :, cols])
                    phi = 0.5 * (1.0 + lax.erf(u * 0.7071067811865476))
                    hw[rows, cols] = (u * phi).astype(BF)
                    dg[rows, cols] = (
                        phi + u * (0.3989422804014327 * jnp.exp(-0.5 * u * u))
                    ).astype(BF)
                return carry

            lax.fori_loop(0, T, chunk, 0)
            @pl.when(m == 0)
            def _():
                local_copy(hw, h_hbm, 1).start()
                local_copy(dg, dg_hbm, 2).start()

        def attend(m):
            for i in range(T):
                icols = slice(i * R, (i + 1) * R)

                def pair(p, carry, i=i, icols=icols):
                    for hh in range(2):
                        h = 2 * p + hh
                        q = head_part(qp[m * PAIRS + p, icols, :], hh)
                        hrows = pl.ds(pl.multiple_of(h * HEAD, HEAD), HEAD)
                        blocks = [scores_t(m, p, i, j, q) for j in range(i + 1)]
                        top = functools.reduce(
                            jnp.maximum, [jnp.max(b, axis=0, keepdims=True) for b in blocks]
                        )
                        total = jnp.zeros_like(top)
                        acc = jnp.zeros((HEAD, R), F32)
                        for j in range(i + 1):
                            e = jnp.exp(blocks[j] - top)
                            total = total + jnp.sum(e, axis=0, keepdims=True)
                            acc = acc + nn(vT[hrows, j * R:(j + 1) * R], e.astype(BF))
                        oT[m, hrows, icols] = (acc * (1.0 / total)).astype(BF)
                        lse[pl.ds(m * HEADS + h, 1), icols] = top + jnp.log(total)
                    return carry

                lax.fori_loop(0, PAIRS, pair, 0)

        def project(m):
            @pl.when(s != m)
            def _():
                weights_from_other((2, 3), m)

            def step(n, carry):
                c = T - 1 - n
                i = across(c)
                rows = block(i)
                o = oT[m, :, rows].T
                hrow = hw[rows, :]
                to = nn(o, ao[m]).astype(BF)
                td = nn(hrow, ad[m]).astype(BF)
                todt[m, 0:RANK, rows] = to.T
                todt[m, RANK:2 * RANK, rows] = td.T
                for n0 in range(0, D, TILE):
                    cols = slice(n0, n0 + TILE)
                    sbuf[i, :, cols] = (
                        nt(o, wout[m, cols, :]) + nt(hrow, wdn[m, cols, :])
                        + nn(to, bo[m, :, cols]) + nn(td, bd[m, :, cols])
                    ).astype(BF)
                blocks_next(m, c)
                return carry

            lax.fori_loop(0, T, step, 0)

        def finish_forward(m):
            blocks_arrive(m)
            for low in range(2):
                rows = slice(low * B, (low + 1) * B)
                y = xw[m, rows, :] + block_sum(m, low)

                @pl.when(m == 0)
                def _(y=y, rows=rows):
                    xw[1, rows, :] = y

                @pl.when(m == 1)
                def _(y=y, rows=rows):
                    yw[rows, :] = y

            @pl.when(m == 0)
            def _():
                send_normed(1)
                act_out(0).start()

            @pl.when(m == 1)
            def _():
                act_out(1).start()

            rows_sent(xh, m, x_ss, x_rs)
            blocks_sent(m)

        def forward(m, carry):
            normed_to_hidden(m)

            @pl.when(s == m)
            def _():
                weights_pass((2, 3), 1, DP - 2)

            attend(m)

            @pl.when(s == m)
            def _():
                weights_pass((2, 3), max(1, DP - 2), DP - 1)
                weights_sent()

            @pl.when(jnp.logical_and(s == 0, m == 0))
            def _():
                pl.semaphore_signal(go, inc=1, device_id={"section": other}, device_id_type=MESH)

            @pl.when(jnp.logical_and(s == 1, m == 0))
            def _():
                pl.semaphore_wait(go, 1)
                weights_start((0, 1))

            project(m)

            @pl.when(jnp.logical_and(s == 1, m == 0))
            def _():
                weights_pass((0, 1), 0, DP - 2)
                weights_start((2, 3))

            finish_forward(m)

            @pl.when(jnp.logical_and(s == 1, m == 0))
            def _():
                weights_pass((0, 1), DP - 2, DP - 1)
            return carry

        lax.fori_loop(0, 2, forward, 0)

        def gradient_to_hidden(m):
            @pl.when(m == 0)
            def _():
                local_copy(dg_hbm, dg, 2).wait()

            def chunk(c, carry):
                src = across(c)
                rows_next(dz, m, c, z_ss, z_rs)
                rows = block(src)
                full = dz[m, rows, :]
                eo = nt(full, bo[m]).astype(BF)
                ed = nt(full, bd[m]).astype(BF)
                edot[0:RANK, rows] = eo.T
                edot[RANK:2 * RANK, rows] = ed.T
                do = nt(eo, ao[m]) + nn(full, wout[m])
                dob = do.astype(BF)
                for p in range(PAIRS):
                    v = dob[:, p * 128:(p + 1) * 128]
                    dop[p, rows, :] = v
                prod = dob.T.astype(F32) * oT[m, :, rows].astype(F32)
                for h in range(HEADS):
                    delta[h:h + 1, rows] = jnp.sum(
                        prod[h * HEAD:(h + 1) * HEAD], axis=0, keepdims=True
                    )
                for n0 in range(0, FFL, TILE):
                    cols = slice(n0, n0 + TILE)
                    v = nt(ed, ad[m, cols, :]) + nn(full, wdn[m, :, cols])
                    dg[rows, cols] = (v * dg[rows, cols].astype(F32)).astype(BF)
                return carry

            lax.fori_loop(0, T, chunk, 0)

        def attention_back(m):
            dk[...] = jnp.zeros_like(dk)
            dv[...] = jnp.zeros_like(dv)
            for i in range(T):
                icols = slice(i * R, (i + 1) * R)

                def pair(p, carry, i=i, icols=icols):
                    for hh in range(2):
                        h = 2 * p + hh
                        q = head_part(qp[m * PAIRS + p, icols, :], hh)
                        do = head_part(dop[p, icols, :], hh)
                        hrows = pl.ds(pl.multiple_of(h * HEAD, HEAD), HEAD)
                        low = lse[pl.ds(m * HEADS + h, 1), icols]
                        dlt = delta[pl.ds(h, 1), icols]
                        acc = jnp.zeros((HEAD, R), F32)
                        for j in range(i + 1):
                            jrows = slice(j * R, (j + 1) * R)
                            prob = jnp.exp(scores_t(m, p, i, j, q) - low)
                            dp_t = nt(vp[m * PAIRS + p, jrows, :], do)
                            ds_t = (prob * (dp_t - dlt)).astype(BF)
                            dv[p, jrows, :] += nn(prob.astype(BF), do)
                            dk[p, jrows, :] += nn(ds_t, q)
                            acc = acc + nn(kT[m, hrows, jrows], ds_t)
                        dqt[hrows, icols] = acc
                    return carry

                lax.fori_loop(0, PAIRS, pair, 0)

        def turn_back(m):
            def step(i, carry):
                rows = block(i)
                cosine, sine = rope_of(i)
                sine = -sine
                dq = dqt[:, rows].T * 0.125
                for p in range(PAIRS):
                    lanes = slice(p * 128, (p + 1) * 128)
                    dqkv[rows, p * 128:(p + 1) * 128] = turn(dq[:, lanes], cosine, sine).astype(BF)
                    dqkv[rows, QC + p * 128:QC + (p + 1) * 128] = turn(
                        dk[p, rows, :], cosine, sine
                    ).astype(BF)
                    dqkv[rows, 2 * QC + p * 128:2 * QC + (p + 1) * 128] = dv[p, rows, :].astype(BF)
                dop[0, rows, :] = nt(dqkv[rows, :], bq[m]).astype(BF)
                dop[1, rows, :] = nt(dg[rows, :], bu[m]).astype(BF)
                return carry

            lax.fori_loop(0, T, step, 0)

        def project_back(m):
            def tail(n, carry):
                c = T - 1 - n
                i = across(c)
                rows = block(i)
                dj = dqkv[rows, :]
                du = dg[rows, :]
                e1 = dop[0, rows, :]
                e2 = dop[1, rows, :]
                for n0 in range(0, D, TILE):
                    cols = slice(n0, n0 + TILE)
                    dn1 = nt(dj, wq[m, cols, :]) + nt(e1, aq[m, cols, :])
                    dn2 = nt(du, wup[m, cols, :]) + nt(e2, au[m, cols, :])
                    xhc = xh[m, rows, cols].astype(F32)
                    gb[0:1, cols] += jnp.sum(dn1 * xhc, axis=0, keepdims=True)
                    gb[1:2, cols] += jnp.sum(dn2 * xhc, axis=0, keepdims=True)
                    gb[2:3, cols] += jnp.sum(dn1, axis=0, keepdims=True)
                    gb[3:4, cols] += jnp.sum(dn2, axis=0, keepdims=True)
                    sbuf[i, :, cols] = (dn1 * gain_of(m, 0, cols) + dn2 * gain_of(m, 1, cols)).astype(BF)
                blocks_next(3 - m, c)
                return carry

            lax.fori_loop(0, T, tail, 0)

            @pl.when(m == 1)
            def _():
                act_out(1).sent()
                local_copy(ct_in.at[s], yw, 0).start()

        def put(buf, base, width, col, value):
            lo = 0
            while lo < value.shape[1]:
                j, at = divmod(col + lo, width)
                n = min(width - at, value.shape[1] - lo)
                buf[base + j, :, at:at + n] = value[:, lo:lo + n].astype(BF)
                lo += n

        def factor_gradients(m):
            put(pa, 0, PW, 0, ADAPTER_SCALE * nn(t12t[m, 0:RANK, :], dqkv[...]))
            put(pa, 0, PW, 3 * QC, ADAPTER_SCALE * nn(t12t[m, RANK:2 * RANK, :], dg[...]))
            put(pa, 0, PW, 3 * QC + FFL, nt(edot[0:RANK, :], oT[m]))
            put(pa, 0, PW, 4 * QC + FFL, nn(edot[RANK:2 * RANK, :], hw[...]))
            if NA * PW > GA:
                put(pa, 0, PW, GA, jnp.zeros((RANK, NA * PW - GA), F32))
            put(pt, 0, GRW, 2 * D, ADAPTER_SCALE * nn(todt[m, 0:RANK, :], dz[m]))
            put(pt, 0, GRW, 3 * D, ADAPTER_SCALE * nn(todt[m, RANK:2 * RANK, :], dz[m]))
            acc[...] = jnp.zeros_like(acc)

            def step(i, carry):
                rows = block(i)
                xhc = xh[m, rows, :].astype(F32)
                n1 = (xhc * gain_of(m, 0) + bias_of(m, 0)).astype(BF)
                acc[0:RANK, :] += nn(dop[0, rows, :].T, n1)
                n2 = (xhc * gain_of(m, 1) + bias_of(m, 1)).astype(BF)
                acc[RANK:2 * RANK, :] += nn(dop[1, rows, :].T, n2)
                return carry

            lax.fori_loop(0, T, step, 0)
            put(pt, 0, GRW, 0, acc[0:RANK, :])
            put(pt, 0, GRW, D, acc[RANK:2 * RANK, :])

        def finish_backward(m):
            @pl.when(m == 1)
            def _():
                local_copy(ct_in.at[s], yw, 0).wait()

            @pl.when(m == 0)
            def _():
                ig_out(1).sent()

            blocks_arrive(3 - m)
            for low in range(2):
                rows = slice(low * B, (low + 1) * B)
                xhat, rstd = norm_parts(xw[m, rows, :])
                g = block_sum(3 - m, low)
                mean_g = jnp.mean(g, axis=1, keepdims=True)
                mean_gx = jnp.mean(g * xhat, axis=1, keepdims=True)
                v = yw[rows, :] + (g - mean_g - xhat * mean_gx) * rstd
                yw[rows, :] = v

                @pl.when(m == 1)
                def _(v=v, low=low):
                    dz[0, half(t, low == 1)] = v.astype(BF)

            @pl.when(m == 1)
            def _():
                rows_start(dz, 0, z_ss, z_rs)
                ig_out(1).start()

            @pl.when(m == 0)
            def _():
                ig_out(0).start()

            rows_sent(dz, m, z_ss, z_rs)
            blocks_sent(3 - m)

        def guarded(full, condition, action):
            if full:
                action()
            else:
                pl.when(condition)(action)

        class Exchange:
            def __init__(self, index, k, pieces, gather, source, landing):
                self.args = index, k, source, landing
                self.full = pieces >= DP
                to, come = lax.rem(d + k, DP), lax.rem(d - k + DP, DP)
                self.sends = d < pieces if gather else to < pieces
                self.hears = come < pieces if gather else d < pieces

            def copy(self):
                index, k, source, landing = self.args
                return to_peer("dp", DP, d, k, source(lax.rem(d + k, DP)), landing(k - 1),
                               ad_ss.at[index, k - 1], ad_rs.at[index, k - 1])

            def start(self):
                guarded(self.full, self.sends, lambda: self.copy().start())

            def wait_send(self):
                guarded(self.full, self.sends, lambda: self.copy().wait_send())

            def wait_recv(self):
                guarded(self.full, self.hears, lambda: self.copy().wait_recv())

        def over_dp(index, source, landing, pieces=DP, gather=False):
            for k in range(1, DP):
                yield Exchange(index, k, pieces, gather, source, landing)

        def over_tensor(index, source, landing):
            for k in range(1, T):
                yield to_peer("tensor", T, t, k, source(lax.rem(t + k, T)), landing(k - 1),
                              at_ss.at[index, k - 1], at_rs.at[index, k - 1])

        def pa_scatter():
            return over_dp(0, lambda j: pa.at[j], lambda k: pa_in.at[k], NA)

        def ga_place(owner):
            return ga_out.at[:, pl.ds(pl.multiple_of(owner * PW, 128), PW)]

        def pa_gather():
            return over_dp(1, lambda j: pa_sum, lambda k: ga_place(d), NA, True)

        def pb_scatter(part):
            return over_dp(
                2 + part, lambda j: pb.at[part * NB + j], lambda k: pb_in.at[part * (DP - 1) + k], NB
            )

        def pb_gather(part):
            return over_dp(
                4 + part, lambda j: pb_all.at[part * NB + d], lambda k: pb_all.at[part * NB + d], NB, True
            )

        def pt_scatter(part):
            return over_tensor(part, lambda j: pt.at[part * T + j], lambda k: pt_in.at[part * (T - 1) + k])

        def pt_gather(part):
            return over_tensor(2 + part, lambda j: pt.at[part * T + t], lambda k: gr_place(part, t))

        def gb_tensor():
            return over_tensor(4, lambda j: gb, lambda k: gb_t.at[k])

        def gb_dp():
            return over_dp(6, lambda j: gb_sum, lambda k: gb_d.at[k])

        def pb_gathered(part):
            for k in range(1, DP):
                owner = lax.rem(d - k + DP, DP)

                def wait(k=k, owner=owner):
                    place = pb_all.at[part * NB + owner]
                    to_peer("dp", DP, d, k, place, place,
                            ad_ss.at[4 + part, k - 1], ad_rs.at[4 + part, k - 1]).wait_recv()

                guarded(NB >= DP, owner < NB, wait)

        def start_all(copies):
            for copy in copies:
                copy.start()

        def arrive_all(copies):
            for copy in copies:
                copy.wait_recv()

        def sent_all(copies):
            for copy in copies:
                copy.wait_send()

        def fill(buf, base, value, width):
            put(buf, base, width, 0, value)
            spare = -value.shape[1] % width
            if spare > 0:
                put(buf, base, width, value.shape[1], jnp.zeros((RANK, spare), F32))

        def pt_to_pb(part):
            arrive_all(pt_scatter(part))
            v = pt[part * T + t].astype(F32)
            for k in range(T - 1):
                v = v + pt_in[part * (T - 1) + k].astype(F32)
            fill(pb, part * NB, v, SW)
            start_all(pb_scatter(part))

        def pb_add(part):
            arrive_all(pb_scatter(part))

            def add():
                v = pb[part * NB + d].astype(F32)
                for k in range(DP - 1):
                    v = v + pb_in[part * (DP - 1) + k].astype(F32)
                pb_all[part * NB + d] = v.astype(BF)

            guarded(NB >= DP, d < NB, add)
            start_all(pb_gather(part))

        def pb_to_pt(part):
            pb_gathered(part)
            for j in range(NB):
                lo, hi = j * SW, min((j + 1) * SW, GRW)
                pt[part * T + t, :, lo:hi] = pb_all[part * NB + j, :, 0:hi - lo]
            start_all(pt_gather(part))

        def gr_place(part, owner):
            return gr_out.at[:, pl.ds(pl.multiple_of(part * 2 * D + owner * GRW, 128), GRW)]

        def parts_over():
            yield to_other(pt, pt_x, c_ss.at[13], c_rs.at[13])
            yield to_other(pa, pa_x, c_ss.at[14], c_rs.at[14])

        def gb_over():
            return to_other(gb, gb_x, c_ss.at[15], c_rs.at[15])

        def sums_start():
            arrive_all(parts_over())
            for j in range(2 * T):
                pt[j] = (pt[j].astype(F32) + pt_x[j].astype(F32)).astype(BF)
            for part in range(2):
                start_all(pt_scatter(part))
            for j in range(NA):
                pa[j] = (pa[j].astype(F32) + pa_x[j].astype(F32)).astype(BF)
            start_all(pa_scatter())

        def sums_next():
            gb_over().wait_recv()
            gb[...] = gb[...] + gb_x[...]
            start_all(gb_tensor())
            for part in range(2):
                pt_to_pb(part)
            arrive_all(pa_scatter())

            def add():
                v = pa[d].astype(F32)
                for k in range(DP - 1):
                    v = v + pa_in[k].astype(F32)
                pa_sum[...] = v.astype(BF)

            guarded(NA >= DP, d < NA, add)
            start_all(pa_gather())

        def ga_store():
            return pltpu.make_async_copy(pa_sum, ga_place(d), f_s.at[0])

        def gr_store(part):
            return pltpu.make_async_copy(pt.at[part * T + t], gr_place(part, t), f_s.at[1 + part])

        def gb_store():
            return pltpu.make_async_copy(gb, gb_out, f_s.at[3])

        def sums_add():
            for part in range(2):
                pb_add(part)
            arrive_all(gb_tensor())
            total = gb[...]
            for k in range(T - 1):
                total = total + gb_t[k]
            gb_sum[...] = total
            start_all(gb_dp())
            guarded(NA >= DP, d < NA, lambda: ga_store().start())

        def sums_spread():
            for part in range(2):
                pb_to_pt(part)
                gr_store(part).start()
            arrive_all(gb_dp())
            sent_all(gb_tensor())
            total = gb_sum[...]
            for k in range(DP - 1):
                total = total + gb_d[k]
            gb[...] = total
            gb_store().start()

        def sums_end():
            for copies in (pa_gather(), pt_gather(0), pt_gather(1)):
                arrive_all(copies)
            for copies in (pa_scatter(), pa_gather(), gb_dp(), pt_scatter(0), pt_scatter(1),
                           pt_gather(0), pt_gather(1), pb_scatter(0), pb_scatter(1),
                           pb_gather(0), pb_gather(1)):
                sent_all(copies)
            guarded(NA >= DP, d < NA, lambda: ga_store().wait())
            for part in range(2):
                gr_store(part).wait()
            gb_store().wait()

        gradient_to_hidden(1)
        attention_back(1)
        turn_back(1)
        project_back(1)
        factor_gradients(1)
        local_copy(h_hbm, hw, 1).start()
        local_copy(dg_hbm, dg, 2).start()

        @pl.when(s == 0)
        def _():
            start_all(parts_over())
            gb_over().start()

        finish_backward(1)

        @pl.when(s == 1)
        def _():
            sums_start()

        gradient_to_hidden(0)

        @pl.when(s == 1)
        def _():
            sums_next()

        attention_back(0)

        @pl.when(s == 1)
        def _():
            sums_add()

        turn_back(0)

        @pl.when(s == 0)
        def _():
            sent_all(parts_over())
            gb_over().wait_send()

        @pl.when(s == 1)
        def _():
            sums_spread()
            sums_end()

        gb[...] = jnp.zeros_like(gb)
        local_copy(h_hbm, hw, 1).wait()
        factor_gradients(0)

        @pl.when(s == 1)
        def _():
            start_all(parts_over())

        @pl.when(s == 0)
        def _():
            sums_start()

        project_back(0)

        @pl.when(s == 1)
        def _():
            gb_over().start()

        @pl.when(s == 0)
        def _():
            sums_next()

        finish_backward(0)

        @pl.when(s == 0)
        def _():
            sums_add()
            sums_spread()
            sums_end()

        @pl.when(s == 1)
        def _():
            sent_all(parts_over())
            gb_over().wait_send()

        ig_out(0).sent()
        act_out(0).sent()
        for layer in range(2):
            act_out(layer).arrive()
            ig_out(layer).arrive()
        for index in range(9):
            factor_over(index, s).wait_send()
        for index in range(4):
            for owner in range(DP):
                weight_over(index, s, owner, False).wait_send()

    any_spec = pl.BlockSpec(memory_space=pl.ANY)
    vmem_spec = pl.BlockSpec(memory_space=pltpu.VMEM)
    smem_spec = pl.BlockSpec(memory_space=pltpu.SMEM)
    shapes = jax.ShapeDtypeStruct
    return pl.pallas_call(
        kernel,
        out_shape=(
            shapes((M, R, D), F32), shapes((M, R, D), F32),
            shapes((RANK, NA * PW), BF), shapes((RANK, 4 * D), BF), shapes((8, D), F32),
            shapes((L, FFL), BF), shapes((L, FFL), BF),
        ),
        in_specs=[any_spec] * 14 + [vmem_spec] * 3 + [smem_spec],
        out_specs=(any_spec,) * 7,
        scratch_shapes=[
            pltpu.VMEM((2, D, RANK), BF), pltpu.VMEM((2, RANK, 3 * QC), BF),
            pltpu.VMEM((2, QC, RANK), BF), pltpu.VMEM((2, RANK, D), BF),
            pltpu.VMEM((2, D, RANK), BF), pltpu.VMEM((2, RANK, FFL), BF),
            pltpu.VMEM((2, FFL, RANK), BF), pltpu.VMEM((2, RANK, D), BF),
            pltpu.VMEM((2, 8, D), F32),
            pltpu.VMEM((2, D, 3 * QC), BF), pltpu.VMEM((2, D, FFL), BF),
            pltpu.VMEM((2, D, QC), BF), pltpu.VMEM((2, D, FFL), BF),
            pltpu.VMEM((M, L, D), BF),
            pltpu.VMEM((M, 2 * RANK, L), BF),
            pltpu.VMEM((M * PAIRS, L, 128), BF),
            pltpu.VMEM((M * PAIRS, L, 128), BF),
            pltpu.VMEM((M * PAIRS, L, 128), BF),
            pltpu.VMEM((M, QC, L), BF),
            pltpu.VMEM((QC, L), BF),
            pltpu.VMEM((M, QC, L), BF),
            pltpu.VMEM((M * HEADS, L), F32),
            pltpu.VMEM((L, FFL), BF),
            pltpu.VMEM((L, FFL), BF),
            pltpu.VMEM((M, 2 * RANK, L), BF),
            pltpu.VMEM((T, R, D), BF),
            pltpu.VMEM((2 * 6, B, D), BF),
            pltpu.VMEM((M, L, D), BF),
            pltpu.VMEM((PAIRS, L, 128), BF),
            pltpu.VMEM((8, L), F32),
            pltpu.VMEM((2 * RANK, L), BF),
            pltpu.VMEM((PAIRS, L, 128), F32),
            pltpu.VMEM((PAIRS, L, 128), F32),
            pltpu.VMEM((QC, L), F32),
            pltpu.VMEM((L, 3 * QC), BF),
            pltpu.VMEM((2 * RANK, D), F32),
            pltpu.VMEM((8, D), F32),
            pltpu.VMEM((M, R, D), F32),
            pltpu.VMEM((R, D), F32),
            pltpu.VMEM((NA, RANK, PW), BF),
            pltpu.VMEM((NA, RANK, PW), BF),
            pltpu.VMEM((DP - 1, RANK, PW), BF),
            pltpu.VMEM((RANK, PW), BF),
            pltpu.VMEM((2 * T, RANK, GRW), BF),
            pltpu.VMEM((2 * T, RANK, GRW), BF),
            pltpu.VMEM((2 * (T - 1), RANK, GRW), BF),
            pltpu.VMEM((2 * NB, RANK, SW), BF),
            pltpu.VMEM((2 * (DP - 1), RANK, SW), BF),
            pltpu.VMEM((2 * NB, RANK, SW), BF),
            pltpu.VMEM((8, D), F32),
            pltpu.VMEM((8, D), F32),
            pltpu.VMEM((T - 1, 8, D), F32),
            pltpu.VMEM((DP - 1, 8, D), F32),
            pltpu.SemaphoreType.DMA((4,)),
            pltpu.SemaphoreType.DMA((4, 2, DP)),
            pltpu.SemaphoreType.DMA((4, 2, DP)),
            pltpu.SemaphoreType.DMA((4, DP)),
            pltpu.SemaphoreType.DMA((4, DP)),
            pltpu.SemaphoreType.DMA((2 * 4,)),
            pltpu.SemaphoreType.DMA((2 * 4,)),
            pltpu.SemaphoreType.DMA((6,)),
            pltpu.SemaphoreType.DMA((4 * 6,)),
            pltpu.SemaphoreType.DMA((2 * 4,)),
            pltpu.SemaphoreType.DMA((2 * 4,)),
            pltpu.SemaphoreType.DMA((16,)),
            pltpu.SemaphoreType.DMA((16,)),
            pltpu.SemaphoreType.DMA((7,)),
            pltpu.SemaphoreType.DMA((8,)),
            pltpu.SemaphoreType.REGULAR,
            pltpu.SemaphoreType.DMA((5, T - 1)),
            pltpu.SemaphoreType.DMA((5, T - 1)),
            pltpu.SemaphoreType.DMA((7, DP - 1)),
            pltpu.SemaphoreType.DMA((7, DP - 1)),
        ],
        compiler_params=pltpu.CompilerParams(
            collective_id=0, has_side_effects=True, vmem_limit_bytes=63 * 2**20
        ),
    )


def rope_table(length):
    half = ROT // 2
    inverse = np.float32(10000.0) ** (-np.arange(half, dtype=np.float32) * np.float32(2.0 / ROT))
    angles = np.arange(length, dtype=np.float32)[:, None] * inverse[None, :]
    cosine, sine = np.cos(angles.astype(np.float64)), np.sin(angles.astype(np.float64))
    rest = np.zeros((length, HEAD - ROT))
    return np.concatenate(
        [cosine, cosine, rest + 1.0, -sine, sine, rest], axis=-1
    ).astype(np.float32)


def solution(mesh):
    T = mesh.shape["tensor"]
    DP = mesh.shape["dp"]

    def per_device(
        inputs, cotangent, split,
        query_key_value_weight, output_weight, up_weight, down_weight,
        qkv_adapter_input, qkv_adapter_output, out_adapter_input, out_adapter_output,
        up_adapter_input, up_adapter_output, down_adapter_input, down_adapter_output,
        ln_gain, ln_bias,
    ):
        M, R, D = inputs.shape
        QC = output_weight.shape[1]
        FFL = up_weight.shape[2]
        RANK = qkv_adapter_input.shape[2]
        L = R * T
        wq = query_key_value_weight[0].reshape(-1, 3 * QC)
        aq = qkv_adapter_input[0].astype(BF)
        bq = (ADAPTER_SCALE * qkv_adapter_output[0].reshape(RANK, -1)).astype(BF)
        ao = out_adapter_input[0].astype(BF)
        bo = (ADAPTER_SCALE * out_adapter_output[0]).astype(BF)
        au = up_adapter_input[0].astype(BF)
        bu = (ADAPTER_SCALE * up_adapter_output[0]).astype(BF)
        ad = down_adapter_input[0].astype(BF)
        bd = (ADAPTER_SCALE * down_adapter_output[0]).astype(BF)
        kernel = make_kernel(T, DP, M, R, D, QC, FFL, RANK)
        act, ig, ga, gr, gb, _, _ = kernel(
            inputs, cotangent, wq, up_weight[0], output_weight[0].T, down_weight[0].T,
            qkv_adapter_input[0], qkv_adapter_output[0].reshape(RANK, -1),
            out_adapter_input[0], out_adapter_output[0],
            up_adapter_input[0], up_adapter_output[0],
            down_adapter_input[0], down_adapter_output[0],
            ln_gain[0], ln_bias[0], jnp.asarray(rope_table(L)), split[:, 0],
        )
        ga = ga.astype(F32)
        gr = gr.astype(F32)
        cuts = [3 * QC, 3 * QC + FFL, 4 * QC + FFL, 4 * QC + 2 * FFL]
        b_qkv, b_up, a_out, a_down, _ = jnp.split(ga, cuts, axis=1)
        a_qkv, a_up, b_out, b_down = jnp.split(gr, 4, axis=1)

        dp_place = lax.axis_index("dp")
        DR = D // DP
        sl = lax.dynamic_slice_in_dim
        c_qkv = wq.astype(F32) + nn(sl(aq, dp_place * DR, DR, 0), bq)
        c_out = output_weight[0].astype(F32) + nn(ao, sl(bo, dp_place * DR, DR, 1))
        c_up = up_weight[0].astype(F32) + nn(sl(au, dp_place * DR, DR, 0), bu)
        c_down = down_weight[0].astype(F32) + nn(ad, sl(bd, dp_place * DR, DR, 1))
        return (
            act[None], ig[None],
            a_qkv.T[None], b_qkv.reshape(qkv_adapter_output.shape),
            a_out.T[None], b_out[None], a_up.T[None], b_up[None], a_down.T[None], b_down[None],
            gb[0:2][None], gb[2:4][None],
            c_qkv.reshape(query_key_value_weight.shape), c_out[None], c_up[None], c_down[None],
        )

    rows = P(None, ("dp", "tensor"), None)
    whole = P("section", None, None)
    in_specs = (
        rows, rows, P(None, "dp"),
        P("section", "dp", None, "tensor"), P("section", "tensor", "dp"),
        P("section", "dp", "tensor"), P("section", "tensor", "dp"),
        whole, P("section", None, None, "tensor"), P("section", "tensor", None), whole,
        whole, P("section", None, "tensor"), P("section", "tensor", None), whole,
        whole, whole,
    )
    layer_rows = P("section", None, ("dp", "tensor"), None)
    out_specs = (
        layer_rows, layer_rows,
        whole, P("section", None, None, "tensor"), P("section", "tensor", None), whole,
        whole, P("section", None, "tensor"), P("section", "tensor", None), whole,
        whole, whole,
        P("section", "dp", None, "tensor"), P("section", "tensor", "dp"),
        P("section", "dp", "tensor"), P("section", "tensor", "dp"),
    )
    return jax.shard_map(
        per_device, mesh=mesh, in_specs=in_specs, out_specs=out_specs, check_vma=False
    )
```

time: 351 us -> 307 us (0.87)
  Pallas kernels: 323 us -> 276 us
  local copies, waits for them, and re-layouts: 17.3 us -> 22.2 us
    pallas_call x1, Pallas kernels: 323 us -> 276 us  [per_device(): kernel(inputs, cotangent, wq, up_weight[0], output_weight[0].T, down_weig...]
    unnamed x34 -> x38, local copies, waits for them, and re-layouts: 13 us -> 16.9 us
where the time goes in v4:
time: 307 us; the launch traced here: 306 us
  Pallas kernels  276 us (90%)
  local copies, waits for them, and re-layouts  22.2 us (7%)
  matrix products  6.01 us (2%)
    pallas_call x1, Pallas kernels, per_device(): kernel(inputs, cotangent, wq, up_weight[0], output_weight[0].T, down_weig...  276 us
    unnamed x38, local copies, waits for them, and re-layouts  16.9 us

profile of v4, /device:TPU:0, one launch (start us, length us, event | category | flops | bytes accessed | tf_op | source)
XLA Modules:
  0.0 306.2 jit_solution(9440417183336405201)
XLA Ops:
  0.7 1.2 copy.46
  1.9 0.9 copy.50.wq_in
  2.8 1.1 copy.49
  4.0 0.9 copy.51.bq_in
  4.9 1.0 copy.48
  5.9 0.8 copy.47
  6.7 275.6 %shard_map.297 = (f32[2,256,1024]{2,1,0:T(8,128)}, f32[2,256,1024]{2,1,0:T(8,128)}, bf16[128,3072]{1,0:T(8,128)(2,1)}, bf16[128,4096]{1,0:T(8,128)(2,1)}, f32[8,...) custom-call(f32[2,256,1024]{2,1,0:T(8,128)} %x_in.1, f32[2,256,1024]{2,1,0:T(8,128)} %ct_in.1, ...), custom_call_target="tpu_custom_call" | custom-call | tf_op jit(solution)/shard_map/pallas_call | solution.py:1191
  282.3 1.4 convert_element_type.43
  283.7 0.1 copy-done.8
  283.8 0.2 convert_element_type.42
  284.0 1.4 slice_bitcast_fusion
  285.4 2.0 copy.55
  287.4 1.0 copy.58
  288.4 1.0 copy.59
  289.4 0.8 copy.57
  290.2 1.0 split.33
  291.2 0.2 copy.52
  291.3 0.9 copy.56
  292.2 0.6 slice_bitcast_fusion.7
  292.9 1.3 convolution_add_fusion.1
  294.1 0.3 copy.54
  294.4 1.1 copy.60
  295.6 1.3 fusion.1
  296.8 0.0 copy-start.3
  296.8 0.0 copy-start.4
  296.9 1.3 copy.62
  298.2 1.3 fusion.4
  299.5 0.8 copy.61
  300.4 2.2 fusion.2
  302.5 1.3 copy.65
  303.8 1.0 copy-done.5
  304.9 1.3 copy.66
  (21 shorter events, 0.0 us)
Async XLA Ops:
  0.6 4.3 %copy-start.9 = (bf16[1,1024,256]{2,1,0:T(8,128)(2,1)S(1)}, bf16[1,1024,256]{2,1,0:T(8,128)(2,1)}, u32[]{:S(2)}) copy-start(bf16[1,1024,256]{2,1,0:T(8,128)(2,1)} %param.24) | copy-start | bytes 1572868
  0.7 5.2 %copy-start.10 = (bf16[1,256,256]{2,1,0:T(8,128)(2,1)S(1)}, bf16[1,256,256]{2,1,0:T(8,128)(2,1)}, u32[]{:S(2)}) copy-start(bf16[1,256,256]{2,1,0:T(8,128)(2,1)} %param.22) | copy-start | bytes 393220
  282.3 1.5 copy-start.8
  288.4 3.8 %copy-start.11 = (f32[8,1024]{1,0:T(8,128)S(1)}, f32[8,1024]{1,0:T(8,128)}, u32[]{:S(2)}) copy-start(f32[8,1024]{1,0:T(8,128)} %get-tuple-element.25) | copy-start | bytes 98308
  288.4 4.4 %copy-start.1 = (bf16[256,768]{1,0:T(8,128)(2,1)S(1)}, bf16[256,768]{1,0:T(8,128)(2,1)}, u32[]{:S(2)}) copy-start(bf16[256,768]{1,0:T(8,128)(2,1)} %copy.50.wq_in) | copy-start | bytes 1179652
  292.9 2.7 copy-start
  292.9 2.7 copy-start.2
  295.6 2.6 copy-start.7
  296.8 3.5 %copy-start.3 = (bf16[1,256,1024]{2,1,0:T(8,128)(2,1)S(1)}, bf16[1,256,1024]{2,1,0:T(8,128)(2,1)}, u32[]{:S(2)}) copy-start(bf16[1,256,1024]{2,1,0:T(8,128)(2,1)} %param.23) | copy-start | bytes 1572868
  296.8 3.5 %copy-start.4 = (f32[1,128,1024]{2,1,0:T(8,128)S(1)}, f32[1,128,1024]{2,1,0:T(8,128)}, u32[]{:S(2)}) copy-start(f32[1,128,1024]{2,1,0:T(8,128)} %param.30) | copy-start | bytes 1572868
  298.2 4.3 %copy-start.6 = (f32[2,256,1024]{2,1,0:T(8,128)S(1)}, f32[2,256,1024]{2,1,0:T(8,128)}, u32[]{:S(2)}) copy-start(f32[2,256,1024]{2,1,0:T(8,128)} %get-tuple-element.21) | copy-start | bytes 6291460
  302.5 2.3 copy-start.5

commit v5 on v4

--- a/solution.py
+++ b/solution.py
@@ -26,6 +26,19 @@
     return lax.dot_general(a, b, (((1,), (1,)), ((), ())), preferred_element_type=F32)
 
 
+class Sizes:
+    def __init__(self, T, DP, alone, both):
+        self.alone, self.both = alone, both
+        self.PW = -(-alone // (DP * 128)) * 128
+        self.GRW = both // T
+        self.SW = -(-self.GRW // (DP * 128)) * 128
+        self.NA, self.NB = -(-alone // self.PW), -(-self.GRW // self.SW)
+
+
+def group_sizes(T, DP, D, QC, FFL):
+    return Sizes(T, DP, QC + 2 * FFL, 3 * D), Sizes(T, DP, 3 * QC, D)
+
+
 def make_kernel(T, DP, M, R, D, QC, FFL, RANK):
     L = R * T
     DR = D // DP
@@ -34,21 +47,18 @@
     HEADS = QC // HEAD
     TILE = 256
     HALF = L // 2
-    GA = 4 * QC + 2 * FFL
-    GRW = 2 * D // T
-    PW = -(-GA // (DP * 128)) * 128
-    SW = -(-GRW // (DP * 128)) * 128
-    NA, NB = -(-GA // PW), -(-GRW // SW)
+    EARLY, LATE = group_sizes(T, DP, D, QC, FFL)
 
     def kernel(
         x_in, ct_in, wq_in, wup_in, wout_in, wdn_in,
         aq_in, bq_in, ao_in, bo_in, au_in, bu_in, ad_in, bd_in, gain_in, bias_in, rope, split,
-        act, ig, ga_out, gr_out, gb_out, h_hbm, dg_hbm,
-        aq, bq, ao, bo, au, bu, ad, bd, norms,
+        act, ig, gb_out, h_hbm, dg_hbm, ga_early, gr_early, ga_late, gr_late,
+        aq, bq, ao, bo, au, bu, ad, bd, norms, wout_raw, wdn_raw,
         wq, wup, wout, wdn, xh, t12t, qp, kp, vp, kT, vT, oT, lse, hw, dg,
         todt, sbuf, rbuf, dz, dop, delta, edot, dk, dv, dqt, dqkv,
-        acc, gb, xw, yw, pa, pa_x, pa_in, pa_sum, pt, pt_x, pt_in, pb, pb_in, pb_all,
-        gb_x, gb_sum, gb_t, gb_d,
+        acc, gb, xw, yw, gb_x, gb_sum, gb_t, gb_d,
+        pa_e, pa_x_e, pa_in_e, pa_sum_e, pt_e, pt_x_e, pt_in_e, pb_e, pb_in_e, pb_all_e,
+        pa_l, pa_x_l, pa_in_l, pa_sum_l, pt_l, pt_x_l, pt_in_l, pb_l, pb_in_l, pb_all_l,
         w_ls, w_ss, w_rs, v_ss, v_rs, x_ss, x_rs, r_ss, r_rs, z_ss, z_rs, c_ss, c_rs, l_s, f_s,
         go, at_ss, at_rs, ad_ss, ad_rs,
     ):
@@ -75,24 +85,20 @@
                 device_id={"section": other}, device_id_type=MESH,
             )
 
-        shards = (wq_in, wup_in, wout_in, wdn_in)
-
         def gathered(index, layer, owner):
             return (wq, wup, wout, wdn)[index].at[layer, pl.ds(pl.multiple_of(owner * DR, DR), DR)]
 
-        def weight_copy(index, way, hop, owner, own):
+        def weight_copy(index, way, hop, owner):
             place = gathered(index, s, owner)
             return pltpu.make_async_remote_copy(
-                src_ref=shards[index] if own else place, dst_ref=place,
+                src_ref=place, dst_ref=place,
                 send_sem=w_ss.at[index, way, hop], recv_sem=w_rs.at[index, way, hop],
                 device_id={"dp": d + 1 if way == 0 else d - 1}, device_id_type=MESH,
             )
 
-        def weight_over(index, layer, owner, own):
+        def weight_over(index, layer, owner):
             place = gathered(index, layer, owner)
-            return to_other(
-                shards[index] if own else place, place, v_ss.at[index, owner], v_rs.at[index, owner]
-            )
+            return to_other(place, place, v_ss.at[index, owner], v_rs.at[index, owner])
 
         has_next = (d < DP - 1, d > 0)
 
@@ -103,15 +109,34 @@
             return d - hop - 1 if way == 0 else d + hop + 1
 
         def weight_local(index):
-            return pltpu.make_async_copy(shards[index], gathered(index, s, d), w_ls.at[index])
+            place = gathered(index, s, d)
+            if index == 0:
+                return [
+                    pltpu.make_async_copy(
+                        wq_in.at[part], place.at[:, part * QC:(part + 1) * QC], w_ls.at[part]
+                    )
+                    for part in range(3)
+                ]
+            stage = (None, place, wout_raw, wdn_raw)[index]
+            return [pltpu.make_async_copy((None, wup_in, wout_in, wdn_in)[index], stage, w_ls.at[2 + index])]
+
+        def weights_own(indices):
+            for index in indices:
+                for copy in weight_local(index):
+                    copy.wait()
+                rows = pl.ds(pl.multiple_of(d * DR, DR), DR)
+                if index == 2:
+                    wout[s, rows, :] = wout_raw[...].T
+                if index == 3:
+                    wdn[s, rows, :] = wdn_raw[...].T
 
         def weights_start(indices):
             for index in indices:
                 for way in range(2):
                     @pl.when(has_next[way])
                     def _(index=index, way=way):
-                        weight_copy(index, way, 0, d, True).start()
-                weight_over(index, s, d, True).start()
+                        weight_copy(index, way, 0, d).start()
+                weight_over(index, s, d).start()
 
         def weights_hop(indices, hop):
             for index in indices:
@@ -119,13 +144,13 @@
                     @pl.when(holds(way, hop))
                     def _(index=index, way=way):
                         owner = owner_of(way, hop)
-                        weight_copy(index, way, hop, owner, False).wait_recv()
+                        weight_copy(index, way, hop, owner).wait_recv()
 
                         @pl.when(has_next[way])
                         def _():
-                            weight_copy(index, way, hop + 1, owner, False).start()
-
-                        weight_over(index, s, owner, False).start()
+                            weight_copy(index, way, hop + 1, owner).start()
+
+                        weight_over(index, s, owner).start()
 
         def weights_pass(indices, first, last):
             if last > first:
@@ -140,14 +165,14 @@
                 for way in range(2):
                     @pl.when(has_next[way])
                     def _(index=index, way=way):
-                        weight_copy(index, way, 0, d, True).wait_send()
+                        weight_copy(index, way, 0, d).wait_send()
 
             def step(hop, carry):
                 for index in range(4):
                     for way in range(2):
                         @pl.when(jnp.logical_and(has_next[way], holds(way, hop)))
                         def _(index=index, way=way):
-                            weight_copy(index, way, hop + 1, owner_of(way, hop), False).wait_send()
+                            weight_copy(index, way, hop + 1, owner_of(way, hop)).wait_send()
                 return carry
 
             lax.fori_loop(0, DP - 1, step, 0)
@@ -155,24 +180,32 @@
         def weights_from_other(indices, layer):
             def step(owner, carry):
                 for index in indices:
-                    weight_over(index, layer, owner, False).wait_recv()
+                    weight_over(index, layer, owner).wait_recv()
                 return carry
 
             lax.fori_loop(0, DP, step, 0)
 
         for index in range(4):
-            weight_local(index).start()
+            for copy in weight_local(index):
+                copy.start()
 
         factors = (
             (aq_in, dk.at[0], aq, 1.0), (au_in, dk.at[1], au, 1.0),
             (ad_in, dv.at[0], ad, 1.0), (ao_in, dv.at[1, 0:QC], ao, 1.0),
-            (bq_in, acc.at[0:RANK, 0:3 * QC], bq, ADAPTER_SCALE), (bu_in, acc.at[RANK:, 0:FFL], bu, ADAPTER_SCALE),
+            (None, xw.at[1, 0:RANK, 0:3 * QC], bq, ADAPTER_SCALE), (bu_in, xw.at[1, RANK:2 * RANK, 0:FFL], bu, ADAPTER_SCALE),
             (bo_in, dqt.at[0:RANK, 0:D], bo, ADAPTER_SCALE), (bd_in, dqt.at[RANK:2 * RANK, 0:D], bd, ADAPTER_SCALE),
         )
 
         def factor_load(index):
             source, stage, _, _ = factors[index]
-            return pltpu.make_async_copy(source, stage, f_s.at[index])
+            if index == 4:
+                return [
+                    pltpu.make_async_copy(
+                        bq_in.at[part], xw.at[1, 0:RANK, part * QC:(part + 1) * QC], f_s.at[7 + part if part else 4]
+                    )
+                    for part in range(3)
+                ]
+            return [pltpu.make_async_copy(source, stage, f_s.at[index])]
 
         def factor_over(index, layer):
             place = norms.at[layer] if index == 8 else factors[index][2].at[layer]
@@ -183,13 +216,15 @@
             norms[s, 2:4, :] = bias_in[...]
             factor_over(8, s).start()
             for index, (_, stage, place, scale) in enumerate(factors):
-                factor_load(index).wait()
+                for copy in factor_load(index):
+                    copy.wait()
                 v = stage[...]
                 place[s] = (v if scale == 1.0 else v * scale).astype(BF)
                 factor_over(index, s).start()
 
         for index in range(8):
-            factor_load(index).start()
+            for copy in factor_load(index):
+                copy.start()
 
         def across(c):
             return lax.rem(t + c, 2) + 2 * lax.rem(t // 2 + c // 2, 2)
@@ -389,6 +424,8 @@
         for copy in loads:
             copy.start()
 
+        weights_own((0, 1))
+
         @pl.when(s == 0)
         def _():
             weights_start((0, 1))
@@ -399,6 +436,7 @@
         dz[1, block(t)] = yw[...].astype(BF)
         rows_start(dz, 1, z_ss, z_rs)
         factors_give()
+        weights_own((2, 3))
         gb[...] = jnp.zeros_like(gb)
 
         @pl.when(s == 0)
@@ -409,9 +447,6 @@
 
         for index in range(9):
             factor_over(index, other).wait_recv()
-        for index in range(4):
-            weight_local(index).wait()
-
         def gain_of(layer, j, cols=slice(None)):
             return norms[layer, j:j + 1, cols]
 
@@ -478,8 +513,7 @@
                 local_copy(hw, h_hbm, 1).start()
                 local_copy(dg, dg_hbm, 2).start()
 
-        def attend(m):
-            for i in range(T):
+        def attend(m, i):
                 icols = slice(i * R, (i + 1) * R)
 
                 def pair(p, carry, i=i, icols=icols):
@@ -503,13 +537,7 @@
 
                 lax.fori_loop(0, PAIRS, pair, 0)
 
-        def project(m):
-            @pl.when(s != m)
-            def _():
-                weights_from_other((2, 3), m)
-
-            def step(n, carry):
-                c = T - 1 - n
+        def project(m, c):
                 i = across(c)
                 rows = block(i)
                 o = oT[m, :, rows].T
@@ -525,9 +553,26 @@
                         + nn(to, bo[m, :, cols]) + nn(td, bd[m, :, cols])
                     ).astype(BF)
                 blocks_next(m, c)
+
+        def attend_and_project(m):
+            def step(n, carry):
+                c = T - 1 - lax.rem(n, T)
+                now = n // T
+                for i in range(T):
+                    @pl.when(jnp.logical_and(across(c) == i, now == m))
+                    def _(i=i):
+                        attend(m, i)
+
+                @pl.when(n == T)
+                def _():
+                    last_weights(m)
+
+                @pl.when(now == 1)
+                def _():
+                    project(m, c)
                 return carry
 
-            lax.fori_loop(0, T, step, 0)
+            lax.fori_loop(0, 2 * T, step, 0)
 
         def finish_forward(m):
             blocks_arrive(m)
@@ -555,6 +600,25 @@
             rows_sent(xh, m, x_ss, x_rs)
             blocks_sent(m)
 
+        def last_weights(m):
+            @pl.when(s == m)
+            def _():
+                weights_pass((2, 3), max(1, DP - 2), DP - 1)
+                weights_sent()
+
+            @pl.when(jnp.logical_and(s == 0, m == 0))
+            def _():
+                pl.semaphore_signal(go, inc=1, device_id={"section": other}, device_id_type=MESH)
+
+            @pl.when(jnp.logical_and(s == 1, m == 0))
+            def _():
+                pl.semaphore_wait(go, 1)
+                weights_start((0, 1))
+
+            @pl.when(s != m)
+            def _():
+                weights_from_other((2, 3), m)
+
         def forward(m, carry):
             normed_to_hidden(m)
 
@@ -562,23 +626,7 @@
             def _():
                 weights_pass((2, 3), 1, DP - 2)
 
-            attend(m)
-
-            @pl.when(s == m)
-            def _():
-                weights_pass((2, 3), max(1, DP - 2), DP - 1)
-                weights_sent()
-
-            @pl.when(jnp.logical_and(s == 0, m == 0))
-            def _():
-                pl.semaphore_signal(go, inc=1, device_id={"section": other}, device_id_type=MESH)
-
-            @pl.when(jnp.logical_and(s == 1, m == 0))
-            def _():
-                pl.semaphore_wait(go, 1)
-                weights_start((0, 1))
-
-            project(m)
+            attend_and_project(m)
 
             @pl.when(jnp.logical_and(s == 1, m == 0))
             def _():
@@ -594,13 +642,14 @@
 
         lax.fori_loop(0, 2, forward, 0)
 
-        def gradient_to_hidden(m):
+        def gradient_to_hidden(m, meanwhile):
             @pl.when(m == 0)
             def _():
                 local_copy(dg_hbm, dg, 2).wait()
 
             def chunk(c, carry):
                 src = across(c)
+                meanwhile(c)
                 rows_next(dz, m, c, z_ss, z_rs)
                 rows = block(src)
                 full = dz[m, rows, :]
@@ -622,11 +671,12 @@
                     cols = slice(n0, n0 + TILE)
                     v = nt(ed, ad[m, cols, :]) + nn(full, wdn[m, :, cols])
                     dg[rows, cols] = (v * dg[rows, cols].astype(F32)).astype(BF)
+                vT[0:RANK, rows] = nt(dg[rows, :], bu[m]).astype(BF).T
                 return carry
 
             lax.fori_loop(0, T, chunk, 0)
 
-        def attention_back(m):
+        def attention_back(m, meanwhile):
             dk[...] = jnp.zeros_like(dk)
             dv[...] = jnp.zeros_like(dv)
             for i in range(T):
@@ -653,6 +703,7 @@
                     return carry
 
                 lax.fori_loop(0, PAIRS, pair, 0)
+                meanwhile(i)
 
         def turn_back(m):
             def step(i, carry):
@@ -668,7 +719,6 @@
                     ).astype(BF)
                     dqkv[rows, 2 * QC + p * 128:2 * QC + (p + 1) * 128] = dv[p, rows, :].astype(BF)
                 dop[0, rows, :] = nt(dqkv[rows, :], bq[m]).astype(BF)
-                dop[1, rows, :] = nt(dg[rows, :], bu[m]).astype(BF)
                 return carry
 
             lax.fori_loop(0, T, step, 0)
@@ -681,7 +731,7 @@
                 dj = dqkv[rows, :]
                 du = dg[rows, :]
                 e1 = dop[0, rows, :]
-                e2 = dop[1, rows, :]
+                e2 = vT[0:RANK, rows].T
                 for n0 in range(0, D, TILE):
                     cols = slice(n0, n0 + TILE)
                     dn1 = nt(dj, wq[m, cols, :]) + nt(e1, aq[m, cols, :])
@@ -710,29 +760,36 @@
                 buf[base + j, :, at:at + n] = value[:, lo:lo + n].astype(BF)
                 lo += n
 
-        def factor_gradients(m):
-            put(pa, 0, PW, 0, ADAPTER_SCALE * nn(t12t[m, 0:RANK, :], dqkv[...]))
-            put(pa, 0, PW, 3 * QC, ADAPTER_SCALE * nn(t12t[m, RANK:2 * RANK, :], dg[...]))
-            put(pa, 0, PW, 3 * QC + FFL, nt(edot[0:RANK, :], oT[m]))
-            put(pa, 0, PW, 4 * QC + FFL, nn(edot[RANK:2 * RANK, :], hw[...]))
-            if NA * PW > GA:
-                put(pa, 0, PW, GA, jnp.zeros((RANK, NA * PW - GA), F32))
-            put(pt, 0, GRW, 2 * D, ADAPTER_SCALE * nn(todt[m, 0:RANK, :], dz[m]))
-            put(pt, 0, GRW, 3 * D, ADAPTER_SCALE * nn(todt[m, RANK:2 * RANK, :], dz[m]))
-            acc[...] = jnp.zeros_like(acc)
+        def pad(buf, base, width, total):
+            spare = -total % width
+            if spare > 0:
+                put(buf, base, width, total, jnp.zeros((RANK, spare), F32))
+
+        def summed_rows(m, j, left):
+            acc[...] = jnp.zeros((RANK, D), F32)
 
             def step(i, carry):
                 rows = block(i)
-                xhc = xh[m, rows, :].astype(F32)
-                n1 = (xhc * gain_of(m, 0) + bias_of(m, 0)).astype(BF)
-                acc[0:RANK, :] += nn(dop[0, rows, :].T, n1)
-                n2 = (xhc * gain_of(m, 1) + bias_of(m, 1)).astype(BF)
-                acc[RANK:2 * RANK, :] += nn(dop[1, rows, :].T, n2)
+                n = (xh[m, rows, :].astype(F32) * gain_of(m, j) + bias_of(m, j)).astype(BF)
+                acc[...] += nn(left(rows), n)
                 return carry
 
             lax.fori_loop(0, T, step, 0)
-            put(pt, 0, GRW, 0, acc[0:RANK, :])
-            put(pt, 0, GRW, D, acc[RANK:2 * RANK, :])
+            return acc[...]
+
+        def early_gradients(m):
+            put(pa_e, 0, EARLY.PW, 0, ADAPTER_SCALE * nn(t12t[m, RANK:2 * RANK, :], dg[...]))
+            put(pa_e, 0, EARLY.PW, FFL, nt(edot[0:RANK, :], oT[m]))
+            put(pa_e, 0, EARLY.PW, FFL + QC, nn(edot[RANK:2 * RANK, :], hw[...]))
+            pad(pa_e, 0, EARLY.PW, EARLY.alone)
+            put(pt_e, 0, EARLY.GRW, D, ADAPTER_SCALE * nn(todt[m, 0:RANK, :], dz[m]))
+            put(pt_e, 0, EARLY.GRW, 2 * D, ADAPTER_SCALE * nn(todt[m, RANK:2 * RANK, :], dz[m]))
+            put(pt_e, 0, EARLY.GRW, 0, summed_rows(m, 1, lambda rows: vT[0:RANK, rows]))
+
+        def late_gradients(m):
+            put(pa_l, 0, LATE.PW, 0, ADAPTER_SCALE * nn(t12t[m, 0:RANK, :], dqkv[...]))
+            pad(pa_l, 0, LATE.PW, LATE.alone)
+            put(pt_l, 0, LATE.GRW, 0, summed_rows(m, 0, lambda rows: dop[0, rows, :].T))
 
         def finish_backward(m):
             @pl.when(m == 1)
@@ -806,47 +863,14 @@
                 yield to_peer("tensor", T, t, k, source(lax.rem(t + k, T)), landing(k - 1),
                               at_ss.at[index, k - 1], at_rs.at[index, k - 1])
 
-        def pa_scatter():
-            return over_dp(0, lambda j: pa.at[j], lambda k: pa_in.at[k], NA)
-
-        def ga_place(owner):
-            return ga_out.at[:, pl.ds(pl.multiple_of(owner * PW, 128), PW)]
-
-        def pa_gather():
-            return over_dp(1, lambda j: pa_sum, lambda k: ga_place(d), NA, True)
-
-        def pb_scatter(part):
-            return over_dp(
-                2 + part, lambda j: pb.at[part * NB + j], lambda k: pb_in.at[part * (DP - 1) + k], NB
-            )
-
-        def pb_gather(part):
-            return over_dp(
-                4 + part, lambda j: pb_all.at[part * NB + d], lambda k: pb_all.at[part * NB + d], NB, True
-            )
-
-        def pt_scatter(part):
-            return over_tensor(part, lambda j: pt.at[part * T + j], lambda k: pt_in.at[part * (T - 1) + k])
-
-        def pt_gather(part):
-            return over_tensor(2 + part, lambda j: pt.at[part * T + t], lambda k: gr_place(part, t))
+        def gb_over():
+            return to_other(gb, gb_x, c_ss.at[17], c_rs.at[17])
 
         def gb_tensor():
             return over_tensor(4, lambda j: gb, lambda k: gb_t.at[k])
 
         def gb_dp():
-            return over_dp(6, lambda j: gb_sum, lambda k: gb_d.at[k])
-
-        def pb_gathered(part):
-            for k in range(1, DP):
-                owner = lax.rem(d - k + DP, DP)
-
-                def wait(k=k, owner=owner):
-                    place = pb_all.at[part * NB + owner]
-                    to_peer("dp", DP, d, k, place, place,
-                            ad_ss.at[4 + part, k - 1], ad_rs.at[4 + part, k - 1]).wait_recv()
-
-                guarded(NB >= DP, owner < NB, wait)
+            return over_dp(8, lambda j: gb_sum, lambda k: gb_d.at[k])
 
         def start_all(copies):
             for copy in copies:
@@ -860,100 +884,133 @@
             for copy in copies:
                 copy.wait_send()
 
-        def fill(buf, base, value, width):
-            put(buf, base, width, 0, value)
-            spare = -value.shape[1] % width
-            if spare > 0:
-                put(buf, base, width, value.shape[1], jnp.zeros((RANK, spare), F32))
-
-        def pt_to_pb(part):
-            arrive_all(pt_scatter(part))
-            v = pt[part * T + t].astype(F32)
-            for k in range(T - 1):
-                v = v + pt_in[part * (T - 1) + k].astype(F32)
-            fill(pb, part * NB, v, SW)
-            start_all(pb_scatter(part))
-
-        def pb_add(part):
-            arrive_all(pb_scatter(part))
-
-            def add():
-                v = pb[part * NB + d].astype(F32)
-                for k in range(DP - 1):
-                    v = v + pb_in[part * (DP - 1) + k].astype(F32)
-                pb_all[part * NB + d] = v.astype(BF)
-
-            guarded(NB >= DP, d < NB, add)
-            start_all(pb_gather(part))
-
-        def pb_to_pt(part):
-            pb_gathered(part)
-            for j in range(NB):
-                lo, hi = j * SW, min((j + 1) * SW, GRW)
-                pt[part * T + t, :, lo:hi] = pb_all[part * NB + j, :, 0:hi - lo]
-            start_all(pt_gather(part))
-
-        def gr_place(part, owner):
-            return gr_out.at[:, pl.ds(pl.multiple_of(part * 2 * D + owner * GRW, 128), GRW)]
-
-        def parts_over():
-            yield to_other(pt, pt_x, c_ss.at[13], c_rs.at[13])
-            yield to_other(pa, pa_x, c_ss.at[14], c_rs.at[14])
-
-        def gb_over():
-            return to_other(gb, gb_x, c_ss.at[15], c_rs.at[15])
-
-        def sums_start():
-            arrive_all(parts_over())
-            for j in range(2 * T):
-                pt[j] = (pt[j].astype(F32) + pt_x[j].astype(F32)).astype(BF)
-            for part in range(2):
-                start_all(pt_scatter(part))
-            for j in range(NA):
-                pa[j] = (pa[j].astype(F32) + pa_x[j].astype(F32)).astype(BF)
-            start_all(pa_scatter())
-
-        def sums_next():
+        class Sums:
+            def __init__(self, group, size, refs, ga_out, gr_out):
+                self.g, self.z = group, size
+                (self.pa, self.pa_x, self.pa_in, self.pa_sum, self.pt, self.pt_x, self.pt_in,
+                 self.pb, self.pb_in, self.pb_all) = refs
+                self.ga_out, self.gr_out = ga_out, gr_out
+
+            def over(self):
+                yield to_other(self.pt, self.pt_x, c_ss.at[13 + 2 * self.g], c_rs.at[13 + 2 * self.g])
+                yield to_other(self.pa, self.pa_x, c_ss.at[14 + 2 * self.g], c_rs.at[14 + 2 * self.g])
+
+            def pa_scatter(self):
+                return over_dp(4 * self.g, lambda j: self.pa.at[lax.rem(j, self.z.NA)], lambda k: self.pa_in.at[k], self.z.NA)
+
+            def pa_gather(self):
+                return over_dp(4 * self.g + 1, lambda j: self.pa_sum, lambda k: self.ga_place(), self.z.NA, True)
+
+            def pb_scatter(self):
+                return over_dp(4 * self.g + 2, lambda j: self.pb.at[lax.rem(j, self.z.NB)], lambda k: self.pb_in.at[k], self.z.NB)
+
+            def pb_gather(self):
+                return over_dp(
+                    4 * self.g + 3, lambda j: self.pb_all.at[lax.rem(d, self.z.NB)], lambda k: self.pb_all.at[lax.rem(d, self.z.NB)], self.z.NB, True
+                )
+
+            def pt_scatter(self):
+                return over_tensor(2 * self.g, lambda j: self.pt.at[j], lambda k: self.pt_in.at[k])
+
+            def pt_gather(self):
+                return over_tensor(2 * self.g + 1, lambda j: self.pt.at[t], lambda k: self.gr_place())
+
+            def ga_place(self):
+                return self.ga_out.at[:, pl.ds(pl.multiple_of(lax.rem(d, self.z.NA) * self.z.PW, 128), self.z.PW)]
+
+            def gr_place(self):
+                return self.gr_out.at[:, pl.ds(pl.multiple_of(t * self.z.GRW, 128), self.z.GRW)]
+
+            def ga_store(self):
+                return pltpu.make_async_copy(self.pa_sum, self.ga_place(), f_s.at[2 * self.g])
+
+            def gr_store(self):
+                return pltpu.make_async_copy(self.pt.at[t], self.gr_place(), f_s.at[2 * self.g + 1])
+
+            def give(self):
+                start_all(self.over())
+
+            def given(self):
+                sent_all(self.over())
+
+            def begin(self):
+                arrive_all(self.over())
+                for j in range(T):
+                    self.pt[j] = (self.pt[j].astype(F32) + self.pt_x[j].astype(F32)).astype(BF)
+                start_all(self.pt_scatter())
+                for j in range(self.z.NA):
+                    self.pa[j] = (self.pa[j].astype(F32) + self.pa_x[j].astype(F32)).astype(BF)
+                start_all(self.pa_scatter())
+
+            def pass_on(self):
+                arrive_all(self.pt_scatter())
+                v = self.pt[t].astype(F32)
+                for k in range(T - 1):
+                    v = v + self.pt_in[k].astype(F32)
+                put(self.pb, 0, self.z.SW, 0, v)
+                pad(self.pb, 0, self.z.SW, self.z.GRW)
+                start_all(self.pb_scatter())
+                arrive_all(self.pa_scatter())
+
+                def add():
+                    v = self.pa[d].astype(F32)
+                    for k in range(DP - 1):
+                        v = v + self.pa_in[k].astype(F32)
+                    self.pa_sum[...] = v.astype(BF)
+                    self.ga_store().start()
+
+                guarded(self.z.NA >= DP, d < self.z.NA, add)
+                start_all(self.pa_gather())
+
+            def add(self):
+                arrive_all(self.pb_scatter())
+
+                def add():
+                    v = self.pb[d].astype(F32)
+                    for k in range(DP - 1):
+                        v = v + self.pb_in[k].astype(F32)
+                    self.pb_all[d] = v.astype(BF)
+
+                guarded(self.z.NB >= DP, d < self.z.NB, add)
+                start_all(self.pb_gather())
+
+            def spread(self):
+                arrive_all(self.pb_gather())
+                for j in range(self.z.NB):
+                    lo, hi = j * self.z.SW, min((j + 1) * self.z.SW, self.z.GRW)
+                    self.pt[t, :, lo:hi] = self.pb_all[j, :, 0:hi - lo]
+                start_all(self.pt_gather())
+                self.gr_store().start()
+
+            def end(self):
+                for copies in (self.pa_gather(), self.pt_gather()):
+                    arrive_all(copies)
+                for copies in (self.pa_scatter(), self.pa_gather(), self.pt_scatter(), self.pt_gather(),
+                               self.pb_scatter(), self.pb_gather()):
+                    sent_all(copies)
+                guarded(self.z.NA >= DP, d < self.z.NA, lambda: self.ga_store().wait())
+                self.gr_store().wait()
+
+        early = Sums(0, EARLY, (pa_e, pa_x_e, pa_in_e, pa_sum_e, pt_e, pt_x_e, pt_in_e, pb_e, pb_in_e, pb_all_e), ga_early, gr_early)
+        late = Sums(1, LATE, (pa_l, pa_x_l, pa_in_l, pa_sum_l, pt_l, pt_x_l, pt_in_l, pb_l, pb_in_l, pb_all_l), ga_late, gr_late)
+
+        def gb_store():
+            return pltpu.make_async_copy(gb, gb_out, f_s.at[4])
+
+        def gb_begin():
             gb_over().wait_recv()
             gb[...] = gb[...] + gb_x[...]
             start_all(gb_tensor())
-            for part in range(2):
-                pt_to_pb(part)
-            arrive_all(pa_scatter())
-
-            def add():
-                v = pa[d].astype(F32)
-                for k in range(DP - 1):
-                    v = v + pa_in[k].astype(F32)
-                pa_sum[...] = v.astype(BF)
-
-            guarded(NA >= DP, d < NA, add)
-            start_all(pa_gather())
-
-        def ga_store():
-            return pltpu.make_async_copy(pa_sum, ga_place(d), f_s.at[0])
-
-        def gr_store(part):
-            return pltpu.make_async_copy(pt.at[part * T + t], gr_place(part, t), f_s.at[1 + part])
-
-        def gb_store():
-            return pltpu.make_async_copy(gb, gb_out, f_s.at[3])
-
-        def sums_add():
-            for part in range(2):
-                pb_add(part)
+
+        def gb_pass_on():
             arrive_all(gb_tensor())
             total = gb[...]
             for k in range(T - 1):
                 total = total + gb_t[k]
             gb_sum[...] = total
             start_all(gb_dp())
-            guarded(NA >= DP, d < NA, lambda: ga_store().start())
-
-        def sums_spread():
-            for part in range(2):
-                pb_to_pt(part)
-                gr_store(part).start()
+
+        def gb_end():
             arrive_all(gb_dp())
             sent_all(gb_tensor())
             total = gb_sum[...]
@@ -961,96 +1018,61 @@
                 total = total + gb_d[k]
             gb[...] = total
             gb_store().start()
-
-        def sums_end():
-            for copies in (pa_gather(), pt_gather(0), pt_gather(1)):
-                arrive_all(copies)
-            for copies in (pa_scatter(), pa_gather(), gb_dp(), pt_scatter(0), pt_scatter(1),
-                           pt_gather(0), pt_gather(1), pb_scatter(0), pb_scatter(1),
-                           pb_gather(0), pb_gather(1)):
-                sent_all(copies)
-            guarded(NA >= DP, d < NA, lambda: ga_store().wait())
-            for part in range(2):
-                gr_store(part).wait()
+            sent_all(gb_dp())
             gb_store().wait()
 
-        gradient_to_hidden(1)
-        attention_back(1)
+        def on_core(core, *actions):
+            @pl.when(s == core)
+            def _():
+                for action in actions:
+                    action()
+
+        gradient_to_hidden(1, lambda c: None)
+        attention_back(1, lambda i: None)
         turn_back(1)
         project_back(1)
-        factor_gradients(1)
+        on_core(0, gb_over().start)
+        early_gradients(1)
+        on_core(0, early.give)
+        late_gradients(1)
+        on_core(0, late.give)
         local_copy(h_hbm, hw, 1).start()
         local_copy(dg_hbm, dg, 2).start()
-
-        @pl.when(s == 0)
-        def _():
-            start_all(parts_over())
-            gb_over().start()
-
+        on_core(1, early.begin)
         finish_backward(1)
-
-        @pl.when(s == 1)
-        def _():
-            sums_start()
-
-        gradient_to_hidden(0)
-
-        @pl.when(s == 1)
-        def _():
-            sums_next()
-
-        attention_back(0)
-
-        @pl.when(s == 1)
-        def _():
-            sums_add()
-
+        on_core(1, late.begin, gb_begin, early.pass_on)
+
+        def meanwhile(c):
+            for when, actions in ((1, (early.add, late.pass_on)), (2, (early.spread, gb_pass_on)), (3, (late.add,))):
+                @pl.when(jnp.logical_and(s == 1, c == when))
+                def _(actions=actions):
+                    for action in actions:
+                        action()
+
+        def in_attention(i):
+            if i == 1:
+                on_core(0, early.begin)
+
+        gradient_to_hidden(0, meanwhile)
+        on_core(1, late.spread, early.end)
+        on_core(0, early.given)
+        local_copy(h_hbm, hw, 1).wait()
+        early_gradients(0)
+        on_core(1, early.give)
+        attention_back(0, in_attention)
+        on_core(1, late.end, gb_end)
+        on_core(0, late.given, gb_over().wait_send)
         turn_back(0)
-
-        @pl.when(s == 0)
-        def _():
-            sent_all(parts_over())
-            gb_over().wait_send()
-
-        @pl.when(s == 1)
-        def _():
-            sums_spread()
-            sums_end()
-
+        late_gradients(0)
+        on_core(1, late.give)
+        on_core(0, early.pass_on, late.begin)
         gb[...] = jnp.zeros_like(gb)
-        local_copy(h_hbm, hw, 1).wait()
-        factor_gradients(0)
-
-        @pl.when(s == 1)
-        def _():
-            start_all(parts_over())
-
-        @pl.when(s == 0)
-        def _():
-            sums_start()
-
         project_back(0)
-
-        @pl.when(s == 1)
-        def _():
-            gb_over().start()
-
-        @pl.when(s == 0)
-        def _():
-            sums_next()
-
+        on_core(1, gb_over().start)
+        on_core(0, early.add, late.pass_on, gb_begin, early.spread)
         finish_backward(0)
-
-        @pl.when(s == 0)
-        def _():
-            sums_add()
-            sums_spread()
-            sums_end()
-
-        @pl.when(s == 1)
-        def _():
-            sent_all(parts_over())
-            gb_over().wait_send()
+        on_core(0, late.add, gb_pass_on, late.spread, gb_end, early.end, late.end)
+        on_core(1, early.given, late.given, gb_over().wait_send)
 
         ig_out(0).sent()
         act_out(0).sent()
@@ -1061,7 +1083,21 @@
             factor_over(index, s).wait_send()
         for index in range(4):
             for owner in range(DP):
-                weight_over(index, s, owner, False).wait_send()
+                weight_over(index, s, owner).wait_send()
+
+    def sums_scratch(z):
+        return [
+            pltpu.VMEM((z.NA, RANK, z.PW), BF),
+            pltpu.VMEM((z.NA, RANK, z.PW), BF),
+            pltpu.VMEM((DP - 1, RANK, z.PW), BF),
+            pltpu.VMEM((RANK, z.PW), BF),
+            pltpu.VMEM((T, RANK, z.GRW), BF),
+            pltpu.VMEM((T, RANK, z.GRW), BF),
+            pltpu.VMEM((T - 1, RANK, z.GRW), BF),
+            pltpu.VMEM((z.NB, RANK, z.SW), BF),
+            pltpu.VMEM((DP - 1, RANK, z.SW), BF),
+            pltpu.VMEM((z.NB, RANK, z.SW), BF),
+        ]
 
     any_spec = pl.BlockSpec(memory_space=pl.ANY)
     vmem_spec = pl.BlockSpec(memory_space=pltpu.VMEM)
@@ -1071,17 +1107,20 @@
         kernel,
         out_shape=(
             shapes((M, R, D), F32), shapes((M, R, D), F32),
-            shapes((RANK, NA * PW), BF), shapes((RANK, 4 * D), BF), shapes((8, D), F32),
+            shapes((8, D), F32),
             shapes((L, FFL), BF), shapes((L, FFL), BF),
+            shapes((RANK, EARLY.NA * EARLY.PW), BF), shapes((RANK, EARLY.both), BF),
+            shapes((RANK, LATE.NA * LATE.PW), BF), shapes((RANK, LATE.both), BF),
         ),
         in_specs=[any_spec] * 14 + [vmem_spec] * 3 + [smem_spec],
-        out_specs=(any_spec,) * 7,
+        out_specs=(any_spec,) * 9,
         scratch_shapes=[
             pltpu.VMEM((2, D, RANK), BF), pltpu.VMEM((2, RANK, 3 * QC), BF),
             pltpu.VMEM((2, QC, RANK), BF), pltpu.VMEM((2, RANK, D), BF),
             pltpu.VMEM((2, D, RANK), BF), pltpu.VMEM((2, RANK, FFL), BF),
             pltpu.VMEM((2, FFL, RANK), BF), pltpu.VMEM((2, RANK, D), BF),
             pltpu.VMEM((2, 8, D), F32),
+            pltpu.VMEM((QC, DR), BF), pltpu.VMEM((FFL, DR), BF),
             pltpu.VMEM((2, D, 3 * QC), BF), pltpu.VMEM((2, D, FFL), BF),
             pltpu.VMEM((2, D, QC), BF), pltpu.VMEM((2, D, FFL), BF),
             pltpu.VMEM((M, L, D), BF),
@@ -1106,25 +1145,16 @@
             pltpu.VMEM((PAIRS, L, 128), F32),
             pltpu.VMEM((QC, L), F32),
             pltpu.VMEM((L, 3 * QC), BF),
-            pltpu.VMEM((2 * RANK, D), F32),
+            pltpu.VMEM((RANK, D), F32),
             pltpu.VMEM((8, D), F32),
             pltpu.VMEM((M, R, D), F32),
             pltpu.VMEM((R, D), F32),
-            pltpu.VMEM((NA, RANK, PW), BF),
-            pltpu.VMEM((NA, RANK, PW), BF),
-            pltpu.VMEM((DP - 1, RANK, PW), BF),
-            pltpu.VMEM((RANK, PW), BF),
-            pltpu.VMEM((2 * T, RANK, GRW), BF),
-            pltpu.VMEM((2 * T, RANK, GRW), BF),
-            pltpu.VMEM((2 * (T - 1), RANK, GRW), BF),
-            pltpu.VMEM((2 * NB, RANK, SW), BF),
-            pltpu.VMEM((2 * (DP - 1), RANK, SW), BF),
-            pltpu.VMEM((2 * NB, RANK, SW), BF),
             pltpu.VMEM((8, D), F32),
             pltpu.VMEM((8, D), F32),
             pltpu.VMEM((T - 1, 8, D), F32),
             pltpu.VMEM((DP - 1, 8, D), F32),
-            pltpu.SemaphoreType.DMA((4,)),
+            *sums_scratch(EARLY), *sums_scratch(LATE),
+            pltpu.SemaphoreType.DMA((6,)),
             pltpu.SemaphoreType.DMA((4, 2, DP)),
             pltpu.SemaphoreType.DMA((4, 2, DP)),
             pltpu.SemaphoreType.DMA((4, DP)),
@@ -1135,19 +1165,123 @@
             pltpu.SemaphoreType.DMA((4 * 6,)),
             pltpu.SemaphoreType.DMA((2 * 4,)),
             pltpu.SemaphoreType.DMA((2 * 4,)),
-            pltpu.SemaphoreType.DMA((16,)),
-            pltpu.SemaphoreType.DMA((16,)),
+            pltpu.SemaphoreType.DMA((18,)),
+            pltpu.SemaphoreType.DMA((18,)),
             pltpu.SemaphoreType.DMA((7,)),
-            pltpu.SemaphoreType.DMA((8,)),
+            pltpu.SemaphoreType.DMA((10,)),
             pltpu.SemaphoreType.REGULAR,
             pltpu.SemaphoreType.DMA((5, T - 1)),
             pltpu.SemaphoreType.DMA((5, T - 1)),
-            pltpu.SemaphoreType.DMA((7, DP - 1)),
-            pltpu.SemaphoreType.DMA((7, DP - 1)),
+            pltpu.SemaphoreType.DMA((9, DP - 1)),
+            pltpu.SemaphoreType.DMA((9, DP - 1)),
         ],
         compiler_params=pltpu.CompilerParams(
             collective_id=0, has_side_effects=True, vmem_limit_bytes=63 * 2**20
         ),
+    )
+
+
+def make_finish(T, DP, M, R, D, QC, FFL, RANK):
+    DR = D // DP
+    EARLY, LATE = group_sizes(T, DP, D, QC, FFL)
+    sliced = DR % 128 != 0
+    loaded = (
+        ((RANK, EARLY.NA * EARLY.PW), BF), ((RANK, EARLY.both), BF),
+        ((RANK, LATE.NA * LATE.PW), BF), ((RANK, LATE.both), BF),
+        ((DR, RANK), F32), ((3, RANK, QC), F32), ((3, DR, QC), BF),
+        ((DR, RANK), F32), ((RANK, FFL), F32), ((DR, FFL), BF),
+        ((FFL, RANK), F32), ((RANK, DR), F32), ((FFL, DR), BF),
+        ((QC, RANK), F32), ((RANK, DR), F32), ((QC, DR), BF),
+        ((M, R, D), F32), ((M, R, D), F32), ((8, D), F32),
+    )
+    made = (
+        (RANK, FFL), (QC, RANK), (FFL, RANK), (D, RANK), (RANK, D), (RANK, D),
+        (3, RANK, QC), (D, RANK), (3, DR, QC), (DR, FFL), (FFL, DR), (QC, DR),
+    )
+    n_in, n_made = len(loaded), len(made)
+
+    def kernel(*refs):
+        sources = list(refs[:n_in])
+        results = refs[n_in:n_in + n_made + 2]
+        gains, biases = refs[n_in + n_made + 2:n_in + n_made + 4]
+        held = refs[n_in + n_made + 4:2 * n_in + n_made + 4]
+        stage = refs[2 * n_in + n_made + 4:2 * n_in + 2 * n_made + 4]
+        in_sem, out_sem = refs[-2:]
+        d = lax.axis_index("dp")
+        for index in (4, 7):
+            sources[index] = sources[index].at[pl.ds(pl.multiple_of(d * DR, DR), DR)]
+        if not sliced:
+            for index in (11, 14):
+                sources[index] = sources[index].at[:, pl.ds(pl.multiple_of(d * DR, 128), DR)]
+        loads = [pltpu.make_async_copy(sources[n], held[n], in_sem.at[n]) for n in range(n_in)]
+        for copy in loads:
+            copy.start()
+        stores = []
+
+        def take(*indices):
+            for index in indices:
+                loads[index].wait()
+
+        def store(index, source):
+            copy = pltpu.make_async_copy(source, results[index], out_sem.at[index])
+            copy.start()
+            stores.append(copy)
+
+        def give(index, value):
+            stage[index][...] = value
+            store(index, stage[index])
+
+        def factor(ref):
+            return (ADAPTER_SCALE * ref).astype(BF)
+
+        take(0)
+        ga = held[0]
+        give(0, ga[:, 0:FFL].astype(F32))
+        give(1, ga[:, FFL:FFL + QC].astype(F32).T)
+        give(2, ga[:, FFL + QC:2 * FFL + QC].astype(F32).T)
+        take(1)
+        gr = held[1]
+        give(3, gr[:, 0:D].astype(F32).T)
+        give(4, gr[:, D:2 * D].astype(F32))
+        give(5, gr[:, 2 * D:3 * D].astype(F32))
+        take(2, 3)
+        for part in range(3):
+            stage[6][part] = held[2][:, part * QC:(part + 1) * QC].astype(F32)
+        store(6, stage[6])
+        give(7, held[3][...].astype(F32).T)
+        take(4, 5, 6)
+        for part in range(3):
+            stage[8][part] = held[6][part].astype(F32) + nn(held[4][...].astype(BF), factor(held[5][part]))
+        store(8, stage[8])
+        take(7, 8, 9)
+        give(9, held[9][...].astype(F32) + nn(held[7][...].astype(BF), factor(held[8][...])))
+        take(10, 11, 12)
+        give(10, held[12][...].astype(F32) + nn(held[10][...].astype(BF), factor(held[11][...])))
+        take(13, 14, 15)
+        give(11, held[15][...].astype(F32) + nn(held[13][...].astype(BF), factor(held[14][...])))
+        for index in range(2):
+            take(16 + index)
+            store(12 + index, held[16 + index])
+        take(18)
+        gains[...] = held[18][0:2]
+        biases[...] = held[18][2:4]
+        for copy in stores:
+            copy.wait()
+
+    any_spec = pl.BlockSpec(memory_space=pl.ANY)
+    rows = ((M, R, D),) * 2
+    vmem_spec = pl.BlockSpec(memory_space=pltpu.VMEM)
+    return pl.pallas_call(
+        kernel,
+        out_shape=tuple(jax.ShapeDtypeStruct(shape, F32) for shape in made + rows + ((2, D),) * 2),
+        in_specs=[any_spec] * n_in,
+        out_specs=(any_spec,) * (n_made + 2) + (vmem_spec,) * 2,
+        scratch_shapes=[
+            *(pltpu.VMEM(shape, dtype) for shape, dtype in loaded),
+            *(pltpu.VMEM(shape, F32) for shape in made),
+            pltpu.SemaphoreType.DMA((n_in,)), pltpu.SemaphoreType.DMA((n_made + 2,)),
+        ],
+        compiler_params=pltpu.CompilerParams(vmem_limit_bytes=63 * 2**20),
     )
 
 
@@ -1178,43 +1312,40 @@
         FFL = up_weight.shape[2]
         RANK = qkv_adapter_input.shape[2]
         L = R * T
-        wq = query_key_value_weight[0].reshape(-1, 3 * QC)
-        aq = qkv_adapter_input[0].astype(BF)
-        bq = (ADAPTER_SCALE * qkv_adapter_output[0].reshape(RANK, -1)).astype(BF)
-        ao = out_adapter_input[0].astype(BF)
-        bo = (ADAPTER_SCALE * out_adapter_output[0]).astype(BF)
-        au = up_adapter_input[0].astype(BF)
-        bu = (ADAPTER_SCALE * up_adapter_output[0]).astype(BF)
-        ad = down_adapter_input[0].astype(BF)
-        bd = (ADAPTER_SCALE * down_adapter_output[0]).astype(BF)
+        wq = query_key_value_weight[0].transpose(1, 0, 2)
+        bq = qkv_adapter_output[0].transpose(1, 0, 2)
+        DR = D // DP
         kernel = make_kernel(T, DP, M, R, D, QC, FFL, RANK)
-        act, ig, ga, gr, gb, _, _ = kernel(
-            inputs, cotangent, wq, up_weight[0], output_weight[0].T, down_weight[0].T,
-            qkv_adapter_input[0], qkv_adapter_output[0].reshape(RANK, -1),
+        act, ig, gb, _, _, ga_early, gr_early, ga_late, gr_late = kernel(
+            inputs, cotangent, wq, up_weight[0], output_weight[0], down_weight[0],
+            qkv_adapter_input[0], bq,
             out_adapter_input[0], out_adapter_output[0],
             up_adapter_input[0], up_adapter_output[0],
             down_adapter_input[0], down_adapter_output[0],
             ln_gain[0], ln_bias[0], jnp.asarray(rope_table(L)), split[:, 0],
         )
-        ga = ga.astype(F32)
-        gr = gr.astype(F32)
-        cuts = [3 * QC, 3 * QC + FFL, 4 * QC + FFL, 4 * QC + 2 * FFL]
-        b_qkv, b_up, a_out, a_down, _ = jnp.split(ga, cuts, axis=1)
-        a_qkv, a_up, b_out, b_down = jnp.split(gr, 4, axis=1)
-
-        dp_place = lax.axis_index("dp")
-        DR = D // DP
-        sl = lax.dynamic_slice_in_dim
-        c_qkv = wq.astype(F32) + nn(sl(aq, dp_place * DR, DR, 0), bq)
-        c_out = output_weight[0].astype(F32) + nn(ao, sl(bo, dp_place * DR, DR, 1))
-        c_up = up_weight[0].astype(F32) + nn(sl(au, dp_place * DR, DR, 0), bu)
-        c_down = down_weight[0].astype(F32) + nn(ad, sl(bd, dp_place * DR, DR, 1))
+        out_factor, down_factor = out_adapter_output[0], down_adapter_output[0]
+        if DR % 128 != 0:
+            start = lax.axis_index("dp") * DR
+            out_factor = lax.dynamic_slice_in_dim(out_factor, start, DR, 1)
+            down_factor = lax.dynamic_slice_in_dim(down_factor, start, DR, 1)
+        (
+            b_up, a_out, a_down, a_up, b_out, b_down, b_qkv, a_qkv, c_qkv, c_up, c_down, c_out, act, ig,
+            grad_gain, grad_bias,
+        ) = make_finish(T, DP, M, R, D, QC, FFL, RANK)(
+            ga_early, gr_early, ga_late, gr_late,
+            qkv_adapter_input[0], bq, wq,
+            up_adapter_input[0], up_adapter_output[0], up_weight[0],
+            down_adapter_input[0], down_factor, down_weight[0],
+            out_adapter_input[0], out_factor, output_weight[0],
+            act, ig, gb,
+        )
         return (
             act[None], ig[None],
-            a_qkv.T[None], b_qkv.reshape(qkv_adapter_output.shape),
-            a_out.T[None], b_out[None], a_up.T[None], b_up[None], a_down.T[None], b_down[None],
-            gb[0:2][None], gb[2:4][None],
-            c_qkv.reshape(query_key_value_weight.shape), c_out[None], c_up[None], c_down[None],
+            a_qkv[None], b_qkv.transpose(1, 0, 2)[None],
+            a_out[None], b_out[None], a_up[None], b_up[None], a_down[None], b_down[None],
+            grad_gain[None], grad_bias[None],
+            c_qkv.transpose(1, 0, 2)[None], c_out[None], c_up[None], c_down[None],
         )
 
     rows = P(None, ("dp", "tensor"), None)

time: 307 us -> 263 us (0.86)
  local copies, waits for them, and re-layouts: 22.2 us -> 0 us
  Pallas kernels: 276 us -> 262 us
  matrix products: 6.01 us -> 0 us
    unnamed x38 -> x0, local copies, waits for them, and re-layouts: 16.9 us -> none
    pallas_call x1 -> x2, Pallas kernels: 276 us -> 262 us  [the longest x1 253 us: per_device(): kernel(inputs, cotangent, wq, up_weight[0], output_weight[0], down_weight...]
    dot_general x4 -> x0, matrix products: 6.01 us -> none  [nn(): lax.dot_general(a, b, (((1,), (0,)), ((), ())), preferred_element_type=F32)]
where the time goes in v5:
time: 263 us
  Pallas kernels  262 us (100%)
    pallas_call x1, Pallas kernels, per_device(): kernel(inputs, cotangent, wq, up_weight[0], output_weight[0], down_weight...  253 us
    pallas_call x1, Pallas kernels, per_device(): make_finish(T, DP, M, R, D, QC, FFL, RANK)  8.67 us

profile of v5, /device:TPU:0, one launch (start us, length us, event | category | flops | bytes accessed | tf_op | source)
XLA Modules:
  0.0 262.8 jit_solution(4389650055141214609)
XLA Ops:
  0.6 253.3 %shard_map.297 = (f32[2,256,1024]{2,1,0:T(8,128)}, f32[2,256,1024]{2,1,0:T(8,128)}, f32[8,1024]{1,0:T(8,128)}, bf16[1024,1024]{1,0:T(8,128)(2,1)}, bf16[1024,102...) custom-call(f32[2,256,1024]{2,1,0:T(8,128)} %x_in.1, ...), custom_call_target="tpu_custom_call" | custom-call | tf_op jit(solution)/shard_map/pallas_call | solution.py:1319
  254.0 8.7 %shard_map.298 = (f32[128,1024]{1,0:T(8,128)}, f32[256,128]{1,0:T(8,128)}, f32[1024,128]{1,0:T(8,128)}, f32[1024,128]{1,0:T(8,128)}, f32[128,1024]{1,0:T(8,128)}...) custom-call(bf16[128,2560]{1,0:T(8,128)(2,1)} %get-tuple-element.39., ...), custom_call_target="tpu_custom_call" | custom-call | tf_op jit(solution)/shard_map/pallas_call | solution.py:1335

commit v6 on v5

--- a/solution.py
+++ b/solution.py
@@ -1214,8 +1214,8 @@
             for index in (11, 14):
                 sources[index] = sources[index].at[:, pl.ds(pl.multiple_of(d * DR, 128), DR)]
         loads = [pltpu.make_async_copy(sources[n], held[n], in_sem.at[n]) for n in range(n_in)]
-        for copy in loads:
-            copy.start()
+        for index in (0, 16, 17, *range(1, 16), 18):
+            loads[index].start()
         stores = []
 
         def take(*indices):
@@ -1239,6 +1239,9 @@
         give(0, ga[:, 0:FFL].astype(F32))
         give(1, ga[:, FFL:FFL + QC].astype(F32).T)
         give(2, ga[:, FFL + QC:2 * FFL + QC].astype(F32).T)
+        for index in range(2):
+            take(16 + index)
+            store(12 + index, held[16 + index])
         take(1)
         gr = held[1]
         give(3, gr[:, 0:D].astype(F32).T)
@@ -1259,9 +1262,6 @@
         give(10, held[12][...].astype(F32) + nn(held[10][...].astype(BF), factor(held[11][...])))
         take(13, 14, 15)
         give(11, held[15][...].astype(F32) + nn(held[13][...].astype(BF), factor(held[14][...])))
-        for index in range(2):
-            take(16 + index)
-            store(12 + index, held[16 + index])
         take(18)
         gains[...] = held[18][0:2]
         biases[...] = held[18][2:4]

time: 263 us -> 263 us (level)
  no operation moved by 1% of the time
where the time goes in v6:
time: 263 us
  Pallas kernels  262 us (100%)
    pallas_call x1, Pallas kernels, per_device(): kernel(inputs, cotangent, wq, up_weight[0], output_weight[0], down_weight...  253 us
    pallas_call x1, Pallas kernels, per_device(): make_finish(T, DP, M, R, D, QC, FFL, RANK)  9.11 us

profile of v6, /device:TPU:0, one launch (start us, length us, event | category | flops | bytes accessed | tf_op | source)
XLA Modules:
  0.0 263.3 jit_solution(7457196396126180974)
XLA Ops:
  0.6 253.3 %shard_map.297 = (f32[2,256,1024]{2,1,0:T(8,128)}, f32[2,256,1024]{2,1,0:T(8,128)}, f32[8,1024]{1,0:T(8,128)}, bf16[1024,1024]{1,0:T(8,128)(2,1)}, bf16[1024,102...) custom-call(f32[2,256,1024]{2,1,0:T(8,128)} %x_in.1, ...), custom_call_target="tpu_custom_call" | custom-call | tf_op jit(solution)/shard_map/pallas_call | solution.py:1319
  254.0 9.1 %shard_map.298 = (f32[128,1024]{1,0:T(8,128)}, f32[256,128]{1,0:T(8,128)}, f32[1024,128]{1,0:T(8,128)}, f32[1024,128]{1,0:T(8,128)}, f32[128,1024]{1,0:T(8,128)}...) custom-call(bf16[128,2560]{1,0:T(8,128)(2,1)} %get-tuple-element.39., ...), custom_call_target="tpu_custom_call" | custom-call | tf_op jit(solution)/shard_map/pallas_call | solution.py:1335
